TPU v7x, 32 devices: a whole 2x2x4 slice. The times are simulated.
32 devices in a mesh: dp: 16 (over z, x, core), mp: 2 (over y).
Axes of the slice: x: 2, y: 2, z: 4, core: 2. Of those that a mesh axis runs over, the one named last changes fastest.
Arguments:
- tokens: bfloat16 [16384, 1024], P(('dp', 'mp')), may hold values from -6 to 6
- w_query: bfloat16 [1024, 1024], P('dp', 'mp'), may hold values from -0.1875 to 0.1875
- w_key: bfloat16 [1024, 1024], P('dp', 'mp'), may hold values from -0.1875 to 0.1875
- w_value: bfloat16 [1024, 1024], P('dp', 'mp'), may hold values from -0.1875 to 0.1875
- w_out: bfloat16 [1024, 1024], P('dp', 'mp'), may hold values from -1.5 to 1.5
- w_up: bfloat16 [1024, 4096], P('dp', 'mp'), may hold values from -0.1875 to 0.1875
- w_down: bfloat16 [1024, 4096], P('dp', 'mp'), may hold values from -0.09375 to 0.09375
- b_query: bfloat16 [1024], P('dp'), may hold values from -3 to 3
- b_value: bfloat16 [1024], P('dp'), may hold values from -3 to 3
- b_up: bfloat16 [4096], P('dp'), may hold values from -3 to 3
- b_out: bfloat16 [1024], P('dp'), may hold values from -2 to 2
- b_down: bfloat16 [1024], P('dp'), may hold values from -2 to 2
- gain_attn: bfloat16 [1024], P('dp'), may hold values from 0.25 to 1.75
- shift_attn: bfloat16 [1024], P('dp'), may hold values from -2 to 2
- gain_ffn: bfloat16 [1024], P('dp'), may hold values from 0.25 to 1.75
- shift_ffn: bfloat16 [1024], P('dp'), may hold values from -2 to 2
- out_grad: bfloat16 [16384, 1024], P(('dp', 'mp')), may hold values from -6 to 6
- seq_len: int32 [64], replicated, may hold values from 0 to 1024, as said below
- seq_group: int32 [64], replicated, may hold values from 0 to 15, as said below
- seq_start: int32 [64], replicated, may hold values from 0 to 1024, as said below
Outputs:
- layer_out: bfloat16 [16384, 1024], P(('dp', 'mp'))
- grad_tokens: float32 [16384, 1024], P(('dp', 'mp'))
- grad_w_query: float32 [1024, 1024], P('dp', 'mp')
- grad_w_key: float32 [1024, 1024], P('dp', 'mp')
- grad_w_value: float32 [1024, 1024], P('dp', 'mp')
- grad_w_out: float32 [1024, 1024], P('dp', 'mp')
- grad_w_up: float32 [1024, 4096], P('dp', 'mp')
- grad_w_down: float32 [1024, 4096], P('dp', 'mp')
- grad_b_query: float32 [1024], P('dp')
- grad_b_value: float32 [1024], P('dp')
- grad_b_up: float32 [4096], P('dp')
- grad_b_out: float32 [1024], P('dp')
- grad_b_down: float32 [1024], P('dp')
- grad_gain_attn: float32 [1024], P('dp')
- grad_shift_attn: float32 [1024], P('dp')
- grad_gain_ffn: float32 [1024], P('dp')
- grad_shift_ffn: float32 [1024], P('dp')
Inputs may be any that keep to these rules, and one draw needn't show every extreme that they name: `seq_len`: each data group is named by exactly 4 slots; slots of length 0 are empty, the others hold 128 tokens or more; the slots of one group lie one after another from place 0 without intersection and within its 1024 places (an empty slot starts where the group's used places end); places not covered are padding; some group holds a single sequence of 1024 tokens. `seq_group`: which group holds which slot. `seq_start`: offsets as described for seq_len.
All inputs are finite; a program needn't handle non-finite values.
Results may differ from a plain program's by a relative error of at most 0.013.
The roundings to bfloat16 on the way count: a program that leaves them out, or rounds other values in their place, can miss the bound.
Values may be sent and summed in bfloat16 or wider, within the bound.
A program may use at most 192 MiB of HBM per device.

v0:
```python
import jax
import jax.numpy as jnp
from jax import lax
from jax.sharding import PartitionSpec as P

HDIM = 64


eps = 1e-05
masked_score = -1e30


def norm_rows(values, gain, shift):
    center = values - jnp.mean(values, axis=-1, keepdims=True)
    spread = jnp.mean(center * center, axis=-1, keepdims=True)
    return center * lax.rsqrt(spread + eps) * gain + shift


def gelu_exact(values):
    return jax.nn.gelu(values, approximate=False)


def token_segments(group_id, group_rows, seq_len, seq_group, seq_start):
    places = jnp.arange(group_rows, dtype=jnp.int32)[None, :]
    starts = seq_start[:, None]
    inside = (
        (seq_group[:, None] == group_id) & (places >= starts) & (places < starts + seq_len[:, None])
    )
    labels = jnp.arange(1, seq_len.shape[0] + 1, dtype=jnp.int32)[:, None]
    return jnp.sum(jnp.where(inside, labels, 0), axis=0) - 1


def block_scores(query_block, key_heads, seg_block, segment, scale):
    scores = (
        jnp.einsum("qhd,khd->hqk", query_block, key_heads, preferred_element_type=jnp.float32)
        * scale
    )
    same_doc = seg_block[:, None] == segment[None, :]
    return jnp.where(same_doc[None], scores, masked_score)


def local_part(full_vector, index, width):
    return lax.dynamic_slice_in_dim(full_vector, index * width, width).astype(jnp.float32)


def widen(local_vector, index, total):
    width = local_vector.shape[0]
    return lax.dynamic_update_slice_in_dim(
        jnp.zeros((total,), jnp.float32), local_vector, index * width, 0
    )


def local(
    tokens,
    w_query,
    w_key,
    w_value,
    w_out,
    w_up,
    w_down,
    b_query,
    b_value,
    b_up,
    b_out,
    b_down,
    gain_attn,
    shift_attn,
    gain_ffn,
    shift_ffn,
    out_grad,
    seq_len,
    seq_group,
    seq_start,
):
    half_rows = tokens.shape[0]
    group_rows = half_rows * lax.axis_size("mp")
    mp_index = lax.axis_index("mp")
    dp_index = lax.axis_index("dp")
    local_width = w_query.shape[1]
    local_hidden = w_up.shape[1]
    local_heads = local_width // HDIM
    scale = HDIM ** (-0.5)
    block_rows = min(512, group_rows)
    f32 = jnp.float32
    bf16 = jnp.bfloat16
    gathered = (
        lax.all_gather(w_query, "dp", axis=0, tiled=True),
        lax.all_gather(w_key, "dp", axis=0, tiled=True),
        lax.all_gather(w_value, "dp", axis=0, tiled=True),
        lax.all_gather(w_out, "dp", axis=0, tiled=True),
        lax.all_gather(w_up, "dp", axis=0, tiled=True),
        lax.all_gather(w_down, "dp", axis=0, tiled=True),
        lax.all_gather(b_query, "dp", axis=0, tiled=True),
        lax.all_gather(b_value, "dp", axis=0, tiled=True),
        lax.all_gather(b_up, "dp", axis=0, tiled=True),
        lax.all_gather(b_out, "dp", axis=0, tiled=True),
        lax.all_gather(b_down, "dp", axis=0, tiled=True),
        lax.all_gather(gain_attn, "dp", axis=0, tiled=True),
        lax.all_gather(shift_attn, "dp", axis=0, tiled=True),
        lax.all_gather(gain_ffn, "dp", axis=0, tiled=True),
        lax.all_gather(shift_ffn, "dp", axis=0, tiled=True),
    )
    (
        query_mat,
        key_mat,
        value_mat,
        out_mat,
        up_mat,
        down_mat,
        query_bias,
        value_bias,
        up_bias,
        out_bias,
        down_bias,
        gain_one,
        shift_one,
        gain_two,
        shift_two,
    ) = gathered
    width = query_bias.shape[0]
    hidden_total = up_bias.shape[0]
    query_local = local_part(query_bias, mp_index, local_width)
    value_local = local_part(value_bias, mp_index, local_width)
    up_local = local_part(up_bias, mp_index, local_hidden)
    segment = token_segments(dp_index, group_rows, seq_len, seq_group, seq_start)
    own_segment = lax.dynamic_slice_in_dim(segment, mp_index * half_rows, half_rows)
    alive = (own_segment >= 0).astype(f32)[:, None]
    rows_all = lax.all_gather(tokens, "mp", axis=0, tiled=True)
    query = (jnp.dot(rows_all, query_mat, preferred_element_type=f32) + query_local).astype(bf16)
    keys = jnp.dot(rows_all, key_mat, preferred_element_type=f32).astype(bf16)
    values = (jnp.dot(rows_all, value_mat, preferred_element_type=f32) + value_local).astype(bf16)
    query_heads = query.reshape(group_rows, local_heads, HDIM)
    key_heads = keys.reshape(group_rows, local_heads, HDIM)
    value_heads = values.reshape(group_rows, local_heads, HDIM)
    contexts = []
    log_totals = []
    for begin in range(0, group_rows, block_rows):
        scores = block_scores(
            query_heads[begin : begin + block_rows],
            key_heads,
            segment[begin : begin + block_rows],
            segment,
            scale,
        )
        row_max = jnp.max(scores, axis=-1, keepdims=True)
        shifted = jnp.exp(scores - row_max)
        row_total = jnp.sum(shifted, axis=-1, keepdims=True)
        probs = (shifted / row_total).astype(bf16)
        piece = jnp.einsum("hqk,khd->qhd", probs, value_heads, preferred_element_type=f32)
        contexts.append(piece.astype(bf16).reshape(block_rows, local_width))
        log_totals.append(row_max + jnp.log(row_total))
    context = jnp.concatenate(contexts, axis=0)
    attn_part = jnp.einsum("tc,oc->to", context, out_mat, preferred_element_type=f32)
    attended = lax.psum_scatter(attn_part, "mp", scatter_dimension=0, tiled=True)
    first_in = tokens.astype(f32) + attended + out_bias.astype(f32)
    first, first_pull = jax.vjp(norm_rows, first_in, gain_one.astype(f32), shift_one.astype(f32))
    first_all = lax.all_gather(first.astype(bf16), "mp", axis=0, tiled=True)
    hidden = jnp.dot(first_all, up_mat, preferred_element_type=f32) + up_local
    active_full, gelu_pull = jax.vjp(gelu_exact, hidden)
    active = active_full.astype(bf16)
    ffn_part = jnp.einsum("tf,of->to", active, down_mat, preferred_element_type=f32)
    branch = lax.psum_scatter(ffn_part, "mp", scatter_dimension=0, tiled=True)
    second_in = first + branch + down_bias.astype(f32)
    final, second_pull = jax.vjp(norm_rows, second_in, gain_two.astype(f32), shift_two.astype(f32))
    layer_out = (final * alive).astype(bf16)
    query_mat, key_mat, value_mat, out_mat, up_mat, down_mat = (
        lax.all_gather(w_query, "dp", axis=0, tiled=True),
        lax.all_gather(w_key, "dp", axis=0, tiled=True),
        lax.all_gather(w_value, "dp", axis=0, tiled=True),
        lax.all_gather(w_out, "dp", axis=0, tiled=True),
        lax.all_gather(w_up, "dp", axis=0, tiled=True),
        lax.all_gather(w_down, "dp", axis=0, tiled=True),
    )
    cotan = out_grad.astype(f32) * alive
    d_second, d_gain_two, d_shift_two = second_pull(cotan)
    d_down_bias = jnp.sum(d_second, axis=0)
    d_branch_all = lax.all_gather(d_second.astype(bf16), "mp", axis=0, tiled=True)
    grad_down = jnp.einsum("to,tf->of", d_branch_all, active, preferred_element_type=f32)
    d_active = jnp.dot(d_branch_all, down_mat, preferred_element_type=f32)
    d_hidden = gelu_pull(d_active)[0].astype(bf16)
    d_up_local = jnp.sum(d_hidden.astype(f32), axis=0)
    grad_up = jnp.einsum("tm,tf->mf", first_all, d_hidden, preferred_element_type=f32)
    d_first_part = jnp.einsum("tf,mf->tm", d_hidden, up_mat, preferred_element_type=f32)
    d_first = d_second + lax.psum_scatter(d_first_part, "mp", scatter_dimension=0, tiled=True)
    d_first_in, d_gain_one, d_shift_one = first_pull(d_first)
    d_out_bias = jnp.sum(d_first_in, axis=0)
    d_attn_all = lax.all_gather(d_first_in.astype(bf16), "mp", axis=0, tiled=True)
    grad_out = jnp.einsum("to,tc->oc", d_attn_all, context, preferred_element_type=f32)
    d_context = jnp.dot(d_attn_all, out_mat, preferred_element_type=f32).astype(bf16)
    d_ctx_heads = d_context.reshape(group_rows, local_heads, HDIM)
    d_key_acc = jnp.zeros((group_rows, local_heads, HDIM), f32)
    d_value_acc = jnp.zeros((group_rows, local_heads, HDIM), f32)
    d_query_parts = []
    for number, begin in enumerate(range(0, group_rows, block_rows)):
        query_block = query_heads[begin : begin + block_rows]
        scores = block_scores(
            query_block, key_heads, segment[begin : begin + block_rows], segment, scale
        )
        probs = jnp.exp(scores - log_totals[number])
        ctx_block = d_ctx_heads[begin : begin + block_rows]
        d_probs = jnp.einsum("qhd,khd->hqk", ctx_block, value_heads, preferred_element_type=f32)
        delta = jnp.sum(d_probs * probs, axis=-1, keepdims=True)
        d_scores = (probs * (d_probs - delta)).astype(bf16)
        d_query_parts.append(
            jnp.einsum("hqk,khd->qhd", d_scores, key_heads, preferred_element_type=f32) * scale
        )
        d_key_acc = (
            d_key_acc
            + jnp.einsum("hqk,qhd->khd", d_scores, query_block, preferred_element_type=f32) * scale
        )
        d_value_acc = d_value_acc + jnp.einsum(
            "hqk,qhd->khd", probs.astype(bf16), ctx_block, preferred_element_type=f32
        )
    d_query = jnp.concatenate(d_query_parts, axis=0).astype(bf16).reshape(group_rows, local_width)
    d_keys = d_key_acc.astype(bf16).reshape(group_rows, local_width)
    d_values = d_value_acc.astype(bf16).reshape(group_rows, local_width)
    grad_query = jnp.einsum("tm,tc->mc", rows_all, d_query, preferred_element_type=f32)
    grad_key = jnp.einsum("tm,tc->mc", rows_all, d_keys, preferred_element_type=f32)
    grad_value = jnp.einsum("tm,tc->mc", rows_all, d_values, preferred_element_type=f32)
    d_query_local = jnp.sum(d_query.astype(f32), axis=0)
    d_value_local = jnp.sum(d_values.astype(f32), axis=0)
    d_rows_part = jnp.einsum("tc,mc->tm", d_query, query_mat, preferred_element_type=f32)
    d_rows_part = d_rows_part + jnp.einsum("tc,mc->tm", d_keys, key_mat, preferred_element_type=f32)
    d_rows_part = d_rows_part + jnp.einsum(
        "tc,mc->tm", d_values, value_mat, preferred_element_type=f32
    )
    grad_tokens = d_first_in + lax.psum_scatter(d_rows_part, "mp", scatter_dimension=0, tiled=True)
    summed = (
        lax.psum_scatter(grad_query, "dp", scatter_dimension=0, tiled=True),
        lax.psum_scatter(grad_key, "dp", scatter_dimension=0, tiled=True),
        lax.psum_scatter(grad_value, "dp", scatter_dimension=0, tiled=True),
        lax.psum_scatter(grad_out, "dp", scatter_dimension=0, tiled=True),
        lax.psum_scatter(grad_up, "dp", scatter_dimension=0, tiled=True),
        lax.psum_scatter(grad_down, "dp", scatter_dimension=0, tiled=True),
        lax.psum_scatter(
            widen(d_query_local, mp_index, width), "dp", scatter_dimension=0, tiled=True
        ),
        lax.psum_scatter(
            widen(d_value_local, mp_index, width), "dp", scatter_dimension=0, tiled=True
        ),
        lax.psum_scatter(
            widen(d_up_local, mp_index, hidden_total), "dp", scatter_dimension=0, tiled=True
        ),
        lax.psum_scatter(d_out_bias, "dp", scatter_dimension=0, tiled=True),
        lax.psum_scatter(d_down_bias, "dp", scatter_dimension=0, tiled=True),
        lax.psum_scatter(d_gain_one, "dp", scatter_dimension=0, tiled=True),
        lax.psum_scatter(d_shift_one, "dp", scatter_dimension=0, tiled=True),
        lax.psum_scatter(d_gain_two, "dp", scatter_dimension=0, tiled=True),
        lax.psum_scatter(d_shift_two, "dp", scatter_dimension=0, tiled=True),
    )
    vectors = lax.psum(
        (
            summed[6],
            summed[7],
            summed[8],
            summed[9],
            summed[10],
            summed[11],
            summed[12],
            summed[13],
            summed[14],
        ),
        "mp",
    )
    return (
        layer_out,
        grad_tokens,
        summed[0],
        summed[1],
        summed[2],
        summed[3],
        summed[4],
        summed[5],
        vectors[0],
        vectors[1],
        vectors[2],
        vectors[3],
        vectors[4],
        vectors[5],
        vectors[6],
        vectors[7],
        vectors[8],
    )


def solution(mesh):
    placed = (
        P(("dp", "mp"), None),
        P("dp", "mp"),
        P("dp", "mp"),
        P("dp", "mp"),
        P("dp", "mp"),
        P("dp", "mp"),
        P("dp", "mp"),
        P("dp"),
        P("dp"),
        P("dp"),
        P("dp"),
        P("dp"),
        P("dp"),
        P("dp"),
        P("dp"),
        P("dp"),
        P(("dp", "mp"), None),
        P(),
        P(),
        P(),
    )
    return jax.shard_map(
        local,
        mesh=mesh,
        in_specs=placed,
        out_specs=(
            P(("dp", "mp"), None),
            P(("dp", "mp"), None),
            P("dp", "mp"),
            P("dp", "mp"),
            P("dp", "mp"),
            P("dp", "mp"),
            P("dp", "mp"),
            P("dp", "mp"),
            P("dp"),
            P("dp"),
            P("dp"),
            P("dp"),
            P("dp"),
            P("dp"),
            P("dp"),
            P("dp"),
            P("dp"),
        ),
        check_vma=False,
    )
```

profile of v0, /device:TPU:1, one launch (start us, length us, event | category | flops | bytes accessed | tf_op | source)
XLA Modules:
  0.0 1254.5 jit_solution(9740725791507557992)
XLA Ops:
  19.3 58.2 %all-reduce.19 = (bf16[1024]{0:T(1024)(128)(2,1)S(1)}, bf16[1024]{0:T(1024)(128)(2,1)S(1)}, bf16[1024]{0:T(1024)(128)(2,1)S(1)}, bf16[1024]{0:T(1024)(128)(2,1)S...) all-reduce(bf16[1024]{0:T(1024)(128)(2,1)S(1)} %dynamic-update-slic, ...), channel_id=1, replica_groups=mesh['dp'=16,'mp'=2] {'dp'}, use_global_device_ids=true, to_apply=%add | all-reduce | flops 8192 | bytes 32768
  80.5 3.4 all-gather.12.cloned.1.call-done
  84.0 3.1 add_convert_fusion.2
  87.2 37.3 %all-gather.18.cloned.1.call-done = bf16[1024,512]{1,0:T(8,128)(2,1)} async-done(((bf16[64,512]{1,0:T(8,128)(2,1)}), bf16[1024,512]{1,0:T(8,128)(2,1)}) %all-gather.18.cloned.1.call-update) | async-done | bytes 1048592 | tf_op jit(solution)/shard_map/all_gather | solution.py:88
  124.5 3.1 convolution_convert_fusion.1
  127.7 3.2 fusion.48
  130.9 5.7 copy-done
  136.7 3.7 fusion.1
  140.4 23.1 %all-gather.14.cloned.1.call-done = bf16[1024,512]{1,0:T(8,128)(2,1)} async-done(((bf16[64,512]{1,0:T(8,128)(2,1)}), bf16[1024,512]{1,0:T(8,128)(2,1)}) %all-gather.14.cloned.1.call-update) | async-done | bytes 1048592 | tf_op jit(solution)/shard_map/all_gather | solution.py:89
  163.4 3.1 add_convert_fusion.3
  166.6 8.1 fusion.25
  174.7 3.2 fusion.49
  177.9 3.5 fusion
  181.5 2.2 copy-done.1
  183.7 3.8 fusion.26
  187.5 14.8 %all-gather.20.cloned.1.call-done = bf16[1024,512]{1,0:T(8,128)(2,1)} async-done(((bf16[64,512]{1,0:T(8,128)(2,1)}), bf16[1024,512]{1,0:T(8,128)(2,1)}) %all-gather.20.cloned.1.call-update) | async-done | bytes 1048592 | tf_op jit(solution)/shard_map/all_gather | solution.py:90
  202.4 4.6 fusion.28
  207.8 52.2 %reduce-scatter.17.cloned.1.call-done = f32[512,1024]{1,0:T(8,128)} async-done(((f32[1024,1024]{1,0:T(8,128)}), f32[512,1024]{1,0:T(8,128)}) %reduce-scatter.17.cloned.1.call-update) | async-done | bytes 2097168 | tf_op jit(solution)/shard_map/reduce_scatter | solution.py:154
  264.5 21.8 %all-gather = bf16[16,1,256]{2,1,0:T(2,128)(2,1)S(1)} all-gather(bf16[1,1,256]{2,1,0:T(2,128)(2,1)S(1)} %reshape.250), channel_id=1, replica_groups=mesh['dp'=16,'mp'=2] {'dp'}, dimensions={0}, use_global_device_ids=true | all-gather | bytes 8704 | tf_op jit(solution)/shard_map/all_gather | solution.py:95
  286.4 27.0 %all-gather.24.cloned.1.call-done = bf16[1024,2048]{1,0:T(8,128)(2,1)} async-done(((bf16[64,2048]{1,0:T(8,128)(2,1)}), bf16[1024,2048]{1,0:T(8,128)(2,1)}) %all-gather.24.cloned.1.call-update) | async-done | bytes 4194320 | tf_op jit(solution)/shard_map/all_gather | solution.py:91
  313.4 33.4 %all-gather.22.cloned.1.call-done = bf16[1024,1024]{1,0:T(8,128)(2,1)} async-done(((bf16[512,1024]{1,0:T(8,128)(2,1)}), bf16[1024,1024]{1,0:T(8,128)(2,1)}) %all-gather.22.cloned.1.call-update) | async-done | bytes 2097168 | tf_op jit(solution)/shard_map/all_gather | solution.py:157
  346.8 26.4 %multiply_convert_fusion.2 = (bf16[1024,2048]{1,0:T(8,128)(2,1)}, f32[1024,2048]{1,0:T(8,128)}, f32[1024,2048]{1,0:T(8,128)}) fusion(f32[2048]{0:T(1024)S(1)} %dynamic-slice_convert_fusion, bf16[1024,1024]{1,0:T(8,128)(2,1)} %all-gather.22.cloned.1.call-done, bf16[1024,2048]{1,0:T(8,128)(2,1)} %all-gather.24.cloned.1.call-done), kind=kOutput, calls=%fused_computation.24 | convolution fusion | flops 4433379328 | bytes 27271168 | tf_op jit(solution)/shard_map/dot_general | solution.py:158
  373.2 27.2 %all-gather.26.cloned.1.call-done = bf16[1024,2048]{1,0:T(8,128)(2,1)} async-done(((bf16[64,2048]{1,0:T(8,128)(2,1)}), bf16[1024,2048]{1,0:T(8,128)(2,1)}) %all-gather.26.cloned.1.call-update) | async-done | bytes 4194320 | tf_op jit(solution)/shard_map/all_gather | solution.py:92
  400.4 9.9 fusion.50
  410.9 52.0 %reduce-scatter.19.cloned.1.call-done = f32[512,1024]{1,0:T(8,128)} async-done(((f32[1024,1024]{1,0:T(8,128)}), f32[512,1024]{1,0:T(8,128)}) %reduce-scatter.19.cloned.1.call-update) | async-done | bytes 2097168 | tf_op jit(solution)/shard_map/reduce_scatter | solution.py:162
  462.9 2.3 fusion.41
  467.1 2.0 fusion.40
  472.3 33.2 %all-gather.28.cloned.1.call-done = bf16[1024,1024]{1,0:T(8,128)(2,1)} async-done(((bf16[512,1024]{1,0:T(8,128)(2,1)}), bf16[1024,1024]{1,0:T(8,128)(2,1)}) %all-gather.28.cloned.1.call-update) | async-done | bytes 2097168 | tf_op jit(solution)/shard_map/all_gather | solution.py:177
  505.5 13.9 %convert_reduce_fusion = (f32[2048]{0:T(1024)}, bf16[1024,2048]{1,0:T(8,128)(2,1)S(1)}) fusion(f32[1024,2048]{1,0:T(8,128)} %get-tuple-element.127, f32[1024,2048]{1,0:T(8,128)} %get-tuple-element.149, f32[2048]{0:T(1024)S(1)} %dynamic-slice_convert_fusion, bf16[1024,1024]{1,0:T(8,128)(2,1)} %all-gather.28.cloned.1.call-done, ...), kind=kOutput, calls=%fused_computation.20 | convolution fusion | flops 4330616832 | bytes 27279360 | tf_op jit(solution)/shard_map/dot_general | solution.py:179
  519.4 2.0 copy-done.38
  521.4 6.1 fusion.51
  527.5 54.4 %reduce-scatter.21.cloned.1.call-done = f32[512,1024]{1,0:T(8,128)} async-done(((f32[1024,1024]{1,0:T(8,128)}), f32[512,1024]{1,0:T(8,128)}) %reduce-scatter.21.cloned.1.call-update) | async-done | bytes 2097168 | tf_op jit(solution)/shard_map/reduce_scatter | solution.py:184
  581.9 3.7 multiply_reduce_fusion.3
  589.6 33.2 %all-gather.30.cloned.1.call-done = bf16[1024,1024]{1,0:T(8,128)(2,1)} async-done(((bf16[512,1024]{1,0:T(8,128)(2,1)}), bf16[1024,1024]{1,0:T(8,128)(2,1)}) %all-gather.30.cloned.1.call-update) | async-done | bytes 2097168 | tf_op jit(solution)/shard_map/all_gather | solution.py:187
  622.8 2.9 convolution_convert_fusion
  625.8 11.2 multiply_reduce_fusion.1
  637.0 15.7 %multiply_convert_fusion.1 = bf16[8,512,1024]{2,1,0:T(8,128)(2,1)} fusion(f32[8,512,1024]{2,1,0:T(8,128)} %get-tuple-element.153, f32[8,512,1024]{2,1,0:T(8,128)} %copy-done.1, f32[8,512]{1,0:T(8,128)S(1)} %get-tuple-element.152, f32[8,512]{1,0:T(8,128)S(1)} %log_add_fusion.1), kind=kLoop, calls=%fused_computation.3 | loop fusion | flops 16777216 | bytes 41975808 | tf_op jit(solution)/shard_map/convert_element_type | solution.py:203
  652.7 7.7 fusion.23
  660.5 6.3 fusion.52
  666.8 4.0 fusion.5
  670.8 9.8 multiply_reduce_fusion
  680.6 8.7 convert_reduce_fusion.1
  689.3 10.4 multiply_convert_fusion
  699.8 6.2 fusion.24
  706.0 3.4 multiply_convert_fusion.3
  712.1 3.3 add_add_fusion
  715.5 10.6 fusion.54
  726.4 10.6 fusion.55
  737.1 4.5 fusion.27
  741.7 4.2 convolution_bitcast_fusion
  745.9 2.9 copy.53
  748.9 4.2 convolution_bitcast_fusion.1
  753.1 3.0 copy.51
  756.1 4.2 convolution_bitcast_fusion.2
  760.4 3.1 copy.49
  765.9 57.7 %all-reduce.17 = (f32[1024]{0:T(1024)S(1)}, f32[1024]{0:T(1024)S(1)}, f32[4096]{0:T(1024)S(1)}, f32[1024]{0:T(1024)S(1)}, f32[1024]{0:T(1024)S(1)}, /*index=5*/f...) all-reduce(f32[1024]{0:T(1024)S(1)} %dynamic_update_slice.9, ...), channel_id=12, replica_groups=mesh['dp'=16,'mp'=2] {'dp'}, use_global_device_ids=true, to_apply=%region_26.27.clone | all-reduce | flops 12288 | bytes 98304
  824.3 4.8 all-reduce.18
  829.1 3.2 add_add_fusion.5
  832.3 46.7 %reduce-scatter.27.cloned.1.call-done = f32[64,2048]{1,0:T(8,128)} async-done(((f32[1024,2048]{1,0:T(8,128)}), f32[64,2048]{1,0:T(8,128)}) %reduce-scatter.27.cloned.1.call-update) | async-done | bytes 524304 | tf_op jit(solution)/shard_map/reduce_scatter | solution.py:233
  879.1 108.9 %reduce-scatter.29.cloned.1.call-done = f32[64,2048]{1,0:T(8,128)} async-done(((f32[1024,2048]{1,0:T(8,128)}), f32[64,2048]{1,0:T(8,128)}) %reduce-scatter.29.cloned.1.call-update) | async-done | bytes 524304 | tf_op jit(solution)/shard_map/reduce_scatter | solution.py:234
  987.9 63.9 %reduce-scatter.25.cloned.1.call-done = f32[64,512]{1,0:T(8,128)} async-done(((f32[1024,512]{1,0:T(8,128)}), f32[64,512]{1,0:T(8,128)}) %reduce-scatter.25.cloned.1.call-update) | async-done | bytes 131088 | tf_op jit(solution)/shard_map/reduce_scatter | solution.py:232
  1051.9 65.2 %reduce-scatter.35.cloned.1.call-done = f32[64,512]{1,0:T(8,128)} async-done(((f32[1024,512]{1,0:T(8,128)}), f32[64,512]{1,0:T(8,128)}) %reduce-scatter.35.cloned.1.call-update) | async-done | bytes 131088
  1117.1 64.9 %reduce-scatter.33.cloned.1.call-done = f32[64,512]{1,0:T(8,128)} async-done(((f32[1024,512]{1,0:T(8,128)}), f32[64,512]{1,0:T(8,128)}) %reduce-scatter.33.cloned.1.call-update) | async-done | bytes 131088
  1182.0 65.2 %reduce-scatter.31.cloned.1.call-done = f32[64,512]{1,0:T(8,128)} async-done(((f32[1024,512]{1,0:T(8,128)}), f32[64,512]{1,0:T(8,128)}) %reduce-scatter.31.cloned.1.call-update) | async-done | bytes 131088
  (202 shorter events, 34.5 us)
Async XLA Ops:
  7.2 73.3 %all-gather.16.cloned.1.call-start = ((), (), s32[]{:S(2)}) async-start(), calls=%async_computation.12 | async-start | bytes 1114112 | tf_op jit(solution)/shard_map/all_gather | solution.py:87
  7.9 76.0 %all-gather.12.cloned.1.call-start = ((), (), s32[]{:S(2)}) async-start(), calls=%async_computation.10 | async-start | bytes 3145728 | tf_op jit(solution)/shard_map/all_gather | solution.py:128
  8.7 115.9 %all-gather.18.cloned.1.call-start = ((), (), s32[]{:S(2)}) async-start(), calls=%async_computation.13 | async-start | bytes 1114112 | tf_op jit(solution)/shard_map/all_gather | solution.py:88
  9.4 154.0 %all-gather.14.cloned.1.call-start = ((), (), s32[]{:S(2)}) async-start(), calls=%async_computation.11 | async-start | bytes 1114112 | tf_op jit(solution)/shard_map/all_gather | solution.py:89
  10.0 192.4 %all-gather.20.cloned.1.call-start = ((), (), s32[]{:S(2)}) async-start(), calls=%async_computation.14 | async-start | bytes 1114112 | tf_op jit(solution)/shard_map/all_gather | solution.py:90
  10.6 249.4 %reduce-scatter.17.cloned.1.call-start = ((), (), s32[]{:S(2)}) async-start(), calls=%async_computation.15 | async-start | bytes 6291456 | tf_op jit(solution)/shard_map/reduce_scatter | solution.py:154
  87.2 43.7 %copy-start.8 = (bf16[512,512]{0,1:T(8,128)(2,1)}, bf16[512,512]{0,1:T(8,128)(2,1)S(1)}, u32[]{:S(2)}) copy-start(bf16[512,512]{0,1:T(8,128)(2,1)S(1)} %get-tuple-element.138) | copy-start | bytes 1572868
  87.2 87.5 %copy-start.10 = (bf16[512,512]{0,1:T(8,128)(2,1)}, bf16[512,512]{0,1:T(8,128)(2,1)S(1)}, u32[]{:S(2)}) copy-start(bf16[512,512]{0,1:T(8,128)(2,1)S(1)} %get-tuple-element.137) | copy-start | bytes 1572868
  127.7 47.0 %copy-start.6 = (bf16[1024,512]{0,1:T(8,128)(2,1)}, bf16[1024,512]{0,1:T(8,128)(2,1)S(1)}, u32[]{:S(2)}) copy-start(bf16[1024,512]{0,1:T(8,128)(2,1)S(1)} %convolution_convert_fusion.1) | copy-start | bytes 3145732
  130.9 5.7 copy-start
  166.6 14.9 %copy-start.12 = (bf16[1024,512]{0,1:T(8,128)(2,1)}, bf16[1024,512]{0,1:T(8,128)(2,1)S(1)}, u32[]{:S(2)}) copy-start(bf16[1024,512]{0,1:T(8,128)(2,1)S(1)} %add_convert_fusion.3) | copy-start | bytes 3145732
  174.7 27.7 %copy-start.36 = (bf16[8,64,512]{2,1,0:T(8,128)(2,1)}, bf16[8,64,512]{2,1,0:T(8,128)(2,1)S(1)}, u32[]{:S(2)}) copy-start(bf16[8,64,512]{2,1,0:T(8,128)(2,1)S(1)} %fusion.25) | copy-start | bytes 1572868
  177.9 5.7 copy-start.1
  187.5 19.4 %copy-start.37 = (bf16[8,64,512]{2,1,0:T(8,128)(2,1)}, bf16[8,64,512]{2,1,0:T(8,128)(2,1)S(1)}, u32[]{:S(2)}) copy-start(bf16[8,64,512]{2,1,0:T(8,128)(2,1)S(1)} %fusion.26) | copy-start | bytes 1572868
  207.0 53.0 %copy-start.14 = (bf16[512,1024]{1,0:T(8,128)(2,1)S(1)}, bf16[512,1024]{1,0:T(8,128)(2,1)}, u32[]{:S(2)}) copy-start(bf16[512,1024]{1,0:T(8,128)(2,1)} %param.20) | copy-start | bytes 3145732
  207.0 106.4 %all-gather.24.cloned.1.call-start = ((), (), s32[]{:S(2)}) async-start(), calls=%async_computation.17 | async-start | bytes 4456448 | tf_op jit(solution)/shard_map/all_gather | solution.py:91
  207.7 139.1 %all-gather.22.cloned.1.call-start = ((), (), s32[]{:S(2)}) async-start(), calls=%async_computation.16 | async-start | bytes 3145728 | tf_op jit(solution)/shard_map/all_gather | solution.py:157
  261.9 2.6 copy-start.35
  263.7 136.7 %all-gather.26.cloned.1.call-start = ((), (), s32[]{:S(2)}) async-start(), calls=%async_computation.18 | async-start | bytes 4456448 | tf_op jit(solution)/shard_map/all_gather | solution.py:92
  264.4 198.4 %reduce-scatter.19.cloned.1.call-start = ((), (), s32[]{:S(2)}) async-start(), calls=%async_computation.19 | async-start | bytes 6291456 | tf_op jit(solution)/shard_map/reduce_scatter | solution.py:162
  410.3 95.1 %all-gather.28.cloned.1.call-start = ((), (), s32[]{:S(2)}) async-start(), calls=%async_computation.20 | async-start | bytes 3145728 | tf_op jit(solution)/shard_map/all_gather | solution.py:177
  410.9 54.7 %copy-start.15 = (bf16[512,1024]{1,0:T(8,128)(2,1)S(1)}, bf16[512,1024]{1,0:T(8,128)(2,1)}, u32[]{:S(2)}) copy-start(bf16[512,1024]{1,0:T(8,128)(2,1)} %param.36) | copy-start | bytes 3145732
  469.1 1.3 copy-start.5
  472.2 109.7 %reduce-scatter.21.cloned.1.call-start = ((), (), s32[]{:S(2)}) async-start(), calls=%async_computation.21 | async-start | bytes 6291456 | tf_op jit(solution)/shard_map/reduce_scatter | solution.py:184
  505.5 15.9 %copy-start.31 = (bf16[1024,2048]{1,0:T(8,128)(2,1)S(1)}, bf16[1024,2048]{1,0:T(8,128)(2,1)}, u32[]{:S(2)}) copy-start(bf16[1024,2048]{1,0:T(8,128)(2,1)} %all-gather.24.cloned.1.call-done) | copy-start | bytes 12582916
  519.4 2.0 copy-start.38
  527.5 95.3 %all-gather.30.cloned.1.call-start = ((), (), s32[]{:S(2)}) async-start(), calls=%async_computation.22 | async-start | bytes 3145728 | tf_op jit(solution)/shard_map/all_gather | solution.py:187
  586.4 1.3 copy-start.3
  586.4 36.4 %copy-start.34 = (bf16[1024,512]{1,0:T(8,128)(2,1)S(1)}, bf16[1024,512]{1,0:T(8,128)(2,1)}, u32[]{:S(2)}) copy-start(bf16[1024,512]{1,0:T(8,128)(2,1)} %all-gather.20.cloned.1.call-done) | copy-start | bytes 3145732
  589.5 239.5 %reduce-scatter.23.cloned.1.call-start = ((), (), s32[]{:S(2)}) async-start(), calls=%async_computation.23 | async-start | bytes 6291456 | tf_op jit(solution)/shard_map/reduce_scatter | solution.py:227
  589.6 81.2 %copy-start.21 = (f32[8,512]{1,0:T(8,128)}, f32[8,512]{1,0:T(8,128)S(1)}, u32[]{:S(2)}) copy-start(f32[8,512]{1,0:T(8,128)S(1)} %log_add_fusion) | copy-start | bytes 49156
  589.6 36.2 %copy-start.13 = (bf16[1024,512]{0,1:T(8,128)(2,1)S(1)}, bf16[1024,512]{0,1:T(8,128)(2,1)}, u32[]{:S(2)}) copy-start(bf16[1024,512]{0,1:T(8,128)(2,1)} %copy-done.12) | copy-start | bytes 3145732
  637.0 15.7 %copy-start.7 = (bf16[1024,512]{0,1:T(8,128)(2,1)S(1)}, bf16[1024,512]{0,1:T(8,128)(2,1)}, u32[]{:S(2)}) copy-start(bf16[1024,512]{0,1:T(8,128)(2,1)} %copy-done.6) | copy-start | bytes 3145732
  637.0 29.8 %slice-start = ((s8[16777216]{0:T(1024)(128)(4,1)}), s8[4194304]{0:T(1024)(128)(4,1)S(1)}, s32[]{:S(2)}) async-start(s8[16777216]{0:T(1024)(128)(4,1)} %bitcast.90), calls=%async_computation.30 | async-start | bytes 8388608
  637.0 29.8 %slice-start.1 = ((s8[16777216]{0:T(1024)(128)(4,1)}), s8[4194304]{0:T(1024)(128)(4,1)S(1)}, s32[]{:S(2)}) async-start(s8[16777216]{0:T(1024)(128)(4,1)} %bitcast.90), calls=%async_computation.31 | async-start | bytes 8388608
  637.0 29.8 %slice-start.2 = ((s8[16777216]{0:T(1024)(128)(4,1)}), s8[4194304]{0:T(1024)(128)(4,1)S(1)}, s32[]{:S(2)}) async-start(s8[16777216]{0:T(1024)(128)(4,1)} %bitcast.90), calls=%async_computation.32 | async-start | bytes 8388608
  652.7 7.7 copy-start.11
  652.7 14.0 %slice-start.3 = ((s8[16777216]{0:T(1024)(128)(4,1)}), s8[4194304]{0:T(1024)(128)(4,1)S(1)}, s32[]{:S(2)}) async-start(s8[16777216]{0:T(1024)(128)(4,1)} %bitcast.90), calls=%async_computation.33 | async-start | bytes 8388608
  680.6 8.8 copy-start.22
  680.6 8.8 copy-start.23
  699.8 6.2 copy-start.2
  699.8 6.2 copy-start.9
  706.0 50.1 %copy-start.18 = (bf16[8,64,512]{2,1,0:T(8,128)(2,1)}, bf16[8,64,512]{2,1,0:T(8,128)(2,1)S(1)}, u32[]{:S(2)}) copy-start(bf16[8,64,512]{2,1,0:T(8,128)(2,1)S(1)} %fusion.24) | copy-start | bytes 1572868
  706.0 3.4 copy-start.33
  709.4 1.3 copy-start.16
  709.4 1.4 copy-start.32
  710.8 1.3 copy-start.20
  715.4 163.7 %reduce-scatter.27.cloned.1.call-start = ((), (), s32[]{:S(2)}) async-start(), calls=%async_computation.25 | async-start | bytes 8912896 | tf_op jit(solution)/shard_map/reduce_scatter | solution.py:233
  726.1 261.8 %reduce-scatter.29.cloned.1.call-start = ((), (), s32[]{:S(2)}) async-start(), calls=%async_computation.26 | async-start | bytes 8912896 | tf_op jit(solution)/shard_map/reduce_scatter | solution.py:234
  737.1 314.8 %reduce-scatter.25.cloned.1.call-start = ((), (), s32[]{:S(2)}) async-start(), calls=%async_computation.24 | async-start | bytes 2228224 | tf_op jit(solution)/shard_map/reduce_scatter | solution.py:232
  741.6 375.4 %reduce-scatter.35.cloned.1.call-start = ((), (), s32[]{:S(2)}) async-start(), calls=%async_computation.29 | async-start | bytes 2228224
  748.9 433.2 %reduce-scatter.33.cloned.1.call-start = ((), (), s32[]{:S(2)}) async-start(), calls=%async_computation.28 | async-start | bytes 2228224
  756.1 491.2 %reduce-scatter.31.cloned.1.call-start = ((), (), s32[]{:S(2)}) async-start(), calls=%async_computation.27 | async-start | bytes 2228224
  760.3 4.5 copy-start.30
  760.3 4.8 copy-start.29
  760.3 5.1 copy-start.17
  760.3 5.1 copy-start.19
  760.3 5.6 copy-start.24
  760.3 5.5 copy-start.25
  760.3 5.5 copy-start.26
  760.3 5.5 copy-start.27
  760.3 5.5 copy-start.28
  760.3 68.7 %copy-start.4 = (f32[512,1024]{1,0:T(8,128)S(1)}, f32[512,1024]{1,0:T(8,128)}, u32[]{:S(2)}) copy-start(f32[512,1024]{1,0:T(8,128)} %copy-done.3) | copy-start | bytes 6291460
Sparse Core Ops, SparseCore 0:
  10.2 40.4 all-gather.15
  52.3 31.6 all-gather.11
  86.1 38.3 all-gather.17
  126.5 36.8 all-gather.13
  165.4 36.8 all-gather.19
  207.1 52.8 reduce-scatter.16
  262.4 50.9 all-gather.23
  315.6 31.1 all-gather.21
  349.2 51.1 all-gather.25
  410.5 52.3 reduce-scatter.18
  472.3 33.1 all-gather.27
  527.6 54.2 reduce-scatter.20
  589.6 33.1 all-gather.29
  715.5 54.3 reduce-scatter.22
  774.4 104.6 reduce-scatter.26
  883.6 104.3 reduce-scatter.28
  992.1 59.7 reduce-scatter.24
  1056.5 60.5 reduce-scatter.34
  1121.4 60.5 reduce-scatter.32
  1186.7 60.5 reduce-scatter.30
where the time goes:
time: 1270 us; the launch traced here: 1250 us
  waiting for transfers between devices  811 us (64%)
  matrix products  193 us (15%)
  blocking collectives  143 us (11%)
  other arithmetic  57.8 us (5%)
  local copies, waits for them, and re-layouts  31.4 us (2%)
  between operations  17.4 us (1%)
    unnamed x23, waiting for transfers between devices  200 us
    unnamed x2, blocking collectives  116 us
    reduce_scatter x1, waiting for transfers between devices, local(): lax.psum_scatter(grad_down, 'dp', scatter_dimension=0, tiled=True)  109 us
    reduce_scatter x1, waiting for transfers between devices, local(): lax.psum_scatter(grad_out, 'dp', scatter_dimension=0, tiled=True)  63.9 us
    reduce_scatter x1, waiting for transfers between devices, local(): lax.psum_scatter(d_first_part, 'mp', scatter_dimension=0, tiled=True)  54.4 us
    reduce_scatter x1, waiting for transfers between devices, local(): lax.psum_scatter(attn_part, 'mp', scatter_dimension=0, tiled=True)  52.2 us
    reduce_scatter x1, waiting for transfers between devices, local(): branch = lax.psum_scatter(ffn_part, 'mp', scatter_dimension=0, tiled=True)  52 us
    reduce_scatter x1, waiting for transfers between devices, local(): lax.psum_scatter(grad_up, 'dp', scatter_dimension=0, tiled=True)  46.7 us
  transfers between devices with their start and end apart: 20, of which 18 were waited for; matrix products, arithmetic and copies ran while one was open for 10% of the time, Pallas kernels for 0%

commit v1 on v0

v1 whole, which is shorter than its diff:
```python
import jax
import jax.numpy as jnp
from jax import lax
from jax.experimental import pallas as pl
from jax.experimental.pallas import tpu as pltpu
from jax.sharding import Mesh, PartitionSpec as P

HDIM = 64
PAIR = 2 * HDIM
eps = 1e-05
masked_score = -1e30
scale = HDIM ** (-0.5)
f32 = jnp.float32
bf16 = jnp.bfloat16
NT = (((1,), (1,)), ((), ()))
NN = (((1,), (0,)), ((), ()))
TN = (((0,), (0,)), ((), ()))


def mm(left, right, dims=NN):
    return lax.dot_general(left, right, dims, preferred_element_type=f32)


def head_lanes(rows, head):
    lane = lax.broadcasted_iota(jnp.int32, (rows, PAIR), 1)
    return (lane >= head * HDIM) & (lane < (head + 1) * HDIM)


def attn_fwd_kernel(seg_col, seg_row, q_ref, k_ref, v_ref, ctx_ref, lse_ref):
    rows = q_ref.shape[0]
    same = seg_col[...] == seg_row[...]
    q = q_ref[...] * jnp.asarray(scale, bf16)
    k = k_ref[...]
    v = v_ref[...]
    first = head_lanes(rows, 0)
    parts = []
    for head in range(2):
        qh = jnp.where(head_lanes(rows, head), q, jnp.zeros_like(q))
        scores = jnp.where(same, mm(qh, k, NT), masked_score)
        top = jnp.max(scores, axis=-1, keepdims=True)
        shifted = jnp.exp(scores - top)
        total = jnp.sum(shifted, axis=-1, keepdims=True)
        piece = mm(shifted.astype(bf16), v) * (1.0 / total)
        parts.append((piece, top + jnp.log(total)))
    ctx_ref[...] = jnp.where(first, parts[0][0], parts[1][0]).astype(bf16)
    lse_ref[...] = jnp.where(first, parts[0][1], parts[1][1])


def attn_bwd_kernel(
    seg_col, seg_row, lse_ref, q_ref, k_ref, v_ref, do_ref, dq_ref, dk_ref, dv_ref, dk_acc, dv_acc
):
    block = pl.program_id(1)

    @pl.when(block == 0)
    def _():
        dk_acc[...] = jnp.zeros_like(dk_acc)
        dv_acc[...] = jnp.zeros_like(dv_acc)

    rows = q_ref.shape[0]
    same = seg_col[...] == seg_row[...]
    q = q_ref[...] * jnp.asarray(scale, bf16)
    k = k_ref[...]
    v = v_ref[...]
    do = do_ref[...]
    parts = []
    for head in range(2):
        lanes = head_lanes(rows, head)
        qh = jnp.where(lanes, q, jnp.zeros_like(q))
        doh = jnp.where(lanes, do, jnp.zeros_like(do))
        lse = lse_ref[:, head * HDIM : head * HDIM + 1]
        scores = jnp.where(same, mm(qh, k, NT), masked_score)
        probs = jnp.exp(scores - lse)
        d_probs = mm(doh, v, NT)
        delta = jnp.sum(probs * d_probs, axis=-1, keepdims=True)
        d_scores = (probs * (d_probs - delta)).astype(bf16)
        parts.append(mm(d_scores, k) * scale)
        dk_acc[...] += mm(qh, d_scores, TN)
        dv_acc[...] += mm(doh, probs.astype(bf16), TN)
    dq_ref[...] = jnp.where(head_lanes(rows, 0), parts[0], parts[1]).astype(bf16)

    @pl.when(block == pl.num_programs(1) - 1)
    def _():
        dk_ref[...] = dk_acc[...].T.astype(bf16)
        dv_ref[...] = dv_acc[...].T.astype(bf16)


def attn_specs(rows, pairs, block):
    return (
        pl.BlockSpec((block, 1), lambda h, j: (j, 0)),
        pl.BlockSpec((1, rows), lambda h, j: (0, 0)),
        pl.BlockSpec((block, PAIR), lambda h, j: (j, h)),
        pl.BlockSpec((rows, PAIR), lambda h, j: (0, pairs + h)),
        pl.BlockSpec((rows, PAIR), lambda h, j: (0, 2 * pairs + h)),
    )


def attn_params():
    return pltpu.CompilerParams(
        dimension_semantics=("arbitrary", "arbitrary"), vmem_limit_bytes=56 * 1024 * 1024
    )


def attn_fwd(qkv, seg):
    rows = qkv.shape[0]
    width = qkv.shape[1] // 3
    pairs = width // PAIR
    block = min(512, rows)
    col, row, qs, ks, vs = attn_specs(rows, pairs, block)
    per_block = pl.BlockSpec((block, PAIR), lambda h, j: (j, h))
    return pl.pallas_call(
        attn_fwd_kernel,
        grid=(pairs, rows // block),
        in_specs=[col, row, qs, ks, vs],
        out_specs=[per_block, per_block],
        out_shape=[
            jax.ShapeDtypeStruct((rows, width), bf16),
            jax.ShapeDtypeStruct((rows, width), f32),
        ],
        compiler_params=attn_params(),
        cost_estimate=pl.CostEstimate(
            flops=8 * rows * rows * width,
            bytes_accessed=rows * width * 12,
            transcendentals=rows * rows * width // HDIM,
        ),
        name="attn_fwd",
    )(seg[:, None], seg[None, :], qkv, qkv, qkv)


def attn_bwd(qkv, seg, lse, do):
    rows = qkv.shape[0]
    width = qkv.shape[1] // 3
    pairs = width // PAIR
    block = min(512, rows)
    col, row, qs, ks, vs = attn_specs(rows, pairs, block)
    per_block = pl.BlockSpec((block, PAIR), lambda h, j: (j, h))
    whole = pl.BlockSpec((rows, PAIR), lambda h, j: (0, h))
    return pl.pallas_call(
        attn_bwd_kernel,
        grid=(pairs, rows // block),
        in_specs=[col, row, per_block, qs, ks, vs, per_block],
        out_specs=[per_block, whole, whole],
        out_shape=[jax.ShapeDtypeStruct((rows, width), bf16)] * 3,
        scratch_shapes=[pltpu.VMEM((PAIR, rows), f32), pltpu.VMEM((PAIR, rows), f32)],
        compiler_params=attn_params(),
        cost_estimate=pl.CostEstimate(
            flops=20 * rows * rows * width,
            bytes_accessed=rows * width * 18,
            transcendentals=rows * rows * width // HDIM,
        ),
        name="attn_bwd",
    )(seg[:, None], seg[None, :], lse, qkv, qkv, qkv, do)


def norm_parts(values):
    center = values - jnp.mean(values, axis=-1, keepdims=True)
    factor = lax.rsqrt(jnp.mean(center * center, axis=-1, keepdims=True) + eps)
    return center * factor, factor


def norm_back(cot, normed, factor, gain):
    e = cot * gain
    mean_e = jnp.mean(e, axis=-1, keepdims=True)
    mean_en = jnp.mean(e * normed, axis=-1, keepdims=True)
    return factor * (e - mean_e - normed * mean_en)


def token_segments(group_id, places, seq_len, seq_group, seq_start):
    places = places[None, :]
    starts = seq_start[:, None]
    inside = (
        (seq_group[:, None] == group_id) & (places >= starts) & (places < starts + seq_len[:, None])
    )
    labels = jnp.arange(1, seq_len.shape[0] + 1, dtype=jnp.int32)[:, None]
    return jnp.sum(jnp.where(inside, labels, 0), axis=0) - 1


def gelu_parts(hidden):
    cdf = 0.5 * (1.0 + lax.erf(hidden * (0.5**0.5)))
    slope = cdf + hidden * jnp.exp(-0.5 * hidden * hidden) * (0.5 / jnp.pi) ** 0.5
    return hidden * cdf, slope


def turned(x):
    return lax.ppermute(x, ("core", "y"), [(0, 0), (1, 2), (2, 1), (3, 3)])


def partner(x):
    return lax.ppermute(x, "core", [(0, 1), (1, 0)])


def local(
    tokens,
    w_query,
    w_key,
    w_value,
    w_out,
    w_up,
    w_down,
    b_query,
    b_value,
    b_up,
    b_out,
    b_down,
    gain_attn,
    shift_attn,
    gain_ffn,
    shift_ffn,
    out_grad,
    seq_len,
    seq_group,
    seq_start,
):
    half = tokens.shape[0]
    core = lax.axis_index("core")
    group = lax.axis_index("pair") * 2 + lax.axis_index("y")
    owner = lax.axis_index("pair") * 2 + core
    width = w_query.shape[1]
    hidden_width = w_up.shape[1]

    def gather(x):
        return lax.all_gather(x, ("pair", "y"), axis=0, tiled=True)

    def scatter(x):
        part = lax.psum_scatter(x.astype(bf16), ("pair", "y"), scatter_dimension=0, tiled=True)
        return turned(part).astype(f32)

    qkv_mat = gather(turned(jnp.concatenate([w_query, w_key, w_value], axis=1)))
    small = (b_query, b_value, b_out, b_down, gain_attn, shift_attn, gain_ffn, shift_ffn, b_up)
    vectors = lax.all_gather(jnp.concatenate(small), ("pair", "core"), axis=0, tiled=False)
    own = turned(tokens)
    rows_all = jnp.concatenate([own, partner(own)], axis=0)
    out_mat = gather(turned(w_out))
    up_mat = gather(turned(w_up))
    down_mat = gather(turned(w_down))
    cot_rows = turned(out_grad)

    piece = b_query.shape[0]
    full = [
        vectors[:, i * piece : (i + 1) * piece].reshape(-1).astype(f32) for i in range(8)
    ]
    up_bias = vectors[:, 8 * piece :].reshape(-1).astype(f32)
    query_bias, value_bias, out_bias, down_bias, gain_one, shift_one, gain_two, shift_two = full
    query_local = lax.dynamic_slice_in_dim(query_bias, core * width, width)
    value_local = lax.dynamic_slice_in_dim(value_bias, core * width, width)
    up_local = lax.dynamic_slice_in_dim(up_bias, core * hidden_width, hidden_width)
    qkv_bias = jnp.concatenate([query_local, jnp.zeros((width,), f32), value_local])

    places = jnp.arange(half, dtype=jnp.int32)
    places = jnp.concatenate([places + core * half, places + (1 - core) * half])
    seg = token_segments(group, places, seq_len, seq_group, seq_start)
    alive = (seg[:half] >= 0).astype(f32)[:, None]

    qkv = (mm(rows_all, qkv_mat) + qkv_bias).astype(bf16)
    context, lse = attn_fwd(qkv, seg)

    def summed_rows(left, right, dims):
        sent = partner(mm(left[half:], right, dims).astype(bf16))
        return mm(left[:half], right, dims) + sent.astype(f32)

    attended = summed_rows(context, out_mat, NT)
    n1, r1 = norm_parts(own.astype(f32) + attended + out_bias)
    first = n1 * gain_one + shift_one
    first_own = first.astype(bf16)
    first_all = jnp.concatenate([first_own, partner(first_own)], axis=0)
    hidden = mm(first_all, up_mat) + up_local
    active = gelu_parts(hidden)[0].astype(bf16)
    branch = summed_rows(active, down_mat, NT)
    n2, r2 = norm_parts(first + branch + down_bias)
    layer_out = turned(((n2 * gain_two + shift_two) * alive).astype(bf16))

    cot = cot_rows.astype(f32) * alive
    d_second = norm_back(cot, n2, r2, gain_two)
    d_branch_own = d_second.astype(bf16)
    d_branch = jnp.concatenate([d_branch_own, partner(d_branch_own)], axis=0)
    d_hidden = (mm(d_branch, down_mat) * gelu_parts(hidden)[1]).astype(bf16)
    grad_down = scatter(mm(d_branch, active, TN))
    d_first = d_second + summed_rows(d_hidden, up_mat, NT)
    grad_up = scatter(mm(first_all, d_hidden, TN))
    d_first_in = norm_back(d_first, n1, r1, gain_one)
    d_attn_own = d_first_in.astype(bf16)
    d_attn = jnp.concatenate([d_attn_own, partner(d_attn_own)], axis=0)
    d_context = mm(d_attn, out_mat).astype(bf16)
    grad_out = scatter(mm(d_attn, context, TN))
    d_query, d_keys, d_values = attn_bwd(qkv, seg, lse, d_context)
    d_qkv = jnp.concatenate([d_query, d_keys, d_values], axis=1)
    grad_qkv = scatter(mm(rows_all, d_qkv, TN))
    d_rows = d_first_in + summed_rows(d_qkv, qkv_mat, NT)
    grad_tokens = turned(d_rows.astype(bf16)).astype(f32)

    def widen(vector):
        total = jnp.zeros((2 * vector.shape[0],), f32)
        return lax.dynamic_update_slice_in_dim(total, vector, core * vector.shape[0], 0)

    sums = (
        widen(jnp.sum(d_query.astype(f32), axis=0)),
        widen(jnp.sum(d_values.astype(f32), axis=0)),
        jnp.sum(d_first_in, axis=0),
        jnp.sum(d_second, axis=0),
        jnp.sum(d_first * n1, axis=0),
        jnp.sum(d_first, axis=0),
        jnp.sum(cot * n2, axis=0),
        jnp.sum(cot, axis=0),
        widen(jnp.sum(d_hidden.astype(f32), axis=0)),
    )
    packed = jnp.concatenate([item.reshape(vectors.shape[0], -1) for item in sums], axis=1)
    totals = lax.psum(packed, ("pair", "core", "y"))
    mine = lax.dynamic_index_in_dim(totals, owner, 0, keepdims=False)
    parts = [mine[i * piece : (i + 1) * piece] for i in range(8)]
    grad_b_query, grad_b_value, grad_b_out, grad_b_down = parts[:4]
    return (
        layer_out,
        grad_tokens,
        grad_qkv[:, :width],
        grad_qkv[:, width : 2 * width],
        grad_qkv[:, 2 * width :],
        grad_out,
        grad_up,
        grad_down,
        grad_b_query,
        grad_b_value,
        mine[8 * piece :],
        grad_b_out,
        grad_b_down,
        parts[4],
        parts[5],
        parts[6],
        parts[7],
    )


def solution(mesh):
    dp, mp = mesh.devices.shape
    folded = Mesh(mesh.devices.reshape(dp // 2, 2, mp), ("pair", "core", "y"))
    rows = P(("pair", "core", "y"), None)
    weight = P(("pair", "core"), "y")
    vector = P(("pair", "core"))
    placed = (rows,) + (weight,) * 6 + (vector,) * 9 + (rows,) + (P(),) * 3
    return jax.shard_map(
        local,
        mesh=folded,
        in_specs=placed,
        out_specs=(rows, rows) + (weight,) * 6 + (vector,) * 9,
        check_vma=False,
    )
```

time: 1270 us -> 821 us (0.65)
  waiting for transfers between devices: 811 us -> 508 us
  matrix products: 193 us -> 89.6 us
  blocking collectives: 143 us -> 57.8 us
  starting transfers between devices: 1.46 us -> 53.5 us
  Pallas kernels: 0 us -> 48.9 us
  other arithmetic: 57.8 us -> 13.9 us
    unnamed x23 -> x8, waiting for transfers between devices: 200 us -> 0.13 us
    unnamed x2 -> x0, blocking collectives: 116 us -> none
    dot_general x30 -> x16, matrix products: 193 us -> 89.6 us  [mm(): return lax.dot_general(left, right, dims, preferred_element_type=f32)]
    reduce_scatter x7 -> x4, waiting for transfers between devices: 378 us -> 294 us  [scatter(): lax.psum_scatter(x.astype(bf16), ('pair', 'y'), scatter_dimension=0, tile...]
    all_gather x10 -> x4, waiting for transfers between devices: 233 us -> 162 us  [gather(): return lax.all_gather(x, ('pair', 'y'), axis=0, tiled=True)]
    ppermute x0 -> x20, starting transfers between devices: none -> 53 us  [the longest x12 47.7 us: turned(): return lax.ppermute(x, ('core', 'y'), [(0, 0), (1, 2), (2, 1), (3, 3)])]
    ppermute x0 -> x20, waiting for transfers between devices: none -> 52.3 us  [the longest x12 42.4 us: turned(): return lax.ppermute(x, ('core', 'y'), [(0, 0), (1, 2), (2, 1), (3, 3)])]
    pallas_call x0 -> x2, Pallas kernels: none -> 48.9 us  [the longest x1 28.4 us: attn_bwd(): pl.pallas_call(attn_bwd_kernel, grid=(pairs, rows // block), in_specs=[co...]
  transfers between devices with their start and end apart: 20 -> 28, of which waited for: 18 -> 17; matrix products, arithmetic and copies ran while one was open for 10% -> 10% of each run, Pallas kernels for 0% -> 3%
where the time goes in v1:
time: 821 us; the launch traced here: 810 us
  waiting for transfers between devices  508 us (62%)
  matrix products  89.6 us (11%)
  blocking collectives  57.8 us (7%)
  starting transfers between devices  53.5 us (7%)
  Pallas kernels  48.9 us (6%)
  local copies, waits for them, and re-layouts  24.2 us (3%)
  between operations  14.8 us (2%)
  other arithmetic  13.9 us (2%)
    reduce_scatter x4, waiting for transfers between devices, scatter(): lax.psum_scatter(x.astype(bf16), ('pair', 'y'), scatter_dimension=0, tile...  294 us
    all_gather x4, waiting for transfers between devices, gather(): return lax.all_gather(x, ('pair', 'y'), axis=0, tiled=True)  162 us
    dot_general x16, matrix products, mm(): return lax.dot_general(left, right, dims, preferred_element_type=f32)  89.6 us
    ppermute x12, starting transfers between devices, turned(): return lax.ppermute(x, ('core', 'y'), [(0, 0), (1, 2), (2, 1), (3, 3)])  47.7 us
    ppermute x12, waiting for transfers between devices, turned(): return lax.ppermute(x, ('core', 'y'), [(0, 0), (1, 2), (2, 1), (3, 3)])  42.4 us
    psum x1, blocking collectives, local(): totals = lax.psum(packed, ('pair', 'core', 'y'))  39.1 us
    pallas_call x1, Pallas kernels, attn_bwd(): pl.pallas_call(attn_bwd_kernel, grid=(pairs, rows // block), in_specs=[co...  28.4 us
    pallas_call x1, Pallas kernels, attn_fwd(): pl.pallas_call(attn_fwd_kernel, grid=(pairs, rows // block), in_specs=[co...  20.5 us
  transfers between devices with their start and end apart: 28, of which 17 were waited for; matrix products, arithmetic and copies ran while one was open for 10% of the time, Pallas kernels for 3%

profile of v1, /device:TPU:1, one launch (start us, length us, event | category | flops | bytes accessed | tf_op | source)
XLA Modules:
  0.0 810.4 jit_solution(1333813896085137574)
XLA Ops:
  7.2 0.9 pad_maximum_fusion.9
  8.2 4.5 collective-permute-start.2
  12.7 3.3 collective-permute-done.2
  16.8 3.6 collective-permute-start.3
  20.4 2.1 collective-permute-done.3
  23.3 3.6 collective-permute-start.6
  26.9 5.7 collective-permute-done.6
  33.4 3.5 collective-permute-start
  36.9 2.1 collective-permute-start.7
  39.0 16.8 %collective-permute-done.7 = bf16[64,2048]{1,0:T(8,128)(2,1)S(1)} collective-permute-done((bf16[64,2048]{1,0:T(8,128)(2,1)}, bf16[64,2048]{1,0:T(8,128)(2,1)S(1)}, u32[]{:S(2)}, u32[]{:S(2)}) %collective-permute-start.7) | collective-permute-done | bytes 262176 | tf_op jit(solution)/shard_map/ppermute | solution.py:184
  56.5 6.1 concatenate.33
  62.6 18.7 %all-gather.1 = bf16[16,1,768]{2,1,0:T(2,128)(2,1)S(1)} all-gather(bf16[1,1,768]{2,1,0:T(2,128)(2,1)S(1)} %reshape.217), channel_id=2, replica_groups=mesh['pair'=8,'core'=2,'y'=2] {'pair','core'}, dimensions={0}, use_global_device_ids=true | all-gather | bytes 26112 | tf_op jit(solution)/shard_map/all_gather | solution.py:229
  84.2 1.0 copy.41.seg_col
  85.2 1.0 constant_dynamic-update-slice_fusion.1
  86.3 1.0 constant_dynamic-update-slice_fusion
  87.3 7.6 add_convert_fusion.q_ref.k_ref.v_ref
  95.0 20.5 %attn_fwd.1 = (bf16[1024,512]{1,0:T(8,128)(2,1)}, f32[1024,512]{1,0:T(8,128)}) custom-call(s32[1024,1]{1,0:T(8,128)} %copy.41.seg_col, s32[1,1024]{1,0:T(1,128)} %bitcast.47, bf16[1024,1536]{1,0:T(8,128)(2,1)} %add_convert_fusion.q_ref.k_ref.v_ref, bf16[1024,1536]{1,0:T(8,128)(2,1)} %add_convert_fusion.q_ref.k_ref.v_ref, ...), custom_call_target="tpu_custom_call" | custom-call | flops 4294967296 | bytes 6291456 | tf_op jit(solution)/shard_map/attn_fwd/pallas_call | solution.py:110
  115.4 27.5 %all-gather.9.cloned.1.call-done = bf16[1024,512]{1,0:T(8,128)(2,1)} async-done(((bf16[64,512]{1,0:T(8,128)(2,1)}), bf16[1024,512]{1,0:T(8,128)(2,1)}) %all-gather.9.cloned.1.call-update) | async-done | bytes 1048592 | tf_op jit(solution)/shard_map/all_gather | solution.py:221
  142.9 2.1 convolution_convert_fusion.5
  145.0 2.0 collective-permute-start.4
  147.3 2.2 collective-permute-done.4
  149.5 2.6 fusion.50
  153.4 67.2 %all-gather.11.cloned.1.call-done = bf16[1024,2048]{1,0:T(8,128)(2,1)} async-done(((bf16[64,2048]{1,0:T(8,128)(2,1)}), bf16[1024,2048]{1,0:T(8,128)(2,1)}) %all-gather.11.cloned.1.call-update) | async-done | bytes 4194320 | tf_op jit(solution)/shard_map/all_gather | solution.py:221
  220.6 10.5 %multiply_convert_fusion = (bf16[1024,2048]{1,0:T(8,128)(2,1)}, f32[1024,2048]{1,0:T(8,128)}) fusion(f32[2048]{0:T(1024)S(1)} %dynamic_slice.15, bf16[1024,2048]{1,0:T(8,128)(2,1)} %all-gather.11.cloned.1.call-done, bf16[512,1024]{1,0:T(8,128)(2,1)} %collective-permute-done.5, bf16[512,1024]{1,0:T(8,128)(2,1)S(1)} %fusion.17), kind=kOutput, calls=%fused_computation.8 | convolution fusion | flops 4311744512 | bytes 18882560 | tf_op jit(solution)/shard_map/dot_general | solution.py:21
  231.1 67.3 %all-gather.13.cloned.1.call-done = bf16[1024,2048]{1,0:T(8,128)(2,1)} async-done(((bf16[64,2048]{1,0:T(8,128)(2,1)}), bf16[1024,2048]{1,0:T(8,128)(2,1)}) %all-gather.13.cloned.1.call-update) | async-done | bytes 4194320 | tf_op jit(solution)/shard_map/all_gather | solution.py:221
  298.3 6.2 fusion.29
  304.5 1.9 collective-permute-start.8
  306.4 3.2 collective-permute-start.10
  309.8 5.8 fusion.51
  316.0 6.7 collective-permute-done.10
  322.7 1.1 multiply_reduce_fusion
  323.8 1.9 fusion.47
  326.0 2.6 collective-permute-done.11
  328.7 8.7 %convert_reduce_fusion = (f32[2048]{0:T(1024)S(1)}, bf16[1024,2048]{1,0:T(8,128)(2,1)S(1)}) fusion(f32[1024,2048]{1,0:T(8,128)S(1)} %copy-done.21, f32[2048]{0:T(1024)S(1)} %dynamic_slice.15, bf16[1024,2048]{1,0:T(8,128)(2,1)S(1)} %copy-done.15, bf16[512,1024]{1,0:T(8,128)(2,1)S(1)} %collective-permute-done.11, bf16[512,1024]{1,0:T(8,128)(2,1)S(1)} %convert_element_type.203), kind=kOutput, calls=%fused_computation.7 | convolution fusion | flops 4326422528 | bytes 18890752 | tf_op jit(solution)/shard_map/dot_general | solution.py:21
  337.4 2.4 fusion.32
  340.0 2.5 collective-permute-done.12
  342.5 3.2 multiply_reduce_fusion.1
  346.8 2.5 collective-permute-done.13
  349.3 2.3 convolution_convert_fusion.4.do_ref
  351.5 28.4 %attn_bwd.1 = (bf16[1024,512]{1,0:T(8,128)(2,1)}, bf16[1024,512]{1,0:T(8,128)(2,1)}, bf16[1024,512]{1,0:T(8,128)(2,1)}) custom-call(s32[1024,1]{1,0:T(8,128)} %copy.41.seg_col, s32[1,1024]{1,0:T(1,128)} %bitcast.48, f32[1024,512]{1,0:T(8,128)} %get-tuple-element.23.lse_ref, bf16[1024,1536]{1,0:T(8,128)(2,1)} %add_convert_fusion.q_ref.k_ref.v_ref, ...), custom_call_target="tpu_custom_call" | custom-call | flops 10737418240 | bytes 9437184 | tf_op jit(solution)/shard_map/attn_bwd/pallas_call | solution.py:137
  380.0 2.5 constant_dynamic-update-slice_fusion.4
  382.5 1.2 constant_dynamic-update-slice_fusion.3
  383.6 1.1 constant_dynamic-update-slice_fusion.2
  384.7 7.6 convolution_convert_fusion
  392.4 3.8 convolution_convert_fusion.3
  396.5 9.1 %convolution_convert_fusion.1 = bf16[1024,2048]{1,0:T(8,128)(2,1)} fusion(bf16[1024,2048]{1,0:T(8,128)(2,1)} %get-tuple-element.61, bf16[512,1024]{1,0:T(8,128)(2,1)} %copy-done.18, bf16[512,1024]{1,0:T(8,128)(2,1)S(1)} %convert_element_type.203), kind=kOutput, calls=%fused_computation.12 | convolution fusion | flops 4301258752 | bytes 10485760 | tf_op jit(solution)/shard_map/dot_general | solution.py:21
  405.6 1.2 copy-done.6
  406.8 9.1 %convolution_convert_fusion.2 = bf16[1024,2048]{1,0:T(8,128)(2,1)} fusion(bf16[1024,2048]{1,0:T(8,128)(2,1)} %copy-done.20, bf16[512,1024]{1,0:T(8,128)(2,1)} %collective-permute-done.5, bf16[512,1024]{1,0:T(8,128)(2,1)S(1)} %copy-done.6), kind=kOutput, calls=%fused_computation.13 | convolution fusion | flops 4301258752 | bytes 10485760 | tf_op jit(solution)/shard_map/dot_general | solution.py:21
  416.0 4.4 fusion.26
  420.5 3.1 collective-permute-start.9
  423.7 4.2 add_convert_fusion.1
  427.9 2.6 collective-permute-start.15
  430.9 7.7 collective-permute-done.9
  439.0 80.8 %reduce-scatter.5.cloned.1.call-done = bf16[64,1536]{1,0:T(8,128)(2,1)} async-done(((bf16[1024,1536]{1,0:T(8,128)(2,1)}), bf16[64,1536]{1,0:T(8,128)(2,1)}) %reduce-scatter.5.cloned.1.call-update) | async-done | bytes 196624 | tf_op jit(solution)/shard_map/reduce_scatter | solution.py:224
  519.8 5.2 collective-permute-start.16
  525.8 39.1 %psum.7 = f32[16,768]{1,0:T(8,128)S(1)} all-reduce(f32[16,768]{1,0:T(8,128)S(1)} %concatenate.39), channel_id=1, replica_groups=mesh['pair'=8,'core'=2,'y'=2] {'pair','core','y'}, use_global_device_ids=true, to_apply=%region_22.23 | all-reduce | flops 12288 | bytes 98304 | tf_op jit(solution)/shard_map/psum | solution.py:306
  564.9 24.9 %reduce-scatter.7.cloned.1.call-done = bf16[64,512]{1,0:T(8,128)(2,1)} async-done(((bf16[1024,512]{1,0:T(8,128)(2,1)}), bf16[64,512]{1,0:T(8,128)(2,1)}) %reduce-scatter.7.cloned.1.call-update) | async-done | bytes 65552 | tf_op jit(solution)/shard_map/reduce_scatter | solution.py:224
  589.8 10.5 %collective-permute-start.17 = (bf16[64,512]{1,0:T(8,128)(2,1)}, bf16[64,512]{1,0:T(8,128)(2,1)S(1)}, u32[]{:S(2)}, u32[]{:S(2)}) collective-permute-start(bf16[64,512]{1,0:T(8,128)(2,1)} %reduce-scatter.7.cloned.1.call-done), channel_id=1, source_target_pairs={{0,0},{1,2},{2,1},{3,3},{4,4},{5,6},{6,5},{7,7},{8,8},{9,10},{10,9... | collective-permute-start | bytes 196616 | tf_op jit(solution)/shard_map/ppermute | solution.py:184
  600.4 94.1 %reduce-scatter.11.cloned.1.call-done = bf16[64,2048]{1,0:T(8,128)(2,1)} async-done(((bf16[1024,2048]{1,0:T(8,128)(2,1)}), bf16[64,2048]{1,0:T(8,128)(2,1)}) %reduce-scatter.11.cloned.1.call-update) | async-done | bytes 262160 | tf_op jit(solution)/shard_map/reduce_scatter | solution.py:224
  694.5 3.2 collective-permute-start.19
  697.6 93.8 %reduce-scatter.9.cloned.1.call-done = bf16[64,2048]{1,0:T(8,128)(2,1)} async-done(((bf16[1024,2048]{1,0:T(8,128)(2,1)}), bf16[64,2048]{1,0:T(8,128)(2,1)}) %reduce-scatter.9.cloned.1.call-update) | async-done | bytes 262160 | tf_op jit(solution)/shard_map/reduce_scatter | solution.py:224
  791.4 2.5 collective-permute-start.18
  795.3 2.8 convert_element_type.212
  801.1 2.3 copy.54
  (140 shorter events, 16.1 us)
Async XLA Ops:
  7.2 80.1 %all-gather.7.cloned.1.call-start = ((), (), s32[]{:S(2)}) async-start(), calls=%async_computation.4 | async-start | bytes 3342336 | tf_op jit(solution)/shard_map/all_gather | solution.py:221
  8.2 7.9 collective-permute-start.2
  16.0 0.7 copy-start.10
  16.7 126.2 %all-gather.9.cloned.1.call-start = ((), (), s32[]{:S(2)}) async-start(), calls=%async_computation.5 | async-start | bytes 1114112 | tf_op jit(solution)/shard_map/all_gather | solution.py:221
  16.8 5.8 collective-permute-start.3
  22.6 0.6 copy-start.11
  23.2 197.3 %all-gather.11.cloned.1.call-start = ((), (), s32[]{:S(2)}) async-start(), calls=%async_computation.6 | async-start | bytes 4456448 | tf_op jit(solution)/shard_map/all_gather | solution.py:221
  23.3 9.3 %collective-permute-start.6 = (bf16[64,2048]{1,0:T(8,128)(2,1)}, bf16[64,2048]{1,0:T(8,128)(2,1)S(1)}, u32[]{:S(2)}, u32[]{:S(2)}) collective-permute-start(bf16[64,2048]{1,0:T(8,128)(2,1)} %param.25), channel_id=1, source_target_pairs={{0,0},{1,2},{2,1},{3,3},{4,4},{5,6},{6,5},{7,7},{8,8},{9,10},{10,9... | collective-permute-start | bytes 786440 | tf_op jit(solution)/shard_map/ppermute | solution.py:184
  32.6 0.7 copy-start.8
  33.3 265.0 %all-gather.13.cloned.1.call-start = ((), (), s32[]{:S(2)}) async-start(), calls=%async_computation.7 | async-start | bytes 4456448 | tf_op jit(solution)/shard_map/all_gather | solution.py:221
  33.4 48.3 %collective-permute-start = (bf16[512,1024]{1,0:T(8,128)(2,1)}, bf16[512,1024]{1,0:T(8,128)(2,1)S(1)}, u32[]{:S(2)}, u32[]{:S(2)}) collective-permute-start(bf16[512,1024]{1,0:T(8,128)(2,1)} %param.20), channel_id=1, source_target_pairs={{0,0},{1,2},{2,1},{3,3},{4,4},{5,6},{6,5},{7,7},{8,8},{9,10},{10,9... | collective-permute-start | bytes 3145736 | tf_op jit(solution)/shard_map/ppermute | solution.py:184
  36.9 18.9 %collective-permute-start.7 = (bf16[64,2048]{1,0:T(8,128)(2,1)}, bf16[64,2048]{1,0:T(8,128)(2,1)S(1)}, u32[]{:S(2)}, u32[]{:S(2)}) collective-permute-start(bf16[64,2048]{1,0:T(8,128)(2,1)} %param.26), channel_id=1, source_target_pairs={{0,0},{1,2},{2,1},{3,3},{4,4},{5,6},{6,5},{7,7},{8,8},{9,10},{10,9... | collective-permute-start | bytes 786440 | tf_op jit(solution)/shard_map/ppermute | solution.py:184
  55.7 0.7 copy-start.9
  56.5 463.4 %reduce-scatter.5.cloned.1.call-start = ((), (), s32[]{:S(2)}) async-start(), calls=%async_computation.8 | async-start | bytes 3342336 | tf_op jit(solution)/shard_map/reduce_scatter | solution.py:224
  81.7 4.6 collective-permute-start.1
  84.2 3.1 copy-start.12
  145.0 4.5 collective-permute-start.4
  152.9 78.2 %copy-start.5 = (bf16[512,1024]{1,0:T(8,128)(2,1)}, bf16[512,1024]{1,0:T(8,128)(2,1)S(1)}, u32[]{:S(2)}) copy-start(bf16[512,1024]{1,0:T(8,128)(2,1)S(1)} %fusion.17) | copy-start | bytes 3145732
  152.9 67.6 %collective-permute-start.5 = (bf16[512,1024]{1,0:T(8,128)(2,1)S(1)}, bf16[512,1024]{1,0:T(8,128)(2,1)}, u32[]{:S(2)}, u32[]{:S(2)}) collective-permute-start(bf16[512,1024]{1,0:T(8,128)(2,1)S(1)} %fusion.17), channel_id=1, source_target_pairs={{0,2},{2,0},{1,3},{3,1},{4,6},{6,4},{5,7},{7,5},{8,10},{10,8},{9,1... | collective-permute-start | bytes 3145736 | tf_op jit(solution)/shard_map/ppermute | solution.py:188
  298.3 11.5 %copy-start.13 = (s32[1024]{0:T(1024)S(1)}, s32[1024]{0:T(1024)}, u32[]{:S(2)}) copy-start(s32[1024]{0:T(1024)} %copy-done.12) | copy-start | bytes 12292
  304.5 5.3 collective-permute-start.8
  306.4 16.3 %collective-permute-start.10 = (bf16[512,1024]{1,0:T(8,128)(2,1)}, bf16[512,1024]{1,0:T(8,128)(2,1)S(1)}, u32[]{:S(2)}, u32[]{:S(2)}) collective-permute-start(bf16[512,1024]{1,0:T(8,128)(2,1)} %param.36), channel_id=1, source_target_pairs={{0,0},{1,2},{2,1},{3,3},{4,4},{5,6},{6,5},{7,7},{8,8},{9,10},{10,9... | collective-permute-start | bytes 3145736 | tf_op jit(solution)/shard_map/ppermute | solution.py:184
  322.7 6.0 copy-start.21
  323.8 4.8 copy-start.15
  325.9 2.7 collective-permute-start.11
  328.6 8.7 %copy-start.18 = (bf16[512,1024]{1,0:T(8,128)(2,1)}, bf16[512,1024]{1,0:T(8,128)(2,1)S(1)}, u32[]{:S(2)}) copy-start(bf16[512,1024]{1,0:T(8,128)(2,1)S(1)} %collective-permute-done.11) | copy-start | bytes 3145732
  328.6 8.7 %copy-start.14 = (bf16[1024,2048]{1,0:T(8,128)(2,1)S(1)}, bf16[1024,2048]{1,0:T(8,128)(2,1)}, u32[]{:S(2)}) copy-start(bf16[1024,2048]{1,0:T(8,128)(2,1)} %all-gather.11.cloned.1.call-done) | copy-start | bytes 12582916
  337.4 5.1 copy-start.20
  339.8 2.7 collective-permute-start.12
  346.4 5.2 copy-start
  346.4 2.9 copy-start.17
  346.5 2.7 collective-permute-start.13
  349.3 2.3 copy-start.19
  379.9 2.5 copy-start.7
  380.0 3.7 copy-start.2
  392.4 197.4 %reduce-scatter.7.cloned.1.call-start = ((), (), s32[]{:S(2)}) async-start(), calls=%async_computation.9 | async-start | bytes 1114112 | tf_op jit(solution)/shard_map/reduce_scatter | solution.py:224
  396.2 298.2 %reduce-scatter.11.cloned.1.call-start = ((), (), s32[]{:S(2)}) async-start(), calls=%async_computation.11 | async-start | bytes 4456448 | tf_op jit(solution)/shard_map/reduce_scatter | solution.py:224
  405.6 1.2 copy-start.6
  405.6 385.8 %reduce-scatter.9.cloned.1.call-start = ((), (), s32[]{:S(2)}) async-start(), calls=%async_computation.10 | async-start | bytes 4456448 | tf_op jit(solution)/shard_map/reduce_scatter | solution.py:224
  415.9 4.6 copy-start.4
  415.9 7.7 copy-start.1
  416.0 7.7 copy-start.16
  420.3 3.3 collective-permute-start.14
  420.5 18.3 %copy-start.3 = (bf16[1024,512]{1,0:T(8,128)(2,1)S(1)}, bf16[1024,512]{1,0:T(8,128)(2,1)}, u32[]{:S(2)}) copy-start(bf16[1024,512]{1,0:T(8,128)(2,1)} %get-tuple-element.24) | copy-start | bytes 3145732
  420.5 18.1 %collective-permute-start.9 = (bf16[512,1024]{1,0:T(8,128)(2,1)S(1)}, bf16[512,1024]{1,0:T(8,128)(2,1)}, u32[]{:S(2)}, u32[]{:S(2)}) collective-permute-start(bf16[512,1024]{1,0:T(8,128)(2,1)S(1)} %copy-done.4), channel_id=1, source_target_pairs={{0,0},{1,2},{2,1},{3,3},{4,4},{5,6},{6,5},{7,7},{8,8},{9,10},{10,9... | collective-permute-start | bytes 3145736 | tf_op jit(solution)/shard_map/ppermute | solution.py:184
  427.9 367.4 %collective-permute-start.15 = (bf16[512,1024]{1,0:T(8,128)(2,1)}, bf16[512,1024]{1,0:T(8,128)(2,1)}, u32[]{:S(2)}, u32[]{:S(2)}) collective-permute-start(bf16[512,1024]{1,0:T(8,128)(2,1)} %add_convert_fusion.1), channel_id=1, source_target_pairs={{0,0},{1,2},{2,1},{3,3},{4,4},{5,6},{6,5},{7,7},{8,8},{9,10},{10,9... | collective-permute-start | bytes 3145736 | tf_op jit(solution)/shard_map/ppermute | solution.py:184
  519.8 278.9 %collective-permute-start.16 = (bf16[64,1536]{1,0:T(8,128)(2,1)}, bf16[64,1536]{1,0:T(8,128)(2,1)S(1)}, u32[]{:S(2)}, u32[]{:S(2)}) collective-permute-start(bf16[64,1536]{1,0:T(8,128)(2,1)} %reduce-scatter.5.cloned.1.call-done), channel_id=1, source_target_pairs={{0,0},{1,2},{2,1},{3,3},{4,4},{5,6},{6,5},{7,7},{8,8},{9,10},{10,9... | collective-permute-start | bytes 589832 | tf_op jit(solution)/shard_map/ppermute | solution.py:184
  589.8 208.2 %collective-permute-start.17 = (bf16[64,512]{1,0:T(8,128)(2,1)}, bf16[64,512]{1,0:T(8,128)(2,1)S(1)}, u32[]{:S(2)}, u32[]{:S(2)}) collective-permute-start(bf16[64,512]{1,0:T(8,128)(2,1)} %reduce-scatter.7.cloned.1.call-done), channel_id=1, source_target_pairs={{0,0},{1,2},{2,1},{3,3},{4,4},{5,6},{6,5},{7,7},{8,8},{9,10},{10,9... | collective-permute-start | bytes 196616 | tf_op jit(solution)/shard_map/ppermute | solution.py:184
  694.5 105.0 %collective-permute-start.19 = (bf16[64,2048]{1,0:T(8,128)(2,1)}, bf16[64,2048]{1,0:T(8,128)(2,1)S(1)}, u32[]{:S(2)}, u32[]{:S(2)}) collective-permute-start(bf16[64,2048]{1,0:T(8,128)(2,1)} %reduce-scatter.11.cloned.1.call-done), channel_id=1, source_target_pairs={{0,0},{1,2},{2,1},{3,3},{4,4},{5,6},{6,5},{7,7},{8,8},{9,10},{10,9... | collective-permute-start | bytes 786440 | tf_op jit(solution)/shard_map/ppermute | solution.py:184
  791.4 8.9 %collective-permute-start.18 = (bf16[64,2048]{1,0:T(8,128)(2,1)}, bf16[64,2048]{1,0:T(8,128)(2,1)S(1)}, u32[]{:S(2)}, u32[]{:S(2)}) collective-permute-start(bf16[64,2048]{1,0:T(8,128)(2,1)} %reduce-scatter.9.cloned.1.call-done), channel_id=1, source_target_pairs={{0,0},{1,2},{2,1},{3,3},{4,4},{5,6},{6,5},{7,7},{8,8},{9,10},{10,9... | collective-permute-start | bytes 786440 | tf_op jit(solution)/shard_map/ppermute | solution.py:184
Sparse Core Ops, SparseCore 0:
  16.9 69.1 all-gather.6
  89.4 53.4 all-gather.8
  145.7 74.8 all-gather.10
  223.8 74.5 all-gather.12
  392.5 127.2 reduce-scatter.4
  522.5 67.2 reduce-scatter.6
  592.2 102.2 reduce-scatter.10
  696.9 94.5 reduce-scatter.8

commit v2 on v1

--- a/solution.py
+++ b/solution.py
@@ -213,25 +213,50 @@
     half = tokens.shape[0]
     core = lax.axis_index("core")
     group = lax.axis_index("pair") * 2 + lax.axis_index("y")
-    owner = lax.axis_index("pair") * 2 + core
     width = w_query.shape[1]
     hidden_width = w_up.shape[1]
 
+    side = lax.axis_index("y")
+    pairs = lax.axis_size("pair")
+    sheet = 16
+
+    def across(x):
+        return lax.ppermute(x, "y", [(0, 1), (1, 0)])
+
     def gather(x):
-        return lax.all_gather(x, ("pair", "y"), axis=0, tiled=True)
+        shard = turned(x)
+        mine = lax.all_gather(shard, "pair", axis=0, tiled=False)
+        other = across(mine)
+        low = jnp.where(side == 0, mine, other)
+        high = jnp.where(side == 0, other, mine)
+        return jnp.stack([low, high], axis=1)
 
     def scatter(x):
-        part = lax.psum_scatter(x.astype(bf16), ("pair", "y"), scatter_dimension=0, tiled=True)
+        blocks = x.reshape(pairs, 2, -1, x.shape[-1])
+        sent = across(lax.dynamic_index_in_dim(blocks, 1 - side, 1, keepdims=False))
+        kept = lax.dynamic_index_in_dim(blocks, side, 1, keepdims=False)
+        total = (kept.astype(f32) + sent.astype(f32)).astype(bf16)
+        total = total.reshape(-1, x.shape[-1])
+        part = lax.psum_scatter(total, "pair", scatter_dimension=0, tiled=True)
         return turned(part).astype(f32)
 
-    qkv_mat = gather(turned(jnp.concatenate([w_query, w_key, w_value], axis=1)))
+    def whole_matrix(x):
+        return x.reshape(-1, x.shape[-1])
+
+    shard_rows = w_query.shape[0]
     small = (b_query, b_value, b_out, b_down, gain_attn, shift_attn, gain_ffn, shift_ffn, b_up)
-    vectors = lax.all_gather(jnp.concatenate(small), ("pair", "core"), axis=0, tiled=False)
+    small = jnp.concatenate(small)
+    small_size = small.shape[0]
+    extra = jnp.pad(small[None, :], ((0, sheet - 1), (0, 3 * width - small_size)))
+    qkv_shard = jnp.concatenate([w_query, w_key, w_value], axis=1)
+    qkv_full = gather(jnp.concatenate([qkv_shard, extra], axis=0))
+    qkv_mat = whole_matrix(qkv_full[:, :, :shard_rows])
+    vectors = qkv_full[:, :, shard_rows, :small_size].reshape(-1, small_size)
     own = turned(tokens)
     rows_all = jnp.concatenate([own, partner(own)], axis=0)
-    out_mat = gather(turned(w_out))
-    up_mat = gather(turned(w_up))
-    down_mat = gather(turned(w_down))
+    out_mat = whole_matrix(gather(w_out))
+    up_mat = whole_matrix(gather(w_up))
+    down_mat = whole_matrix(gather(w_down))
     cot_rows = turned(out_grad)
 
     piece = b_query.shape[0]
@@ -273,17 +298,23 @@
     d_branch_own = d_second.astype(bf16)
     d_branch = jnp.concatenate([d_branch_own, partner(d_branch_own)], axis=0)
     d_hidden = (mm(d_branch, down_mat) * gelu_parts(hidden)[1]).astype(bf16)
-    grad_down = scatter(mm(d_branch, active, TN))
+    part_down = mm(d_branch, active, TN).astype(bf16)
+    d_hidden, part_down = lax.optimization_barrier((d_hidden, part_down))
+    grad_down = scatter(part_down)
     d_first = d_second + summed_rows(d_hidden, up_mat, NT)
-    grad_up = scatter(mm(first_all, d_hidden, TN))
+    part_up = mm(first_all, d_hidden, TN).astype(bf16)
+    d_first, part_up = lax.optimization_barrier((d_first, part_up))
+    grad_up = scatter(part_up)
     d_first_in = norm_back(d_first, n1, r1, gain_one)
     d_attn_own = d_first_in.astype(bf16)
     d_attn = jnp.concatenate([d_attn_own, partner(d_attn_own)], axis=0)
     d_context = mm(d_attn, out_mat).astype(bf16)
-    grad_out = scatter(mm(d_attn, context, TN))
+    part_out = mm(d_attn, context, TN).astype(bf16)
+    d_context, part_out = lax.optimization_barrier((d_context, part_out))
+    grad_out = scatter(part_out)
     d_query, d_keys, d_values = attn_bwd(qkv, seg, lse, d_context)
     d_qkv = jnp.concatenate([d_query, d_keys, d_values], axis=1)
-    grad_qkv = scatter(mm(rows_all, d_qkv, TN))
+    part_qkv = mm(rows_all, d_qkv, TN).astype(bf16)
     d_rows = d_first_in + summed_rows(d_qkv, qkv_mat, NT)
     grad_tokens = turned(d_rows.astype(bf16)).astype(f32)
 
@@ -303,8 +334,13 @@
         widen(jnp.sum(d_hidden.astype(f32), axis=0)),
     )
     packed = jnp.concatenate([item.reshape(vectors.shape[0], -1) for item in sums], axis=1)
-    totals = lax.psum(packed, ("pair", "core", "y"))
-    mine = lax.dynamic_index_in_dim(totals, owner, 0, keepdims=False)
+    packed = (packed + partner(packed)).astype(bf16)
+    packed = jnp.pad(packed[:, None, :], ((0, 0), (0, sheet - 1), (0, 3 * width - small_size)))
+    part_qkv = part_qkv.reshape(packed.shape[0], shard_rows, 3 * width)
+    part_qkv = jnp.concatenate([part_qkv, packed], axis=1)
+    grad_qkv = scatter(whole_matrix(part_qkv))
+    mine = grad_qkv[shard_rows, :small_size]
+    grad_qkv = grad_qkv[:shard_rows]
     parts = [mine[i * piece : (i + 1) * piece] for i in range(8)]
     grad_b_query, grad_b_value, grad_b_out, grad_b_down = parts[:4]
     return (

time: 821 us -> 668 us (0.81)
  waiting for transfers between devices: 508 us -> 348 us
  blocking collectives: 57.8 us -> 24.8 us
  other arithmetic: 13.9 us -> 37.4 us
  starting transfers between devices: 53.5 us -> 66.2 us
    reduce_scatter x4, waiting for transfers between devices: 294 us -> 116 us  [scatter(): part = lax.psum_scatter(total, 'pair', scatter_dimension=0, tiled=True)]
    ppermute x0 -> x8, waiting for transfers between devices: none -> 133 us  [across(): return lax.ppermute(x, 'y', [(0, 1), (1, 0)])]
    all_gather x4 -> x3, waiting for transfers between devices: 162 us -> 36 us  [gather(): mine = lax.all_gather(shard, 'pair', axis=0, tiled=False)]
    psum x1 -> x0, blocking collectives: 39.1 us -> none  [local(): totals = lax.psum(packed, ('pair', 'core', 'y'))]
    ppermute x8 -> x9, starting transfers between devices: 5.34 us -> 22.2 us  [partner(): return lax.ppermute(x, 'core', [(0, 1), (1, 0)])]
    ppermute x12, waiting for transfers between devices: 42.4 us -> 59 us  [turned(): return lax.ppermute(x, ('core', 'y'), [(0, 0), (1, 2), (2, 1), (3, 3)])]
    another operation x0 -> x8, other arithmetic: none -> 10.2 us  [gather(): return jnp.stack([low, high], axis=1)]
    convert_element_type x0 -> x4, other arithmetic: none -> 8.63 us  [scatter(): total = (kept.astype(f32) + sent.astype(f32)).astype(bf16)]
  transfers between devices with their start and end apart: 28 -> 36, of which waited for: 17 -> 16; matrix products, arithmetic and copies ran while one was open for 10% -> 14% of each run, Pallas kernels for 3% -> 7%
where the time goes in v2:
time: 668 us; the launch traced here: 664 us
  waiting for transfers between devices  348 us (52%)
  matrix products  94.3 us (14%)
  starting transfers between devices  66.2 us (10%)
  Pallas kernels  48.4 us (7%)
  other arithmetic  37.4 us (6%)
  local copies, waits for them, and re-layouts  29.7 us (4%)
  blocking collectives  24.8 us (4%)
  between operations  15.2 us (2%)
    ppermute x8, waiting for transfers between devices, across(): return lax.ppermute(x, 'y', [(0, 1), (1, 0)])  133 us
    reduce_scatter x4, waiting for transfers between devices, scatter(): part = lax.psum_scatter(total, 'pair', scatter_dimension=0, tiled=True)  116 us
    dot_general x16, matrix products, mm(): return lax.dot_general(left, right, dims, preferred_element_type=f32)  94.3 us
    ppermute x12, waiting for transfers between devices, turned(): return lax.ppermute(x, ('core', 'y'), [(0, 0), (1, 2), (2, 1), (3, 3)])  59 us
    ppermute x12, starting transfers between devices, turned(): return lax.ppermute(x, ('core', 'y'), [(0, 0), (1, 2), (2, 1), (3, 3)])  42.2 us
    all_gather x3, waiting for transfers between devices, gather(): mine = lax.all_gather(shard, 'pair', axis=0, tiled=False)  36 us
    pallas_call x1, Pallas kernels, attn_bwd(): pl.pallas_call(attn_bwd_kernel, grid=(pairs, rows // block), in_specs=[co...  28 us
    all_gather x1, blocking collectives, gather(): mine = lax.all_gather(shard, 'pair', axis=0, tiled=False)  24.8 us
  transfers between devices with their start and end apart: 36, of which 16 were waited for; matrix products, arithmetic and copies ran while one was open for 14% of the time, Pallas kernels for 7%

profile of v2, /device:TPU:1, one launch (start us, length us, event | category | flops | bytes accessed | tf_op | source)
XLA Modules:
  0.0 663.9 jit_solution(5322181508374939557)
XLA Ops:
  7.2 6.1 concatenate.44
  14.2 4.5 collective-permute-start.2
  18.8 3.9 collective-permute-done.2
  23.4 3.6 collective-permute-start.10
  27.1 4.3 collective-permute-done.10
  32.1 3.6 collective-permute-start
  35.8 36.0 %all-gather.8.cloned.1.call-done = bf16[640,1536]{1,0:T(8,128)(2,1)} async-done(((bf16[80,1536]{1,0:T(8,128)(2,1)}), bf16[640,1536]{1,0:T(8,128)(2,1)}) %all-gather.8.cloned.1.call-update) | async-done | bytes 1966096 | tf_op jit(solution)/shard_map/all_gather | solution.py:228
  73.0 3.5 collective-permute-start.8
  76.4 2.1 collective-permute-start.4
  79.2 41.2 %collective-permute-done.4 = bf16[64,512]{1,0:T(8,128)(2,1)S(1)} collective-permute-done((bf16[64,512]{1,0:T(8,128)(2,1)}, bf16[64,512]{1,0:T(8,128)(2,1)S(1)}, u32[]{:S(2)}, u32[]{:S(2)}) %collective-permute-start.4) | collective-permute-done | bytes 65568 | tf_op jit(solution)/shard_map/ppermute | solution.py:184
  120.4 24.8 %all-gather.1 = bf16[512,512]{1,0:T(8,128)(2,1)S(1)} all-gather(bf16[64,512]{1,0:T(8,128)(2,1)S(1)} %collective-permute-done.4), channel_id=3, replica_groups=mesh['pair'=8,'core'=2,'y'=2] {'pair'}, dimensions={0}, use_global_device_ids=true | all-gather | bytes 589824 | tf_op jit(solution)/shard_map/all_gather | solution.py:228
  145.3 8.1 %collective-permute-start.1 = (bf16[512,1024]{1,0:T(8,128)(2,1)S(1)}, bf16[512,1024]{1,0:T(8,128)(2,1)}, u32[]{:S(2)}, u32[]{:S(2)}) collective-permute-start(bf16[512,1024]{1,0:T(8,128)(2,1)S(1)} %collective-permute-done), channel_id=1, source_target_pairs={{0,2},{2,0},{1,3},{3,1},{4,6},{6,4},{5,7},{7,5},{8,10},{10,8},{9,1... | collective-permute-start | bytes 3145736 | tf_op jit(solution)/shard_map/ppermute | solution.py:188
  158.1 2.3 constant_dynamic-update-slice_fusion
  160.4 2.4 select_bitcast_fusion.5
  164.3 3.0 fusion.9
  167.7 7.7 %add_convert_fusion.q_ref.k_ref.v_ref = bf16[1024,1536]{1,0:T(8,128)(2,1)} fusion(bf16[1024,1024]{1,0:T(8,128)(2,1)} %constant_dynamic-update-slice_fusion, bf16[1024,1536]{1,0:T(8,128)(2,1)} %bitcast.120, f32[1536]{0:T(1024)S(1)} %pad_maximum_fusion.13), kind=kOutput, calls=%fused_computation.10 | convolution fusion | flops 3224371200 | bytes 8394752 | tf_op jit(solution)/shard_map/dot_general | solution.py:21
  175.3 20.5 %attn_fwd.1 = (bf16[1024,512]{1,0:T(8,128)(2,1)}, f32[1024,512]{1,0:T(8,128)}) custom-call(s32[1024,1]{1,0:T(8,128)} %copy.45.seg_col, s32[1,1024]{1,0:T(1,128)} %bitcast.139, bf16[1024,1536]{1,0:T(8,128)(2,1)} %add_convert_fusion.q_ref.k_ref.v_ref, bf16[1024,1536]{1,0:T(8,128)(2,1)} %add_convert_fusion.q_ref.k_ref.v_ref, ...), custom_call_target="tpu_custom_call" | custom-call | flops 4294967296 | bytes 6291456 | tf_op jit(solution)/shard_map/attn_fwd/pallas_call | solution.py:110
  195.8 3.0 convolution_convert_fusion.5
  198.8 5.8 collective-permute-start.6
  204.9 2.0 select_bitcast_fusion.1
  207.2 2.2 fusion.65
  210.2 4.1 collective-permute-start.7
  215.3 37.3 %collective-permute-done.9 = bf16[8,64,2048]{2,1,0:T(8,128)(2,1)} collective-permute-done((bf16[8,64,2048]{2,1,0:T(8,128)(2,1)}, bf16[8,64,2048]{2,1,0:T(8,128)(2,1)}, u32[]{:S(2)}, u32[]{:S(2)}) %collective-permute-start.9) | collective-permute-done | bytes 2097184 | tf_op jit(solution)/shard_map/ppermute | solution.py:224
  252.6 1.9 select_bitcast_fusion.3
  254.9 20.6 %multiply_convert_fusion = (bf16[1024,2048]{1,0:T(8,128)(2,1)S(1)}, f32[1024,2048]{1,0:T(8,128)}) fusion(f32[2048]{0:T(1024)S(1)} %dynamic_slice.38, bf16[1024,2048]{1,0:T(8,128)(2,1)S(1)} %bitcast.114, bf16[512,1024]{1,0:T(8,128)(2,1)S(1)} %collective-permute-done.7, bf16[512,1024]{1,0:T(8,128)(2,1)S(1)} %fusion.25), kind=kOutput, calls=%fused_computation.8 | convolution fusion | flops 4311744512 | bytes 18882560 | tf_op jit(solution)/shard_map/dot_general | solution.py:21
  275.6 3.4 fusion.36
  280.0 1.9 collective-permute-start.14
  282.6 5.8 fusion.63
  288.8 7.5 %collective-permute-done.14 = bf16[512,1024]{1,0:T(8,128)(2,1)S(1)} collective-permute-done((bf16[512,1024]{1,0:T(8,128)(2,1)}, bf16[512,1024]{1,0:T(8,128)(2,1)S(1)}, u32[]{:S(2)}, u32[]{:S(2)}) %collective-permute-start.14) | collective-permute-done | bytes 1048608 | tf_op jit(solution)/shard_map/ppermute | solution.py:184
  297.4 1.9 fusion.61
  300.9 2.8 collective-permute-done.15
  303.7 7.1 %convolution_convert_fusion.2 = bf16[1024,2048]{1,0:T(8,128)(2,1)S(1)} fusion(bf16[1024,2048]{1,0:T(8,128)(2,1)} %copy-done.34, bf16[512,1024]{1,0:T(8,128)(2,1)} %collective-permute-done.15, bf16[512,1024]{1,0:T(8,128)(2,1)S(1)} %convert_element_type.258), kind=kOutput, calls=%fused_computation.27 | convolution fusion | flops 4301258752 | bytes 10485760 | tf_op jit(solution)/shard_map/dot_general | solution.py:21
  310.8 9.5 %fusion.5 = bf16[1024,2048]{1,0:T(8,128)(2,1)S(1)} fusion(f32[1024,2048]{1,0:T(8,128)} %get-tuple-element.84, bf16[1024,2048]{1,0:T(8,128)(2,1)S(1)} %bitcast.119, f32[2048]{0:T(1024)S(1)} %dynamic_slice.38, bf16[512,1024]{1,0:T(8,128)(2,1)} %collective-permute-done.15, bf16[512,1024]{1,0:T(8,128)(2,1)S(1)} %convert_element_type.258), kind=kOutput, calls=%fused_computation.6 | convolution fusion | flops 4322230272 | bytes 18882560 | tf_op jit(solution)/shard_map/dot_general | solution.py:21
  320.3 2.4 fusion.33
  324.4 6.7 %convolution_convert_fusion.1 = bf16[1024,2048]{1,0:T(8,128)(2,1)} fusion(bf16[1024,2048]{1,0:T(8,128)(2,1)S(1)} %fusion.5, bf16[512,1024]{1,0:T(8,128)(2,1)S(1)} %copy-done.31, bf16[512,1024]{1,0:T(8,128)(2,1)S(1)} %copy-done.21), kind=kOutput, calls=%fused_computation.26 | convolution fusion | flops 4301258752 | bytes 10485760 | tf_op jit(solution)/shard_map/dot_general | solution.py:21
  331.1 2.4 add_add_fusion
  334.9 35.1 %collective-permute-done.27 = bf16[8,64,2048]{2,1,0:T(8,128)(2,1)S(1)} collective-permute-done((bf16[8,64,2048]{2,1,0:T(8,128)(2,1)S(1)}, bf16[8,64,2048]{2,1,0:T(8,128)(2,1)S(1)}, u32[]{:S(2)}, u32[]{:S(2)}) %collective-permute-start.27) | collective-permute-done | bytes 2097184 | tf_op jit(solution)/shard_map/ppermute | solution.py:224
  370.0 2.2 fusion.6
  372.3 2.2 fusion.62
  377.5 3.3 dynamic-slice_bitcast_fusion.1
  382.2 3.9 convolution_convert_fusion.4.do_ref
  386.1 3.5 convolution_convert_fusion.3
  389.6 28.0 %attn_bwd.1 = (bf16[1024,512]{1,0:T(8,128)(2,1)}, bf16[1024,512]{1,0:T(8,128)(2,1)}, bf16[1024,512]{1,0:T(8,128)(2,1)}) custom-call(s32[1024,1]{1,0:T(8,128)} %copy.45.seg_col, s32[1,1024]{1,0:T(1,128)} %bitcast.140, f32[1024,512]{1,0:T(8,128)} %get-tuple-element.31.lse_ref, bf16[1024,1536]{1,0:T(8,128)(2,1)} %add_convert_fusion.q_ref.k_ref.v_ref, ...), custom_call_target="tpu_custom_call" | custom-call | flops 10737418240 | bytes 9437184 | tf_op jit(solution)/shard_map/attn_bwd/pallas_call | solution.py:137
  417.6 1.4 convert_reduce_fusion.2
  419.3 1.4 convert_reduce_fusion.1
  421.4 7.1 %collective-permute-done.25 = bf16[8,64,2048]{2,1,0:T(8,128)(2,1)S(1)} collective-permute-done((bf16[8,64,2048]{2,1,0:T(8,128)(2,1)}, bf16[8,64,2048]{2,1,0:T(8,128)(2,1)S(1)}, u32[]{:S(2)}, u32[]{:S(2)}) %collective-permute-start.25) | collective-permute-done | bytes 2097184 | tf_op jit(solution)/shard_map/ppermute | solution.py:224
  428.5 3.8 fusion.7
  434.2 6.5 convolution_convert_fusion
  441.2 43.8 %collective-permute-done.21 = bf16[8,80,1536]{2,1,0:T(8,128)(2,1)S(1)} collective-permute-done((bf16[8,80,1536]{2,1,0:T(8,128)(2,1)S(1)}, bf16[8,80,1536]{2,1,0:T(8,128)(2,1)S(1)}, u32[]{:S(2)}, u32[]{:S(2)}) %collective-permute-start.21) | collective-permute-done | bytes 1966112 | tf_op jit(solution)/shard_map/ppermute | solution.py:224
  485.0 1.8 fusion.8
  486.8 4.3 fusion.30
  491.1 1.4 collective-permute-start.18
  492.7 3.5 collective-permute-start.13
  496.2 10.1 %collective-permute-done.23 = bf16[8,64,512]{2,1,0:T(8,128)(2,1)S(1)} collective-permute-done((bf16[8,64,512]{2,1,0:T(8,128)(2,1)S(1)}, bf16[8,64,512]{2,1,0:T(8,128)(2,1)S(1)}, u32[]{:S(2)}, u32[]{:S(2)}) %collective-permute-start.23) | collective-permute-done | bytes 524320 | tf_op jit(solution)/shard_map/ppermute | solution.py:224
  507.3 5.4 add_convert_fusion.1
  512.7 2.9 collective-permute-start.19
  515.7 2.6 collective-permute-start.28
  518.3 2.9 collective-permute-start.26
  521.3 56.0 %reduce-scatter.5.cloned.1.call-done = bf16[80,1536]{1,0:T(8,128)(2,1)} async-done(((bf16[640,1536]{1,0:T(8,128)(2,1)}), bf16[80,1536]{1,0:T(8,128)(2,1)}) %reduce-scatter.5.cloned.1.call-update) | async-done | bytes 245776 | tf_op jit(solution)/shard_map/reduce_scatter | solution.py:240
  577.3 5.4 collective-permute-start.22
  582.7 59.6 %reduce-scatter.7.cloned.1.call-done = bf16[64,512]{1,0:T(8,128)(2,1)} async-done(((bf16[512,512]{1,0:T(8,128)(2,1)}), bf16[64,512]{1,0:T(8,128)(2,1)}) %reduce-scatter.7.cloned.1.call-update) | async-done | bytes 65552 | tf_op jit(solution)/shard_map/reduce_scatter | solution.py:240
  642.4 5.5 collective-permute-start.24
  647.9 2.1 collective-permute-done.24
  650.7 1.6 convert_element_type.270
  (204 shorter events, 35.5 us)
Async XLA Ops:
  7.2 64.6 %all-gather.8.cloned.1.call-start = ((), (), s32[]{:S(2)}) async-start(), calls=%async_computation.8 | async-start | bytes 2211840 | tf_op jit(solution)/shard_map/all_gather | solution.py:228
  14.2 8.4 %collective-permute-start.2 = (bf16[80,1536]{1,0:T(8,128)(2,1)S(1)}, bf16[80,1536]{1,0:T(8,128)(2,1)S(1)}, u32[]{:S(2)}, u32[]{:S(2)}) collective-permute-start(bf16[80,1536]{1,0:T(8,128)(2,1)S(1)} %fusion.51), channel_id=1, source_target_pairs={{0,0},{1,2},{2,1},{3,3},{4,4},{5,6},{6,5},{7,7},{8,8},{9,10},{10,9... | collective-permute-start | bytes 737288 | tf_op jit(solution)/shard_map/ppermute | solution.py:184
  23.4 137.0 %all-gather.12.cloned.1.call-start = ((), (), s32[]{:S(2)}) async-start(), calls=%async_computation.10 | async-start | bytes 2359296 | tf_op jit(solution)/shard_map/all_gather | solution.py:228
  23.4 7.9 %collective-permute-start.10 = (bf16[64,2048]{1,0:T(8,128)(2,1)}, bf16[64,2048]{1,0:T(8,128)(2,1)S(1)}, u32[]{:S(2)}, u32[]{:S(2)}) collective-permute-start(bf16[64,2048]{1,0:T(8,128)(2,1)} %param.26), channel_id=1, source_target_pairs={{0,0},{1,2},{2,1},{3,3},{4,4},{5,6},{6,5},{7,7},{8,8},{9,10},{10,9... | collective-permute-start | bytes 786440 | tf_op jit(solution)/shard_map/ppermute | solution.py:184
  32.1 172.5 %all-gather.10.cloned.1.call-start = ((), (), s32[]{:S(2)}) async-start(), calls=%async_computation.9 | async-start | bytes 2359296 | tf_op jit(solution)/shard_map/all_gather | solution.py:228
  32.1 113.1 %collective-permute-start = (bf16[512,1024]{1,0:T(8,128)(2,1)}, bf16[512,1024]{1,0:T(8,128)(2,1)S(1)}, u32[]{:S(2)}, u32[]{:S(2)}) collective-permute-start(bf16[512,1024]{1,0:T(8,128)(2,1)} %param.20), channel_id=1, source_target_pairs={{0,0},{1,2},{2,1},{3,3},{4,4},{5,6},{6,5},{7,7},{8,8},{9,10},{10,9... | collective-permute-start | bytes 3145736 | tf_op jit(solution)/shard_map/ppermute | solution.py:184
  71.8 88.6 %collective-permute-start.3 = (bf16[8,80,1536]{2,1,0:T(8,128)(2,1)}, bf16[8,80,1536]{2,1,0:T(8,128)(2,1)}, u32[]{:S(2)}, u32[]{:S(2)}) collective-permute-start(bf16[8,80,1536]{2,1,0:T(8,128)(2,1)} %bitcast.130), channel_id=1, source_target_pairs={{0,1},{1,0},{2,3},{3,2},{4,5},{5,4},{6,7},{7,6},{8,9},{9,8},{10,11... | collective-permute-start | bytes 5898248 | tf_op jit(solution)/shard_map/ppermute | solution.py:224
  73.0 83.0 %collective-permute-start.8 = (bf16[64,2048]{1,0:T(8,128)(2,1)}, bf16[64,2048]{1,0:T(8,128)(2,1)S(1)}, u32[]{:S(2)}, u32[]{:S(2)}) collective-permute-start(bf16[64,2048]{1,0:T(8,128)(2,1)} %param.25), channel_id=1, source_target_pairs={{0,0},{1,2},{2,1},{3,3},{4,4},{5,6},{6,5},{7,7},{8,8},{9,10},{10,9... | collective-permute-start | bytes 786440 | tf_op jit(solution)/shard_map/ppermute | solution.py:184
  76.4 44.0 %collective-permute-start.4 = (bf16[64,512]{1,0:T(8,128)(2,1)}, bf16[64,512]{1,0:T(8,128)(2,1)S(1)}, u32[]{:S(2)}, u32[]{:S(2)}) collective-permute-start(bf16[64,512]{1,0:T(8,128)(2,1)} %param.24), channel_id=1, source_target_pairs={{0,0},{1,2},{2,1},{3,3},{4,4},{5,6},{6,5},{7,7},{8,8},{9,10},{10,9... | collective-permute-start | bytes 196616 | tf_op jit(solution)/shard_map/ppermute | solution.py:184
  145.2 11.5 %collective-permute-start.5 = (bf16[8,64,512]{2,1,0:T(8,128)(2,1)S(1)}, bf16[8,64,512]{2,1,0:T(8,128)(2,1)S(1)}, u32[]{:S(2)}, u32[]{:S(2)}) collective-permute-start(bf16[8,64,512]{2,1,0:T(8,128)(2,1)S(1)} %bitcast.123), channel_id=1, source_target_pairs={{0,1},{1,0},{2,3},{3,2},{4,5},{5,4},{6,7},{7,6},{8,9},{9,8},{10,11... | collective-permute-start | bytes 1572872 | tf_op jit(solution)/shard_map/ppermute | solution.py:224
  145.3 11.7 %copy-start.18 = (bf16[512,1024]{1,0:T(8,128)(2,1)}, bf16[512,1024]{1,0:T(8,128)(2,1)S(1)}, u32[]{:S(2)}) copy-start(bf16[512,1024]{1,0:T(8,128)(2,1)S(1)} %collective-permute-done) | copy-start | bytes 3145732
  145.3 12.8 %collective-permute-start.1 = (bf16[512,1024]{1,0:T(8,128)(2,1)S(1)}, bf16[512,1024]{1,0:T(8,128)(2,1)}, u32[]{:S(2)}, u32[]{:S(2)}) collective-permute-start(bf16[512,1024]{1,0:T(8,128)(2,1)S(1)} %collective-permute-done), channel_id=1, source_target_pairs={{0,2},{2,0},{1,3},{3,1},{4,6},{6,4},{5,7},{7,5},{8,10},{10,8},{9,1... | collective-permute-start | bytes 3145736 | tf_op jit(solution)/shard_map/ppermute | solution.py:188
  154.9 7.9 %copy-start.28 = (s32[1024]{0:T(1024)}, s32[1024]{0:T(1024)S(1)}, u32[]{:S(2)}) copy-start(s32[1024]{0:T(1024)S(1)} %broadcast_add_fusion) | copy-start | bytes 12292
  156.7 359.0 %reduce-scatter.11.cloned.1.call-start = ((), (), s32[]{:S(2)}) async-start(), calls=%async_computation.7 | async-start | bytes 2359296 | tf_op jit(solution)/shard_map/reduce_scatter | solution.py:240
  156.9 50.3 %copy-start.17 = (bf16[8,2,64,512]{3,2,1,0:T(8,128)(2,1)}, bf16[8,2,64,512]{3,2,1,0:T(8,128)(2,1)S(1)}, u32[]{:S(2)}) copy-start(bf16[8,2,64,512]{3,2,1,0:T(8,128)(2,1)S(1)} %pad_maximum_fusion.11) | copy-start | bytes 3145732
  160.4 44.5 %collective-permute-start.11 = (bf16[8,64,2048]{2,1,0:T(8,128)(2,1)}, bf16[8,64,2048]{2,1,0:T(8,128)(2,1)}, u32[]{:S(2)}, u32[]{:S(2)}) collective-permute-start(bf16[8,64,2048]{2,1,0:T(8,128)(2,1)} %bitcast.126), channel_id=1, source_target_pairs={{0,1},{1,0},{2,3},{3,2},{4,5},{5,4},{6,7},{7,6},{8,9},{9,8},{10,11... | collective-permute-start | bytes 6291464 | tf_op jit(solution)/shard_map/ppermute | solution.py:224
  195.8 9.0 %copy-start.15 = (bf16[512,2048]{1,0:T(8,128)(2,1)S(1)}, bf16[512,2048]{1,0:T(8,128)(2,1)}, u32[]{:S(2)}) copy-start(bf16[512,2048]{1,0:T(8,128)(2,1)} %all-gather.12.cloned.1.call-done) | copy-start | bytes 6291460
  198.8 8.4 %collective-permute-start.6 = (bf16[512,1024]{1,0:T(8,128)(2,1)}, bf16[512,1024]{1,0:T(8,128)(2,1)}, u32[]{:S(2)}, u32[]{:S(2)}) collective-permute-start(bf16[512,1024]{1,0:T(8,128)(2,1)} %convolution_convert_fusion.5), channel_id=1, source_target_pairs={{0,2},{2,0},{1,3},{3,1},{4,6},{6,4},{5,7},{7,5},{8,10},{10,8},{9,1... | collective-permute-start | bytes 3145736 | tf_op jit(solution)/shard_map/ppermute | solution.py:188
  204.6 48.0 %collective-permute-start.9 = (bf16[8,64,2048]{2,1,0:T(8,128)(2,1)}, bf16[8,64,2048]{2,1,0:T(8,128)(2,1)}, u32[]{:S(2)}, u32[]{:S(2)}) collective-permute-start(bf16[8,64,2048]{2,1,0:T(8,128)(2,1)} %bitcast.128), channel_id=1, source_target_pairs={{0,1},{1,0},{2,3},{3,2},{4,5},{5,4},{6,7},{7,6},{8,9},{9,8},{10,11... | collective-permute-start | bytes 6291464 | tf_op jit(solution)/shard_map/ppermute | solution.py:224
  204.8 2.4 copy-start.19
  204.8 2.4 copy-start.32
  210.2 44.7 %copy-start.20 = (bf16[512,1024]{1,0:T(8,128)(2,1)}, bf16[512,1024]{1,0:T(8,128)(2,1)S(1)}, u32[]{:S(2)}) copy-start(bf16[512,1024]{1,0:T(8,128)(2,1)S(1)} %fusion.25) | copy-start | bytes 3145732
  210.2 44.7 %collective-permute-start.7 = (bf16[512,1024]{1,0:T(8,128)(2,1)S(1)}, bf16[512,1024]{1,0:T(8,128)(2,1)S(1)}, u32[]{:S(2)}, u32[]{:S(2)}) collective-permute-start(bf16[512,1024]{1,0:T(8,128)(2,1)S(1)} %fusion.25), channel_id=1, source_target_pairs={{0,2},{2,0},{1,3},{3,1},{4,6},{6,4},{5,7},{7,5},{8,10},{10,8},{9,1... | collective-permute-start | bytes 3145736 | tf_op jit(solution)/shard_map/ppermute | solution.py:188
  214.7 38.0 %copy-start.16 = (bf16[512,2048]{1,0:T(8,128)(2,1)S(1)}, bf16[512,2048]{1,0:T(8,128)(2,1)}, u32[]{:S(2)}) copy-start(bf16[512,2048]{1,0:T(8,128)(2,1)} %all-gather.10.cloned.1.call-done) | copy-start | bytes 6291460
  215.3 60.3 %copy-start.8 = (bf16[8,2,64,2048]{3,2,1,0:T(8,128)(2,1)}, bf16[8,2,64,2048]{3,2,1,0:T(8,128)(2,1)S(1)}, u32[]{:S(2)}) copy-start(bf16[8,2,64,2048]{3,2,1,0:T(8,128)(2,1)S(1)} %copy.48) | copy-start | bytes 12582916
  254.9 20.6 %copy-start.6 = (bf16[8,2,64,2048]{3,2,1,0:T(8,128)(2,1)}, bf16[8,2,64,2048]{3,2,1,0:T(8,128)(2,1)S(1)}, u32[]{:S(2)}) copy-start(bf16[8,2,64,2048]{3,2,1,0:T(8,128)(2,1)S(1)} %pad_maximum_fusion) | copy-start | bytes 12582916
  254.9 20.6 %copy-start.30 = (bf16[512,1024]{1,0:T(8,128)(2,1)}, bf16[512,1024]{1,0:T(8,128)(2,1)S(1)}, u32[]{:S(2)}) copy-start(bf16[512,1024]{1,0:T(8,128)(2,1)S(1)} %collective-permute-done.7) | copy-start | bytes 3145732
  275.6 3.4 copy-start.34
  275.6 6.3 copy-start.29
  279.0 3.6 collective-permute-start.12
  280.0 16.3 %collective-permute-start.14 = (bf16[512,1024]{1,0:T(8,128)(2,1)}, bf16[512,1024]{1,0:T(8,128)(2,1)S(1)}, u32[]{:S(2)}, u32[]{:S(2)}) collective-permute-start(bf16[512,1024]{1,0:T(8,128)(2,1)} %param.36), channel_id=1, source_target_pairs={{0,0},{1,2},{2,1},{3,3},{4,4},{5,6},{6,5},{7,7},{8,8},{9,10},{10,9... | collective-permute-start | bytes 3145736 | tf_op jit(solution)/shard_map/ppermute | solution.py:184
  300.8 2.9 collective-permute-start.15
  300.9 9.9 %copy-start.9 = (bf16[8,2,64,2048]{3,2,1,0:T(8,128)(2,1)S(1)}, bf16[8,2,64,2048]{3,2,1,0:T(8,128)(2,1)}, u32[]{:S(2)}) copy-start(bf16[8,2,64,2048]{3,2,1,0:T(8,128)(2,1)} %copy-done.8) | copy-start | bytes 12582916
  310.8 9.5 %copy-start.7 = (bf16[8,2,64,2048]{3,2,1,0:T(8,128)(2,1)S(1)}, bf16[8,2,64,2048]{3,2,1,0:T(8,128)(2,1)}, u32[]{:S(2)}) copy-start(bf16[8,2,64,2048]{3,2,1,0:T(8,128)(2,1)} %copy-done.6) | copy-start | bytes 12582916
  320.3 10.8 %copy-start.10 = (bf16[1024,2048]{1,0:T(8,128)(2,1)}, bf16[1024,2048]{1,0:T(8,128)(2,1)S(1)}, u32[]{:S(2)}) copy-start(bf16[1024,2048]{1,0:T(8,128)(2,1)S(1)} %fusion.5) | copy-start | bytes 12582916
  322.7 8.4 %collective-permute-start.16 = (bf16[512,1024]{1,0:T(8,128)(2,1)S(1)}, bf16[512,1024]{1,0:T(8,128)(2,1)S(1)}, u32[]{:S(2)}, u32[]{:S(2)}) collective-permute-start(bf16[512,1024]{1,0:T(8,128)(2,1)S(1)} %fusion.33), channel_id=1, source_target_pairs={{0,2},{2,0},{1,3},{3,1},{4,6},{6,4},{5,7},{7,5},{8,10},{10,8},{9,1... | collective-permute-start | bytes 3145736 | tf_op jit(solution)/shard_map/ppermute | solution.py:188
  322.9 1.5 copy-start.31
  323.1 8.0 %copy-start.5 = (f32[512,1024]{1,0:T(8,128)S(1)}, f32[512,1024]{1,0:T(8,128)}, u32[]{:S(2)}) copy-start(f32[512,1024]{1,0:T(8,128)} %copy-done.4) | copy-start | bytes 6291460
  323.1 46.9 %collective-permute-start.27 = (bf16[8,64,2048]{2,1,0:T(8,128)(2,1)S(1)}, bf16[8,64,2048]{2,1,0:T(8,128)(2,1)S(1)}, u32[]{:S(2)}, u32[]{:S(2)}) collective-permute-start(bf16[8,64,2048]{2,1,0:T(8,128)(2,1)S(1)} %dynamic-slice_bitcast_fusion), channel_id=1, source_target_pairs={{0,1},{1,0},{2,3},{3,2},{4,5},{5,4},{6,7},{7,6},{8,9},{9,8},{10,11... | collective-permute-start | bytes 6291464 | tf_op jit(solution)/shard_map/ppermute | solution.py:224
  333.6 1.4 copy-start.1
  372.2 146.1 %reduce-scatter.9.cloned.1.call-start = ((), (), s32[]{:S(2)}) async-start(), calls=%async_computation.6 | async-start | bytes 2359296 | tf_op jit(solution)/shard_map/reduce_scatter | solution.py:240
  374.5 1.4 copy-start.2
  376.0 6.2 collective-permute-start.17
  377.5 3.4 copy-start.11
  380.9 47.6 %collective-permute-start.25 = (bf16[8,64,2048]{2,1,0:T(8,128)(2,1)}, bf16[8,64,2048]{2,1,0:T(8,128)(2,1)S(1)}, u32[]{:S(2)}, u32[]{:S(2)}) collective-permute-start(bf16[8,64,2048]{2,1,0:T(8,128)(2,1)} %dynamic-slice_bitcast_fusion.1), channel_id=1, source_target_pairs={{0,1},{1,0},{2,3},{3,2},{4,5},{5,4},{6,7},{7,6},{8,9},{9,8},{10,11... | collective-permute-start | bytes 6291464 | tf_op jit(solution)/shard_map/ppermute | solution.py:224
  382.2 3.9 copy-start.33
  421.1 19.6 %collective-permute-start.20 = (f32[16,768]{1,0:T(8,128)S(1)}, f32[16,768]{1,0:T(8,128)S(1)}, u32[]{:S(2)}, u32[]{:S(2)}) collective-permute-start(f32[16,768]{1,0:T(8,128)S(1)} %concatenate.52), channel_id=1, source_target_pairs={{0,2},{2,0},{1,3},{3,1},{4,6},{6,4},{5,7},{7,5},{8,10},{10,8},{9,1... | collective-permute-start | bytes 147464 | tf_op jit(solution)/shard_map/ppermute | solution.py:188
  432.2 1.6 copy-start.22
  432.3 1.9 copy-start.12
  432.3 145.0 %reduce-scatter.5.cloned.1.call-start = ((), (), s32[]{:S(2)}) async-start(), calls=%async_computation.4 | async-start | bytes 2211840 | tf_op jit(solution)/shard_map/reduce_scatter | solution.py:240
  434.2 6.5 copy-start.24
  441.1 45.8 %copy-start.14 = (bf16[8,2,64,1536]{3,2,1,0:T(8,128)(2,1)S(1)}, bf16[8,2,64,1536]{3,2,1,0:T(8,128)(2,1)}, u32[]{:S(2)}) copy-start(bf16[8,2,64,1536]{3,2,1,0:T(8,128)(2,1)} %fusion.9) | copy-start | bytes 9437188
  441.1 43.9 %collective-permute-start.21 = (bf16[8,80,1536]{2,1,0:T(8,128)(2,1)S(1)}, bf16[8,80,1536]{2,1,0:T(8,128)(2,1)S(1)}, u32[]{:S(2)}, u32[]{:S(2)}) collective-permute-start(bf16[8,80,1536]{2,1,0:T(8,128)(2,1)S(1)} %fusion.22), channel_id=1, source_target_pairs={{0,1},{1,0},{2,3},{3,2},{4,5},{5,4},{6,7},{7,6},{8,9},{9,8},{10,11... | collective-permute-start | bytes 5898248 | tf_op jit(solution)/shard_map/ppermute | solution.py:224
  486.8 155.6 %reduce-scatter.7.cloned.1.call-start = ((), (), s32[]{:S(2)}) async-start(), calls=%async_computation.5 | async-start | bytes 589824 | tf_op jit(solution)/shard_map/reduce_scatter | solution.py:240
  486.8 5.7 copy-start.23
  491.1 16.2 %copy-start.3 = (f32[512,1024]{1,0:T(8,128)S(1)}, f32[512,1024]{1,0:T(8,128)}, u32[]{:S(2)}) copy-start(f32[512,1024]{1,0:T(8,128)} %copy-done.2) | copy-start | bytes 6291460
  491.1 16.1 %collective-permute-start.18 = (bf16[512,1024]{1,0:T(8,128)(2,1)}, bf16[512,1024]{1,0:T(8,128)(2,1)}, u32[]{:S(2)}, u32[]{:S(2)}) collective-permute-start(bf16[512,1024]{1,0:T(8,128)(2,1)} %fusion.30), channel_id=1, source_target_pairs={{0,2},{2,0},{1,3},{3,1},{4,6},{6,4},{5,7},{7,5},{8,10},{10,8},{9,1... | collective-permute-start | bytes 3145736 | tf_op jit(solution)/shard_map/ppermute | solution.py:188
  492.6 13.7 %collective-permute-start.23 = (bf16[8,64,512]{2,1,0:T(8,128)(2,1)S(1)}, bf16[8,64,512]{2,1,0:T(8,128)(2,1)S(1)}, u32[]{:S(2)}, u32[]{:S(2)}) collective-permute-start(bf16[8,64,512]{2,1,0:T(8,128)(2,1)S(1)} %dynamic-slice_bitcast_fusion.2), channel_id=1, source_target_pairs={{0,1},{1,0},{2,3},{3,2},{4,5},{5,4},{6,7},{7,6},{8,9},{9,8},{10,11... | collective-permute-start | bytes 1572872 | tf_op jit(solution)/shard_map/ppermute | solution.py:224
  492.7 90.0 %collective-permute-start.13 = (bf16[512,1024]{1,0:T(8,128)(2,1)}, bf16[512,1024]{1,0:T(8,128)(2,1)S(1)}, u32[]{:S(2)}, u32[]{:S(2)}) collective-permute-start(bf16[512,1024]{1,0:T(8,128)(2,1)} %get-tuple-element.59), channel_id=1, source_target_pairs={{0,0},{1,2},{2,1},{3,3},{4,4},{5,6},{6,5},{7,7},{8,8},{9,10},{10,9... | collective-permute-start | bytes 3145736 | tf_op jit(solution)/shard_map/ppermute | solution.py:184
  512.7 138.0 %collective-permute-start.19 = (bf16[512,1024]{1,0:T(8,128)(2,1)}, bf16[512,1024]{1,0:T(8,128)(2,1)S(1)}, u32[]{:S(2)}, u32[]{:S(2)}) collective-permute-start(bf16[512,1024]{1,0:T(8,128)(2,1)} %add_convert_fusion.1), channel_id=1, source_target_pairs={{0,0},{1,2},{2,1},{3,3},{4,4},{5,6},{6,5},{7,7},{8,8},{9,10},{10,9... | collective-permute-start | bytes 3145736 | tf_op jit(solution)/shard_map/ppermute | solution.py:184
  515.7 136.6 %collective-permute-start.28 = (bf16[64,2048]{1,0:T(8,128)(2,1)}, bf16[64,2048]{1,0:T(8,128)(2,1)S(1)}, u32[]{:S(2)}, u32[]{:S(2)}) collective-permute-start(bf16[64,2048]{1,0:T(8,128)(2,1)} %reduce-scatter.11.cloned.1.call-done), channel_id=1, source_target_pairs={{0,0},{1,2},{2,1},{3,3},{4,4},{5,6},{6,5},{7,7},{8,8},{9,10},{10,9... | collective-permute-start | bytes 786440 | tf_op jit(solution)/shard_map/ppermute | solution.py:184
  518.3 134.8 %collective-permute-start.26 = (bf16[64,2048]{1,0:T(8,128)(2,1)}, bf16[64,2048]{1,0:T(8,128)(2,1)S(1)}, u32[]{:S(2)}, u32[]{:S(2)}) collective-permute-start(bf16[64,2048]{1,0:T(8,128)(2,1)} %reduce-scatter.9.cloned.1.call-done), channel_id=1, source_target_pairs={{0,0},{1,2},{2,1},{3,3},{4,4},{5,6},{6,5},{7,7},{8,8},{9,10},{10,9... | collective-permute-start | bytes 786440 | tf_op jit(solution)/shard_map/ppermute | solution.py:184
  577.3 76.6 %collective-permute-start.22 = (bf16[80,1536]{1,0:T(8,128)(2,1)}, bf16[80,1536]{1,0:T(8,128)(2,1)S(1)}, u32[]{:S(2)}, u32[]{:S(2)}) collective-permute-start(bf16[80,1536]{1,0:T(8,128)(2,1)} %reduce-scatter.5.cloned.1.call-done), channel_id=1, source_target_pairs={{0,0},{1,2},{2,1},{3,3},{4,4},{5,6},{6,5},{7,7},{8,8},{9,10},{10,9... | collective-permute-start | bytes 737288 | tf_op jit(solution)/shard_map/ppermute | solution.py:184
  642.4 7.7 %collective-permute-start.24 = (bf16[64,512]{1,0:T(8,128)(2,1)}, bf16[64,512]{1,0:T(8,128)(2,1)S(1)}, u32[]{:S(2)}, u32[]{:S(2)}) collective-permute-start(bf16[64,512]{1,0:T(8,128)(2,1)} %reduce-scatter.7.cloned.1.call-done), channel_id=1, source_target_pairs={{0,0},{1,2},{2,1},{3,3},{4,4},{5,6},{6,5},{7,7},{8,8},{9,10},{10,9... | collective-permute-start | bytes 196616 | tf_op jit(solution)/shard_map/ppermute | solution.py:184
  (7 other events, 7.2 us)
Sparse Core Ops, SparseCore 0:
  23.5 48.2 all-gather.7
  74.5 49.0 all-gather.11
  156.8 46.3 all-gather.9
  372.4 64.9 reduce-scatter.10
  440.7 66.7 reduce-scatter.8
  511.4 65.8 reduce-scatter.4
  581.6 60.7 reduce-scatter.6

commit v3 on v2

--- a/solution.py
+++ b/solution.py
@@ -247,14 +247,14 @@
     small = (b_query, b_value, b_out, b_down, gain_attn, shift_attn, gain_ffn, shift_ffn, b_up)
     small = jnp.concatenate(small)
     small_size = small.shape[0]
-    extra = jnp.pad(small[None, :], ((0, sheet - 1), (0, 3 * width - small_size)))
-    qkv_shard = jnp.concatenate([w_query, w_key, w_value], axis=1)
+    extra = jnp.pad(small[None, :], ((0, sheet - 1), (0, 4 * width - small_size)))
+    qkv_shard = jnp.concatenate([w_query, w_key, w_value, w_out], axis=1)
     qkv_full = gather(jnp.concatenate([qkv_shard, extra], axis=0))
-    qkv_mat = whole_matrix(qkv_full[:, :, :shard_rows])
+    qkv_mat = whole_matrix(qkv_full[:, :, :shard_rows, : 3 * width])
+    out_mat = whole_matrix(qkv_full[:, :, :shard_rows, 3 * width :])
     vectors = qkv_full[:, :, shard_rows, :small_size].reshape(-1, small_size)
     own = turned(tokens)
     rows_all = jnp.concatenate([own, partner(own)], axis=0)
-    out_mat = whole_matrix(gather(w_out))
     up_mat = whole_matrix(gather(w_up))
     down_mat = whole_matrix(gather(w_down))
     cot_rows = turned(out_grad)
@@ -311,10 +311,10 @@
     d_context = mm(d_attn, out_mat).astype(bf16)
     part_out = mm(d_attn, context, TN).astype(bf16)
     d_context, part_out = lax.optimization_barrier((d_context, part_out))
-    grad_out = scatter(part_out)
     d_query, d_keys, d_values = attn_bwd(qkv, seg, lse, d_context)
     d_qkv = jnp.concatenate([d_query, d_keys, d_values], axis=1)
     part_qkv = mm(rows_all, d_qkv, TN).astype(bf16)
+    part_qkv = jnp.concatenate([part_qkv, part_out], axis=1)
     d_rows = d_first_in + summed_rows(d_qkv, qkv_mat, NT)
     grad_tokens = turned(d_rows.astype(bf16)).astype(f32)
 
@@ -335,8 +335,8 @@
     )
     packed = jnp.concatenate([item.reshape(vectors.shape[0], -1) for item in sums], axis=1)
     packed = (packed + partner(packed)).astype(bf16)
-    packed = jnp.pad(packed[:, None, :], ((0, 0), (0, sheet - 1), (0, 3 * width - small_size)))
-    part_qkv = part_qkv.reshape(packed.shape[0], shard_rows, 3 * width)
+    packed = jnp.pad(packed[:, None, :], ((0, 0), (0, sheet - 1), (0, 4 * width - small_size)))
+    part_qkv = part_qkv.reshape(packed.shape[0], shard_rows, 4 * width)
     part_qkv = jnp.concatenate([part_qkv, packed], axis=1)
     grad_qkv = scatter(whole_matrix(part_qkv))
     mine = grad_qkv[shard_rows, :small_size]
@@ -348,8 +348,8 @@
         grad_tokens,
         grad_qkv[:, :width],
         grad_qkv[:, width : 2 * width],
-        grad_qkv[:, 2 * width :],
-        grad_out,
+        grad_qkv[:, 2 * width : 3 * width],
+        grad_qkv[:, 3 * width :],
         grad_up,
         grad_down,
         grad_b_query,

time: 668 us -> 668 us (level)
  waiting for transfers between devices: 348 us -> 408 us
  blocking collectives: 24.8 us -> 0 us
  starting transfers between devices: 66.2 us -> 47.3 us
  matrix products: 94.3 us -> 76.7 us
    ppermute x8 -> x6, waiting for transfers between devices: 133 us -> 186 us  [across(): return lax.ppermute(x, 'y', [(0, 1), (1, 0)])]
    reduce_scatter x4 -> x3, waiting for transfers between devices: 116 us -> 86.4 us  [scatter(): part = lax.psum_scatter(total, 'pair', scatter_dimension=0, tiled=True)]
    all_gather x1 -> x0, blocking collectives: 24.8 us -> none  [gather(): mine = lax.all_gather(shard, 'pair', axis=0, tiled=False)]
    ppermute x12 -> x10, waiting for transfers between devices: 59 us -> 82.2 us  [turned(): return lax.ppermute(x, ('core', 'y'), [(0, 0), (1, 2), (2, 1), (3, 3)])]
    dot_general x16, matrix products: 94.3 us -> 76.7 us  [mm(): return lax.dot_general(left, right, dims, preferred_element_type=f32)]
    all_gather x3, waiting for transfers between devices: 36 us -> 49.4 us  [gather(): mine = lax.all_gather(shard, 'pair', axis=0, tiled=False)]
    ppermute x9, starting transfers between devices: 22.2 us -> 9.07 us  [partner(): return lax.ppermute(x, 'core', [(0, 1), (1, 0)])]
    ppermute x12 -> x10, starting transfers between devices: 42.2 us -> 34.9 us  [turned(): return lax.ppermute(x, ('core', 'y'), [(0, 0), (1, 2), (2, 1), (3, 3)])]
  transfers between devices with their start and end apart: 36 -> 31, of which waited for: 16 -> 17; matrix products, arithmetic and copies ran while one was open for 14% -> 10% of each run, Pallas kernels for 7% -> 3%
where the time goes in v3:
time: 668 us; the launch traced here: 664 us
  waiting for transfers between devices  408 us (61%)
  matrix products  76.7 us (11%)
  Pallas kernels  48.4 us (7%)
  starting transfers between devices  47.3 us (7%)
  other arithmetic  38.6 us (6%)
  local copies, waits for them, and re-layouts  30.5 us (5%)
  between operations  15.1 us (2%)
    ppermute x6, waiting for transfers between devices, across(): return lax.ppermute(x, 'y', [(0, 1), (1, 0)])  186 us
    reduce_scatter x3, waiting for transfers between devices, scatter(): part = lax.psum_scatter(total, 'pair', scatter_dimension=0, tiled=True)  86.4 us
    ppermute x10, waiting for transfers between devices, turned(): return lax.ppermute(x, ('core', 'y'), [(0, 0), (1, 2), (2, 1), (3, 3)])  82.2 us
    dot_general x16, matrix products, mm(): return lax.dot_general(left, right, dims, preferred_element_type=f32)  76.7 us
    all_gather x3, waiting for transfers between devices, gather(): mine = lax.all_gather(shard, 'pair', axis=0, tiled=False)  49.4 us
    ppermute x10, starting transfers between devices, turned(): return lax.ppermute(x, ('core', 'y'), [(0, 0), (1, 2), (2, 1), (3, 3)])  34.9 us
    pallas_call x1, Pallas kernels, attn_bwd(): pl.pallas_call(attn_bwd_kernel, grid=(pairs, rows // block), in_specs=[co...  27.9 us
    pallas_call x1, Pallas kernels, attn_fwd(): pl.pallas_call(attn_fwd_kernel, grid=(pairs, rows // block), in_specs=[co...  20.5 us
  transfers between devices with their start and end apart: 31, of which 17 were waited for; matrix products, arithmetic and copies ran while one was open for 10% of the time, Pallas kernels for 3%

profile of v3, /device:TPU:1, one launch (start us, length us, event | category | flops | bytes accessed | tf_op | source)
XLA Modules:
  0.0 664.2 jit_solution(10055901698274001250)
XLA Ops:
  7.2 6.1 concatenate.47
  14.3 4.5 collective-permute-start.2
  18.8 4.7 collective-permute-done.2
  24.4 3.6 collective-permute-start.8
  28.0 4.3 collective-permute-done.8
  33.1 46.0 %all-gather.7.cloned.1.call-done = bf16[640,2048]{1,0:T(8,128)(2,1)} async-done(((bf16[80,2048]{1,0:T(8,128)(2,1)}), bf16[640,2048]{1,0:T(8,128)(2,1)}) %all-gather.7.cloned.1.call-update) | async-done | bytes 2621456 | tf_op jit(solution)/shard_map/all_gather | solution.py:228
  80.3 4.3 collective-permute-start
  84.5 1.9 collective-permute-start.6
  86.5 62.6 %collective-permute-done = bf16[512,1024]{1,0:T(8,128)(2,1)S(1)} collective-permute-done((bf16[512,1024]{1,0:T(8,128)(2,1)}, bf16[512,1024]{1,0:T(8,128)(2,1)S(1)}, u32[]{:S(2)}, u32[]{:S(2)}) %collective-permute-start) | collective-permute-done | bytes 1048608 | tf_op jit(solution)/shard_map/ppermute | solution.py:184
  157.1 2.9 select_bitcast_fusion.1
  160.0 1.5 copy-done
  164.4 7.7 %add_convert_fusion.q_ref.k_ref.v_ref = bf16[1024,1536]{1,0:T(8,128)(2,1)} fusion(bf16[1024,1024]{1,0:T(8,128)(2,1)} %constant_dynamic-update-slice_fusion, bf16[1024,1536]{1,0:T(8,128)(2,1)S(1)} %bitcast.106, f32[1536]{0:T(1024)S(1)} %pad_maximum_fusion.13), kind=kOutput, calls=%fused_computation.12 | convolution fusion | flops 3224371200 | bytes 8394752 | tf_op jit(solution)/shard_map/dot_general | solution.py:21
  172.1 20.5 %attn_fwd.1 = (bf16[1024,512]{1,0:T(8,128)(2,1)}, f32[1024,512]{1,0:T(8,128)}) custom-call(s32[1024,1]{1,0:T(8,128)} %copy.44.seg_col, s32[1,1024]{1,0:T(1,128)} %bitcast.120, bf16[1024,1536]{1,0:T(8,128)(2,1)} %add_convert_fusion.q_ref.k_ref.v_ref, bf16[1024,1536]{1,0:T(8,128)(2,1)} %add_convert_fusion.q_ref.k_ref.v_ref, ...), custom_call_target="tpu_custom_call" | custom-call | flops 4294967296 | bytes 6291456 | tf_op jit(solution)/shard_map/attn_fwd/pallas_call | solution.py:110
  192.6 2.9 convolution_convert_fusion.5
  195.5 1.9 collective-permute-start.4
  197.4 3.4 all-gather.9.cloned.1.call-done
  202.0 2.1 collective-permute-done.9
  204.1 1.9 select_bitcast_fusion.3
  206.3 2.2 copy.46
  208.8 2.6 fusion.65
  212.2 1.5 collective-permute-start.5
  213.8 34.3 %collective-permute-done.7 = bf16[8,64,2048]{2,1,0:T(8,128)(2,1)} collective-permute-done((bf16[8,64,2048]{2,1,0:T(8,128)(2,1)}, bf16[8,64,2048]{2,1,0:T(8,128)(2,1)}, u32[]{:S(2)}, u32[]{:S(2)}) %collective-permute-start.7) | collective-permute-done | bytes 2097184 | tf_op jit(solution)/shard_map/ppermute | solution.py:224
  248.1 2.1 select_bitcast_fusion.5
  250.7 8.4 %multiply_convert_fusion = (bf16[1024,2048]{1,0:T(8,128)(2,1)S(1)}, f32[1024,2048]{1,0:T(8,128)}) fusion(f32[2048]{0:T(1024)S(1)} %dynamic_slice.31, bf16[1024,2048]{1,0:T(8,128)(2,1)S(1)} %bitcast.103, bf16[512,1024]{1,0:T(8,128)(2,1)S(1)} %collective-permute-done.5, bf16[512,1024]{1,0:T(8,128)(2,1)S(1)} %fusion.25), kind=kOutput, calls=%fused_computation.8 | convolution fusion | flops 4311744512 | bytes 18882560 | tf_op jit(solution)/shard_map/dot_general | solution.py:21
  259.1 3.4 fusion.36
  262.4 1.9 collective-permute-start.10
  264.4 2.4 collective-permute-start.12
  267.0 5.8 fusion.63
  273.2 7.4 %collective-permute-done.12 = bf16[512,1024]{1,0:T(8,128)(2,1)S(1)} collective-permute-done((bf16[512,1024]{1,0:T(8,128)(2,1)}, bf16[512,1024]{1,0:T(8,128)(2,1)S(1)}, u32[]{:S(2)}, u32[]{:S(2)}) %collective-permute-start.12) | collective-permute-done | bytes 1048608 | tf_op jit(solution)/shard_map/ppermute | solution.py:184
  281.8 1.9 fusion.61
  284.0 2.6 collective-permute-done.13
  286.6 6.3 convolution_convert_fusion.2
  293.0 8.3 %fusion.5 = bf16[1024,2048]{1,0:T(8,128)(2,1)S(1)} fusion(f32[1024,2048]{1,0:T(8,128)S(1)} %bitcast.124, bf16[1024,2048]{1,0:T(8,128)(2,1)S(1)} %bitcast.102, f32[2048]{0:T(1024)S(1)} %dynamic_slice.31, bf16[512,1024]{1,0:T(8,128)(2,1)S(1)} %collective-permute-done.13, bf16[512,1024]{1,0:T(8,128)(2,1)S(1)} %convert_element_type.243), kind=kOutput, calls=%fused_computation.6 | convolution fusion | flops 4322230272 | bytes 18882560 | tf_op jit(solution)/shard_map/dot_general | solution.py:21
  301.3 2.4 fusion.33
  304.4 6.7 %convolution_convert_fusion.1 = bf16[1024,2048]{1,0:T(8,128)(2,1)} fusion(bf16[1024,2048]{1,0:T(8,128)(2,1)S(1)} %fusion.5, bf16[512,1024]{1,0:T(8,128)(2,1)S(1)} %copy-done.33, bf16[512,1024]{1,0:T(8,128)(2,1)S(1)} %copy-done.21), kind=kOutput, calls=%fused_computation.29 | convolution fusion | flops 4301258752 | bytes 10485760 | tf_op jit(solution)/shard_map/dot_general | solution.py:21
  311.1 2.4 add_add_fusion
  317.0 2.9 convert_reduce_fusion
  320.5 3.6 convolution_convert_fusion.4.do_ref
  324.1 3.5 convolution_convert_fusion.3
  327.6 27.9 %attn_bwd.1 = (bf16[1024,512]{1,0:T(8,128)(2,1)}, bf16[1024,512]{1,0:T(8,128)(2,1)}, bf16[1024,512]{1,0:T(8,128)(2,1)}) custom-call(s32[1024,1]{1,0:T(8,128)} %copy.44.seg_col, s32[1,1024]{1,0:T(1,128)} %bitcast.121, f32[1024,512]{1,0:T(8,128)} %get-tuple-element.31.lse_ref, bf16[1024,1536]{1,0:T(8,128)(2,1)} %add_convert_fusion.q_ref.k_ref.v_ref, ...), custom_call_target="tpu_custom_call" | custom-call | flops 10737418240 | bytes 9437184 | tf_op jit(solution)/shard_map/attn_bwd/pallas_call | solution.py:137
  357.8 6.5 convolution_convert_fusion
  365.5 1.8 pad_maximum_fusion.2
  367.5 1.9 fusion.11
  370.1 58.6 %collective-permute-done.19 = bf16[8,80,2048]{2,1,0:T(8,128)(2,1)} collective-permute-done((bf16[8,80,2048]{2,1,0:T(8,128)(2,1)}, bf16[8,80,2048]{2,1,0:T(8,128)(2,1)}, u32[]{:S(2)}, u32[]{:S(2)}) %collective-permute-start.19) | collective-permute-done | bytes 2621472 | tf_op jit(solution)/shard_map/ppermute | solution.py:224
  428.7 5.1 fusion.6
  433.9 1.9 dynamic-slice_bitcast_fusion
  435.9 46.2 %collective-permute-done.23 = bf16[8,64,2048]{2,1,0:T(8,128)(2,1)S(1)} collective-permute-done((bf16[8,64,2048]{2,1,0:T(8,128)(2,1)S(1)}, bf16[8,64,2048]{2,1,0:T(8,128)(2,1)S(1)}, u32[]{:S(2)}, u32[]{:S(2)}) %collective-permute-start.23) | collective-permute-done | bytes 2097184 | tf_op jit(solution)/shard_map/ppermute | solution.py:224
  482.0 2.1 fusion.7
  484.2 1.9 dynamic-slice_bitcast_fusion.1
  486.2 45.2 %collective-permute-done.21 = bf16[8,64,2048]{2,1,0:T(8,128)(2,1)S(1)} collective-permute-done((bf16[8,64,2048]{2,1,0:T(8,128)(2,1)S(1)}, bf16[8,64,2048]{2,1,0:T(8,128)(2,1)S(1)}, u32[]{:S(2)}, u32[]{:S(2)}) %collective-permute-start.21) | collective-permute-done | bytes 2097184 | tf_op jit(solution)/shard_map/ppermute | solution.py:224
  531.4 2.1 fusion.8
  533.8 3.4 fusion.30
  537.2 2.8 collective-permute-start.16
  540.0 1.9 collective-permute-start.11
  542.3 2.8 add_convert_fusion.1
  545.1 3.3 collective-permute-start.17
  548.5 2.3 collective-permute-start.20
  550.7 20.9 %reduce-scatter.8.cloned.1.call-done = bf16[64,2048]{1,0:T(8,128)(2,1)} async-done(((bf16[512,2048]{1,0:T(8,128)(2,1)}), bf16[64,2048]{1,0:T(8,128)(2,1)}) %reduce-scatter.8.cloned.1.call-update) | async-done | bytes 262160 | tf_op jit(solution)/shard_map/reduce_scatter | solution.py:240
  571.7 5.5 collective-permute-start.24
  577.2 65.4 %reduce-scatter.6.cloned.1.call-done = bf16[64,2048]{1,0:T(8,128)(2,1)} async-done(((bf16[512,2048]{1,0:T(8,128)(2,1)}), bf16[64,2048]{1,0:T(8,128)(2,1)}) %reduce-scatter.6.cloned.1.call-update) | async-done | bytes 262160 | tf_op jit(solution)/shard_map/reduce_scatter | solution.py:240
  642.6 5.2 collective-permute-start.22
  647.8 1.6 convert_element_type.255
  650.2 1.8 collective-permute-done.22
  654.9 2.3 copy.60
  (198 shorter events, 33.1 us)
Async XLA Ops:
  7.2 71.9 %all-gather.7.cloned.1.call-start = ((), (), s32[]{:S(2)}) async-start(), calls=%async_computation.6 | async-start | bytes 2949120 | tf_op jit(solution)/shard_map/all_gather | solution.py:228
  14.3 9.3 %collective-permute-start.2 = (bf16[80,2048]{1,0:T(8,128)(2,1)S(1)}, bf16[80,2048]{1,0:T(8,128)(2,1)S(1)}, u32[]{:S(2)}, u32[]{:S(2)}) collective-permute-start(bf16[80,2048]{1,0:T(8,128)(2,1)S(1)} %fusion.50), channel_id=1, source_target_pairs={{0,0},{1,2},{2,1},{3,3},{4,4},{5,6},{6,5},{7,7},{8,8},{9,10},{10,9... | collective-permute-start | bytes 983048 | tf_op jit(solution)/shard_map/ppermute | solution.py:184
  24.3 132.3 %all-gather.11.cloned.1.call-start = ((), (), s32[]{:S(2)}) async-start(), calls=%async_computation.8 | async-start | bytes 2359296 | tf_op jit(solution)/shard_map/all_gather | solution.py:228
  24.4 7.9 %collective-permute-start.8 = (bf16[64,2048]{1,0:T(8,128)(2,1)}, bf16[64,2048]{1,0:T(8,128)(2,1)S(1)}, u32[]{:S(2)}, u32[]{:S(2)}) collective-permute-start(bf16[64,2048]{1,0:T(8,128)(2,1)} %param.26), channel_id=1, source_target_pairs={{0,0},{1,2},{2,1},{3,3},{4,4},{5,6},{6,5},{7,7},{8,8},{9,10},{10,9... | collective-permute-start | bytes 786440 | tf_op jit(solution)/shard_map/ppermute | solution.py:184
  33.0 167.8 %all-gather.9.cloned.1.call-start = ((), (), s32[]{:S(2)}) async-start(), calls=%async_computation.7 | async-start | bytes 2359296 | tf_op jit(solution)/shard_map/all_gather | solution.py:228
  79.1 78.0 %collective-permute-start.3 = (bf16[8,80,2048]{2,1,0:T(8,128)(2,1)}, bf16[8,80,2048]{2,1,0:T(8,128)(2,1)}, u32[]{:S(2)}, u32[]{:S(2)}) collective-permute-start(bf16[8,80,2048]{2,1,0:T(8,128)(2,1)} %bitcast.109), channel_id=1, source_target_pairs={{0,1},{1,0},{2,3},{3,2},{4,5},{5,4},{6,7},{7,6},{8,9},{9,8},{10,11... | collective-permute-start | bytes 7864328 | tf_op jit(solution)/shard_map/ppermute | solution.py:224
  80.3 68.8 %collective-permute-start = (bf16[512,1024]{1,0:T(8,128)(2,1)}, bf16[512,1024]{1,0:T(8,128)(2,1)S(1)}, u32[]{:S(2)}, u32[]{:S(2)}) collective-permute-start(bf16[512,1024]{1,0:T(8,128)(2,1)} %param.20), channel_id=1, source_target_pairs={{0,0},{1,2},{2,1},{3,3},{4,4},{5,6},{6,5},{7,7},{8,8},{9,10},{10,9... | collective-permute-start | bytes 3145736 | tf_op jit(solution)/shard_map/ppermute | solution.py:184
  84.5 67.4 %collective-permute-start.6 = (bf16[64,2048]{1,0:T(8,128)(2,1)}, bf16[64,2048]{1,0:T(8,128)(2,1)S(1)}, u32[]{:S(2)}, u32[]{:S(2)}) collective-permute-start(bf16[64,2048]{1,0:T(8,128)(2,1)} %param.25), channel_id=1, source_target_pairs={{0,0},{1,2},{2,1},{3,3},{4,4},{5,6},{6,5},{7,7},{8,8},{9,10},{10,9... | collective-permute-start | bytes 786440 | tf_op jit(solution)/shard_map/ppermute | solution.py:184
  149.1 7.5 %copy-start.18 = (bf16[512,1024]{1,0:T(8,128)(2,1)}, bf16[512,1024]{1,0:T(8,128)(2,1)S(1)}, u32[]{:S(2)}) copy-start(bf16[512,1024]{1,0:T(8,128)(2,1)S(1)} %collective-permute-done) | copy-start | bytes 3145732
  149.1 6.5 collective-permute-start.1
  152.6 395.8 %reduce-scatter.4.cloned.1.call-start = ((), (), s32[]{:S(2)}) async-start(), calls=%async_computation.3 | async-start | bytes 2949120 | tf_op jit(solution)/shard_map/reduce_scatter | solution.py:240
  153.5 3.1 copy-start.30
  156.7 47.4 %collective-permute-start.9 = (bf16[8,64,2048]{2,1,0:T(8,128)(2,1)}, bf16[8,64,2048]{2,1,0:T(8,128)(2,1)}, u32[]{:S(2)}, u32[]{:S(2)}) collective-permute-start(bf16[8,64,2048]{2,1,0:T(8,128)(2,1)} %bitcast.111), channel_id=1, source_target_pairs={{0,1},{1,0},{2,3},{3,2},{4,5},{5,4},{6,7},{7,6},{8,9},{9,8},{10,11... | collective-permute-start | bytes 6291464 | tf_op jit(solution)/shard_map/ppermute | solution.py:224
  162.0 1.9 copy-start.1
  163.9 28.7 %copy-start.23 = (bf16[8,2,64,512]{3,2,1,0:T(8,128)(2,1)}, bf16[8,2,64,512]{3,2,1,0:T(8,128)(2,1)S(1)}, u32[]{:S(2)}) copy-start(bf16[8,2,64,512]{3,2,1,0:T(8,128)(2,1)S(1)} %pad_maximum_fusion.12) | copy-start | bytes 3145732
  164.4 7.7 %copy-start.14 = (bf16[8,2,64,1536]{3,2,1,0:T(8,128)(2,1)}, bf16[8,2,64,1536]{3,2,1,0:T(8,128)(2,1)S(1)}, u32[]{:S(2)}) copy-start(bf16[8,2,64,1536]{3,2,1,0:T(8,128)(2,1)S(1)} %fusion.9) | copy-start | bytes 9437188
  192.6 11.5 %copy-start.16 = (bf16[512,2048]{1,0:T(8,128)(2,1)S(1)}, bf16[512,2048]{1,0:T(8,128)(2,1)}, u32[]{:S(2)}) copy-start(bf16[512,2048]{1,0:T(8,128)(2,1)} %all-gather.11.cloned.1.call-done) | copy-start | bytes 6291460
  195.5 13.3 %collective-permute-start.4 = (bf16[512,1024]{1,0:T(8,128)(2,1)}, bf16[512,1024]{1,0:T(8,128)(2,1)}, u32[]{:S(2)}, u32[]{:S(2)}) collective-permute-start(bf16[512,1024]{1,0:T(8,128)(2,1)} %convolution_convert_fusion.5), channel_id=1, source_target_pairs={{0,2},{2,0},{1,3},{3,1},{4,6},{6,4},{5,7},{7,5},{8,10},{10,8},{9,1... | collective-permute-start | bytes 3145736 | tf_op jit(solution)/shard_map/ppermute | solution.py:188
  200.8 47.3 %collective-permute-start.7 = (bf16[8,64,2048]{2,1,0:T(8,128)(2,1)}, bf16[8,64,2048]{2,1,0:T(8,128)(2,1)}, u32[]{:S(2)}, u32[]{:S(2)}) collective-permute-start(bf16[8,64,2048]{2,1,0:T(8,128)(2,1)} %bitcast.113), channel_id=1, source_target_pairs={{0,1},{1,0},{2,3},{3,2},{4,5},{5,4},{6,7},{7,6},{8,9},{9,8},{10,11... | collective-permute-start | bytes 6291464 | tf_op jit(solution)/shard_map/ppermute | solution.py:224
  206.3 2.5 copy-start.19
  211.8 36.3 %copy-start.17 = (bf16[512,2048]{1,0:T(8,128)(2,1)S(1)}, bf16[512,2048]{1,0:T(8,128)(2,1)}, u32[]{:S(2)}) copy-start(bf16[512,2048]{1,0:T(8,128)(2,1)} %all-gather.9.cloned.1.call-done) | copy-start | bytes 6291460
  212.2 38.4 %copy-start.20 = (bf16[512,1024]{1,0:T(8,128)(2,1)}, bf16[512,1024]{1,0:T(8,128)(2,1)S(1)}, u32[]{:S(2)}) copy-start(bf16[512,1024]{1,0:T(8,128)(2,1)S(1)} %fusion.25) | copy-start | bytes 3145732
  212.2 38.4 %collective-permute-start.5 = (bf16[512,1024]{1,0:T(8,128)(2,1)S(1)}, bf16[512,1024]{1,0:T(8,128)(2,1)S(1)}, u32[]{:S(2)}, u32[]{:S(2)}) collective-permute-start(bf16[512,1024]{1,0:T(8,128)(2,1)S(1)} %fusion.25), channel_id=1, source_target_pairs={{0,2},{2,0},{1,3},{3,1},{4,6},{6,4},{5,7},{7,5},{8,10},{10,8},{9,1... | collective-permute-start | bytes 3145736 | tf_op jit(solution)/shard_map/ppermute | solution.py:188
  250.6 8.5 %copy-start.9 = (bf16[8,2,64,2048]{3,2,1,0:T(8,128)(2,1)}, bf16[8,2,64,2048]{3,2,1,0:T(8,128)(2,1)S(1)}, u32[]{:S(2)}) copy-start(bf16[8,2,64,2048]{3,2,1,0:T(8,128)(2,1)S(1)} %pad_maximum_fusion) | copy-start | bytes 12582916
  250.7 8.4 %copy-start.32 = (bf16[512,1024]{1,0:T(8,128)(2,1)}, bf16[512,1024]{1,0:T(8,128)(2,1)S(1)}, u32[]{:S(2)}) copy-start(bf16[512,1024]{1,0:T(8,128)(2,1)S(1)} %collective-permute-done.5) | copy-start | bytes 3145732
  250.7 8.4 %copy-start.7 = (bf16[8,2,64,2048]{3,2,1,0:T(8,128)(2,1)S(1)}, bf16[8,2,64,2048]{3,2,1,0:T(8,128)(2,1)}, u32[]{:S(2)}) copy-start(bf16[8,2,64,2048]{3,2,1,0:T(8,128)(2,1)} %copy.46) | copy-start | bytes 12582916
  259.1 3.4 copy-start.35
  259.1 7.8 %copy-start.31 = (s32[1024]{0:T(1024)S(1)}, s32[1024]{0:T(1024)}, u32[]{:S(2)}) copy-start(s32[1024]{0:T(1024)} %copy-done.30) | copy-start | bytes 12292
  262.4 4.6 collective-permute-start.10
  264.4 16.3 %collective-permute-start.12 = (bf16[512,1024]{1,0:T(8,128)(2,1)}, bf16[512,1024]{1,0:T(8,128)(2,1)S(1)}, u32[]{:S(2)}, u32[]{:S(2)}) collective-permute-start(bf16[512,1024]{1,0:T(8,128)(2,1)} %param.36), channel_id=1, source_target_pairs={{0,0},{1,2},{2,1},{3,3},{4,4},{5,6},{6,5},{7,7},{8,8},{9,10},{10,9... | collective-permute-start | bytes 3145736 | tf_op jit(solution)/shard_map/ppermute | solution.py:184
  281.8 4.8 copy-start.36
  283.7 9.2 %slice-start = ((s8[8388608]{0:T(1024)(128)(4,1)}), s8[4194304]{0:T(1024)(128)(4,1)S(1)}, s32[]{:S(2)}) async-start(s8[8388608]{0:T(1024)(128)(4,1)} %bitcast.123), calls=%async_computation.9 | async-start | bytes 8388608
  283.9 9.1 %copy-start.8 = (bf16[8,2,64,2048]{3,2,1,0:T(8,128)(2,1)S(1)}, bf16[8,2,64,2048]{3,2,1,0:T(8,128)(2,1)}, u32[]{:S(2)}) copy-start(bf16[8,2,64,2048]{3,2,1,0:T(8,128)(2,1)} %copy.46) | copy-start | bytes 12582916
  283.9 9.0 %slice-start.1 = ((s8[8388608]{0:T(1024)(128)(4,1)}), s8[4194304]{0:T(1024)(128)(4,1)S(1)}, s32[]{:S(2)}) async-start(s8[8388608]{0:T(1024)(128)(4,1)} %bitcast.123), calls=%async_computation.10 | async-start | bytes 8388608
  283.9 2.7 collective-permute-start.13
  293.0 8.3 %copy-start.10 = (bf16[8,2,64,2048]{3,2,1,0:T(8,128)(2,1)S(1)}, bf16[8,2,64,2048]{3,2,1,0:T(8,128)(2,1)}, u32[]{:S(2)}) copy-start(bf16[8,2,64,2048]{3,2,1,0:T(8,128)(2,1)} %copy-done.9) | copy-start | bytes 12582916
  301.3 9.7 %copy-start.11 = (bf16[1024,2048]{1,0:T(8,128)(2,1)}, bf16[1024,2048]{1,0:T(8,128)(2,1)S(1)}, u32[]{:S(2)}) copy-start(bf16[1024,2048]{1,0:T(8,128)(2,1)S(1)} %fusion.5) | copy-start | bytes 12582916
  301.3 2.6 copy-start.21
  301.3 3.0 copy-start.33
  303.7 7.3 %collective-permute-start.14 = (bf16[512,1024]{1,0:T(8,128)(2,1)S(1)}, bf16[512,1024]{1,0:T(8,128)(2,1)S(1)}, u32[]{:S(2)}, u32[]{:S(2)}) collective-permute-start(bf16[512,1024]{1,0:T(8,128)(2,1)S(1)} %fusion.33), channel_id=1, source_target_pairs={{0,2},{2,0},{1,3},{3,1},{4,6},{6,4},{5,7},{7,5},{8,10},{10,8},{9,1... | collective-permute-start | bytes 3145736 | tf_op jit(solution)/shard_map/ppermute | solution.py:188
  316.6 3.9 collective-permute-start.15
  317.0 3.4 copy-start.24
  320.5 3.6 copy-start.34
  355.5 1.9 copy-start.12
  355.5 2.2 copy-start.22
  357.8 6.5 copy-start.25
  365.0 2.3 collective-permute-start.18
  367.3 2.8 copy-start.2
  370.1 58.6 %collective-permute-start.19 = (bf16[8,80,2048]{2,1,0:T(8,128)(2,1)}, bf16[8,80,2048]{2,1,0:T(8,128)(2,1)}, u32[]{:S(2)}, u32[]{:S(2)}) collective-permute-start(bf16[8,80,2048]{2,1,0:T(8,128)(2,1)} %fusion.11), channel_id=1, source_target_pairs={{0,1},{1,0},{2,3},{3,2},{4,5},{5,4},{6,7},{7,6},{8,9},{9,8},{10,11... | collective-permute-start | bytes 7864328 | tf_op jit(solution)/shard_map/ppermute | solution.py:224
  433.8 137.9 %reduce-scatter.8.cloned.1.call-start = ((), (), s32[]{:S(2)}) async-start(), calls=%async_computation.5 | async-start | bytes 2359296 | tf_op jit(solution)/shard_map/reduce_scatter | solution.py:240
  433.9 48.2 %copy-start.6 = (bf16[1024,2048]{1,0:T(8,128)(2,1)S(1)}, bf16[1024,2048]{1,0:T(8,128)(2,1)}, u32[]{:S(2)}) copy-start(bf16[1024,2048]{1,0:T(8,128)(2,1)} %convolution_convert_fusion.2) | copy-start | bytes 12582916
  435.8 46.3 %collective-permute-start.23 = (bf16[8,64,2048]{2,1,0:T(8,128)(2,1)S(1)}, bf16[8,64,2048]{2,1,0:T(8,128)(2,1)S(1)}, u32[]{:S(2)}, u32[]{:S(2)}) collective-permute-start(bf16[8,64,2048]{2,1,0:T(8,128)(2,1)S(1)} %dynamic-slice_bitcast_fusion), channel_id=1, source_target_pairs={{0,1},{1,0},{2,3},{3,2},{4,5},{5,4},{6,7},{7,6},{8,9},{9,8},{10,11... | collective-permute-start | bytes 6291464 | tf_op jit(solution)/shard_map/ppermute | solution.py:224
  484.1 158.5 %reduce-scatter.6.cloned.1.call-start = ((), (), s32[]{:S(2)}) async-start(), calls=%async_computation.4 | async-start | bytes 2359296 | tf_op jit(solution)/shard_map/reduce_scatter | solution.py:240
  484.2 47.2 %copy-start.5 = (bf16[1024,2048]{1,0:T(8,128)(2,1)S(1)}, bf16[1024,2048]{1,0:T(8,128)(2,1)}, u32[]{:S(2)}) copy-start(bf16[1024,2048]{1,0:T(8,128)(2,1)} %convolution_convert_fusion.1) | copy-start | bytes 12582916
  486.1 45.3 %collective-permute-start.21 = (bf16[8,64,2048]{2,1,0:T(8,128)(2,1)S(1)}, bf16[8,64,2048]{2,1,0:T(8,128)(2,1)S(1)}, u32[]{:S(2)}, u32[]{:S(2)}) collective-permute-start(bf16[8,64,2048]{2,1,0:T(8,128)(2,1)S(1)} %dynamic-slice_bitcast_fusion.1), channel_id=1, source_target_pairs={{0,1},{1,0},{2,3},{3,2},{4,5},{5,4},{6,7},{7,6},{8,9},{9,8},{10,11... | collective-permute-start | bytes 6291464 | tf_op jit(solution)/shard_map/ppermute | solution.py:224
  531.4 2.4 copy-start.15
  533.8 8.5 %copy-start.4 = (f32[512,1024]{1,0:T(8,128)S(1)}, f32[512,1024]{1,0:T(8,128)}, u32[]{:S(2)}) copy-start(f32[512,1024]{1,0:T(8,128)} %copy-done.3) | copy-start | bytes 6291460
  533.8 8.5 %copy-start.26 = (bf16[1024,1536]{1,0:T(8,128)(2,1)S(1)}, bf16[1024,1536]{1,0:T(8,128)(2,1)}, u32[]{:S(2)}) copy-start(bf16[1024,1536]{1,0:T(8,128)(2,1)} %copy-done.25) | copy-start | bytes 9437188
  537.2 5.1 collective-permute-start.16
  540.0 107.7 %collective-permute-start.11 = (bf16[512,1024]{1,0:T(8,128)(2,1)}, bf16[512,1024]{1,0:T(8,128)(2,1)}, u32[]{:S(2)}, u32[]{:S(2)}) collective-permute-start(bf16[512,1024]{1,0:T(8,128)(2,1)} %get-tuple-element.59), channel_id=1, source_target_pairs={{0,0},{1,2},{2,1},{3,3},{4,4},{5,6},{6,5},{7,7},{8,8},{9,10},{10,9... | collective-permute-start | bytes 3145736 | tf_op jit(solution)/shard_map/ppermute | solution.py:184
  545.1 102.7 %collective-permute-start.17 = (bf16[512,1024]{1,0:T(8,128)(2,1)}, bf16[512,1024]{1,0:T(8,128)(2,1)S(1)}, u32[]{:S(2)}, u32[]{:S(2)}) collective-permute-start(bf16[512,1024]{1,0:T(8,128)(2,1)} %add_convert_fusion.1), channel_id=1, source_target_pairs={{0,0},{1,2},{2,1},{3,3},{4,4},{5,6},{6,5},{7,7},{8,8},{9,10},{10,9... | collective-permute-start | bytes 3145736 | tf_op jit(solution)/shard_map/ppermute | solution.py:184
  548.5 104.4 %collective-permute-start.20 = (bf16[80,2048]{1,0:T(8,128)(2,1)}, bf16[80,2048]{1,0:T(8,128)(2,1)S(1)}, u32[]{:S(2)}, u32[]{:S(2)}) collective-permute-start(bf16[80,2048]{1,0:T(8,128)(2,1)} %reduce-scatter.4.cloned.1.call-done), channel_id=1, source_target_pairs={{0,0},{1,2},{2,1},{3,3},{4,4},{5,6},{6,5},{7,7},{8,8},{9,10},{10,9... | collective-permute-start | bytes 983048 | tf_op jit(solution)/shard_map/ppermute | solution.py:184
  571.7 77.7 %collective-permute-start.24 = (bf16[64,2048]{1,0:T(8,128)(2,1)}, bf16[64,2048]{1,0:T(8,128)(2,1)S(1)}, u32[]{:S(2)}, u32[]{:S(2)}) collective-permute-start(bf16[64,2048]{1,0:T(8,128)(2,1)} %reduce-scatter.8.cloned.1.call-done), channel_id=1, source_target_pairs={{0,0},{1,2},{2,1},{3,3},{4,4},{5,6},{6,5},{7,7},{8,8},{9,10},{10,9... | collective-permute-start | bytes 786440 | tf_op jit(solution)/shard_map/ppermute | solution.py:184
  642.6 9.4 %collective-permute-start.22 = (bf16[64,2048]{1,0:T(8,128)(2,1)}, bf16[64,2048]{1,0:T(8,128)(2,1)S(1)}, u32[]{:S(2)}, u32[]{:S(2)}) collective-permute-start(bf16[64,2048]{1,0:T(8,128)(2,1)} %reduce-scatter.6.cloned.1.call-done), channel_id=1, source_target_pairs={{0,0},{1,2},{2,1},{3,3},{4,4},{5,6},{6,5},{7,7},{8,8},{9,10},{10,9... | collective-permute-start | bytes 786440 | tf_op jit(solution)/shard_map/ppermute | solution.py:184
  (6 other events, 6.5 us)
Sparse Core Ops, SparseCore 0:
  24.4 54.5 all-gather.6
  81.8 47.9 all-gather.10
  152.8 47.9 all-gather.8
  433.9 68.5 reduce-scatter.3
  505.9 65.7 reduce-scatter.7
  575.6 66.9 reduce-scatter.5

commit v4 on v3

--- a/solution.py
+++ b/solution.py
@@ -231,12 +231,14 @@
         high = jnp.where(side == 0, other, mine)
         return jnp.stack([low, high], axis=1)
 
-    def scatter(x):
+    def halve(x):
         blocks = x.reshape(pairs, 2, -1, x.shape[-1])
         sent = across(lax.dynamic_index_in_dim(blocks, 1 - side, 1, keepdims=False))
         kept = lax.dynamic_index_in_dim(blocks, side, 1, keepdims=False)
         total = (kept.astype(f32) + sent.astype(f32)).astype(bf16)
-        total = total.reshape(-1, x.shape[-1])
+        return total.reshape(-1, x.shape[-1])
+
+    def finish(total):
         part = lax.psum_scatter(total, "pair", scatter_dimension=0, tiled=True)
         return turned(part).astype(f32)
 
@@ -300,18 +302,21 @@
     d_hidden = (mm(d_branch, down_mat) * gelu_parts(hidden)[1]).astype(bf16)
     part_down = mm(d_branch, active, TN).astype(bf16)
     d_hidden, part_down = lax.optimization_barrier((d_hidden, part_down))
-    grad_down = scatter(part_down)
+    half_down = halve(part_down)
     d_first = d_second + summed_rows(d_hidden, up_mat, NT)
     part_up = mm(first_all, d_hidden, TN).astype(bf16)
     d_first, part_up = lax.optimization_barrier((d_first, part_up))
-    grad_up = scatter(part_up)
+    half_up = halve(part_up)
     d_first_in = norm_back(d_first, n1, r1, gain_one)
     d_attn_own = d_first_in.astype(bf16)
     d_attn = jnp.concatenate([d_attn_own, partner(d_attn_own)], axis=0)
     d_context = mm(d_attn, out_mat).astype(bf16)
     part_out = mm(d_attn, context, TN).astype(bf16)
-    d_context, part_out = lax.optimization_barrier((d_context, part_out))
+    d_context, part_out, half_down = lax.optimization_barrier((d_context, part_out, half_down))
+    grad_down = finish(half_down)
     d_query, d_keys, d_values = attn_bwd(qkv, seg, lse, d_context)
+    d_query, half_up = lax.optimization_barrier((d_query, half_up))
+    grad_up = finish(half_up)
     d_qkv = jnp.concatenate([d_query, d_keys, d_values], axis=1)
     part_qkv = mm(rows_all, d_qkv, TN).astype(bf16)
     part_qkv = jnp.concatenate([part_qkv, part_out], axis=1)
@@ -338,7 +343,7 @@
     packed = jnp.pad(packed[:, None, :], ((0, 0), (0, sheet - 1), (0, 4 * width - small_size)))
     part_qkv = part_qkv.reshape(packed.shape[0], shard_rows, 4 * width)
     part_qkv = jnp.concatenate([part_qkv, packed], axis=1)
-    grad_qkv = scatter(whole_matrix(part_qkv))
+    grad_qkv = finish(halve(whole_matrix(part_qkv)))
     mine = grad_qkv[shard_rows, :small_size]
     grad_qkv = grad_qkv[:shard_rows]
     parts = [mine[i * piece : (i + 1) * piece] for i in range(8)]

time: 668 us -> 713 us (1.067)
  waiting for transfers between devices: 408 us -> 444 us
    reduce_scatter x3, waiting for transfers between devices: 86.4 us -> 184 us  [finish(): part = lax.psum_scatter(total, 'pair', scatter_dimension=0, tiled=True)]
    ppermute x6, waiting for transfers between devices: 186 us -> 125 us  [across(): return lax.ppermute(x, 'y', [(0, 1), (1, 0)])]
  transfers between devices with their start and end apart: 31 -> 31, of which waited for: 17 -> 18; matrix products, arithmetic and copies ran while one was open for 10% -> 11% of each run, Pallas kernels for 3% -> 7%
where the time goes in v4:
time: 713 us; the launch traced here: 709 us
  waiting for transfers between devices  444 us (62%)
  matrix products  80 us (11%)
  starting transfers between devices  50.3 us (7%)
  Pallas kernels  48.4 us (7%)
  other arithmetic  38.8 us (5%)
  local copies, waits for them, and re-layouts  32.4 us (5%)
  between operations  15.1 us (2%)
    reduce_scatter x3, waiting for transfers between devices, finish(): part = lax.psum_scatter(total, 'pair', scatter_dimension=0, tiled=True)  184 us
    ppermute x6, waiting for transfers between devices, across(): return lax.ppermute(x, 'y', [(0, 1), (1, 0)])  125 us
    ppermute x10, waiting for transfers between devices, turned(): return lax.ppermute(x, ('core', 'y'), [(0, 0), (1, 2), (2, 1), (3, 3)])  82 us
    dot_general x16, matrix products, mm(): return lax.dot_general(left, right, dims, preferred_element_type=f32)  80 us
    all_gather x3, waiting for transfers between devices, gather(): mine = lax.all_gather(shard, 'pair', axis=0, tiled=False)  49.5 us
    ppermute x10, starting transfers between devices, turned(): return lax.ppermute(x, ('core', 'y'), [(0, 0), (1, 2), (2, 1), (3, 3)])  37.5 us
    pallas_call x1, Pallas kernels, attn_bwd(): pl.pallas_call(attn_bwd_kernel, grid=(pairs, rows // block), in_specs=[co...  27.9 us
    pallas_call x1, Pallas kernels, attn_fwd(): pl.pallas_call(attn_fwd_kernel, grid=(pairs, rows // block), in_specs=[co...  20.5 us
  transfers between devices with their start and end apart: 31, of which 18 were waited for; matrix products, arithmetic and copies ran while one was open for 11% of the time, Pallas kernels for 7%

profile of v4, /device:TPU:1, one launch (start us, length us, event | category | flops | bytes accessed | tf_op | source)
XLA Modules:
  0.0 709.2 jit_solution(16001555950782914263)
XLA Ops:
  7.2 6.1 concatenate.47
  14.3 4.5 collective-permute-start.2
  18.8 4.7 collective-permute-done.2
  24.4 3.6 collective-permute-start.8
  28.0 4.3 collective-permute-done.8
  33.1 46.0 %all-gather.7.cloned.1.call-done = bf16[640,2048]{1,0:T(8,128)(2,1)} async-done(((bf16[80,2048]{1,0:T(8,128)(2,1)}), bf16[640,2048]{1,0:T(8,128)(2,1)}) %all-gather.7.cloned.1.call-update) | async-done | bytes 2621456 | tf_op jit(solution)/shard_map/all_gather | solution.py:228
  80.3 4.3 collective-permute-start
  84.5 1.9 collective-permute-start.6
  86.5 62.6 %collective-permute-done = bf16[512,1024]{1,0:T(8,128)(2,1)S(1)} collective-permute-done((bf16[512,1024]{1,0:T(8,128)(2,1)}, bf16[512,1024]{1,0:T(8,128)(2,1)S(1)}, u32[]{:S(2)}, u32[]{:S(2)}) %collective-permute-start) | collective-permute-done | bytes 1048608 | tf_op jit(solution)/shard_map/ppermute | solution.py:184
  157.1 2.9 select_bitcast_fusion.1
  160.0 1.5 copy-done
  164.5 7.5 %add_convert_fusion.q_ref.k_ref.v_ref = bf16[1024,1536]{1,0:T(8,128)(2,1)} fusion(bf16[1024,1024]{1,0:T(8,128)(2,1)} %constant_dynamic-update-slice_fusion, bf16[1024,1536]{1,0:T(8,128)(2,1)S(1)} %bitcast.106, f32[1536]{0:T(1024)S(1)} %pad_maximum_fusion.13), kind=kOutput, calls=%fused_computation.12 | convolution fusion | flops 3224371200 | bytes 8394752 | tf_op jit(solution)/shard_map/dot_general | solution.py:21
  172.0 20.5 %attn_fwd.1 = (bf16[1024,512]{1,0:T(8,128)(2,1)}, f32[1024,512]{1,0:T(8,128)}) custom-call(s32[1024,1]{1,0:T(8,128)} %copy.44.seg_col, s32[1,1024]{1,0:T(1,128)} %bitcast.120, bf16[1024,1536]{1,0:T(8,128)(2,1)} %add_convert_fusion.q_ref.k_ref.v_ref, bf16[1024,1536]{1,0:T(8,128)(2,1)} %add_convert_fusion.q_ref.k_ref.v_ref, ...), custom_call_target="tpu_custom_call" | custom-call | flops 4294967296 | bytes 6291456 | tf_op jit(solution)/shard_map/attn_fwd/pallas_call | solution.py:110
  192.5 2.9 convolution_convert_fusion.5
  195.4 1.9 collective-permute-start.4
  197.3 3.5 all-gather.9.cloned.1.call-done
  202.0 2.1 collective-permute-done.9
  204.1 1.9 select_bitcast_fusion.3
  206.3 2.2 copy.46
  208.8 2.6 fusion.65
  212.2 1.5 collective-permute-start.5
  213.8 34.3 %collective-permute-done.7 = bf16[8,64,2048]{2,1,0:T(8,128)(2,1)} collective-permute-done((bf16[8,64,2048]{2,1,0:T(8,128)(2,1)}, bf16[8,64,2048]{2,1,0:T(8,128)(2,1)}, u32[]{:S(2)}, u32[]{:S(2)}) %collective-permute-start.7) | collective-permute-done | bytes 2097184 | tf_op jit(solution)/shard_map/ppermute | solution.py:224
  248.0 2.1 select_bitcast_fusion.5
  250.7 8.4 %multiply_convert_fusion = (bf16[1024,2048]{1,0:T(8,128)(2,1)S(1)}, f32[1024,2048]{1,0:T(8,128)}) fusion(f32[2048]{0:T(1024)S(1)} %dynamic_slice.31, bf16[1024,2048]{1,0:T(8,128)(2,1)S(1)} %bitcast.103, bf16[512,1024]{1,0:T(8,128)(2,1)S(1)} %collective-permute-done.5, bf16[512,1024]{1,0:T(8,128)(2,1)S(1)} %fusion.25), kind=kOutput, calls=%fused_computation.8 | convolution fusion | flops 4311744512 | bytes 18882560 | tf_op jit(solution)/shard_map/dot_general | solution.py:21
  259.1 3.4 fusion.36
  262.5 1.9 collective-permute-start.10
  264.4 2.7 collective-permute-start.12
  267.3 5.8 fusion.63
  273.5 7.2 %collective-permute-done.12 = bf16[512,1024]{1,0:T(8,128)(2,1)S(1)} collective-permute-done((bf16[512,1024]{1,0:T(8,128)(2,1)}, bf16[512,1024]{1,0:T(8,128)(2,1)S(1)}, u32[]{:S(2)}, u32[]{:S(2)}) %collective-permute-start.12) | collective-permute-done | bytes 1048608 | tf_op jit(solution)/shard_map/ppermute | solution.py:184
  281.8 1.9 fusion.61
  285.3 2.8 collective-permute-done.13
  288.0 7.1 convolution_convert_fusion.2
  295.2 10.9 %fusion.5 = bf16[1024,2048]{1,0:T(8,128)(2,1)S(1)} fusion(f32[1024,2048]{1,0:T(8,128)} %get-tuple-element.89, bf16[1024,2048]{1,0:T(8,128)(2,1)S(1)} %bitcast.102, f32[2048]{0:T(1024)S(1)} %dynamic_slice.31, bf16[512,1024]{1,0:T(8,128)(2,1)} %collective-permute-done.13, bf16[512,1024]{1,0:T(8,128)(2,1)S(1)} %convert_element_type.243), kind=kOutput, calls=%fused_computation.6 | convolution fusion | flops 4322230272 | bytes 18882560 | tf_op jit(solution)/shard_map/dot_general | solution.py:21
  306.0 2.4 fusion.33
  308.6 1.4 dynamic-slice_bitcast_fusion.1
  310.9 6.4 convolution_convert_fusion.1
  317.4 2.4 add_add_fusion
  323.6 2.8 convert_reduce_fusion
  326.7 3.2 dynamic-slice_bitcast_fusion
  331.0 3.8 convolution_convert_fusion.4.do_ref
  334.9 3.7 convolution_convert_fusion.3
  338.5 18.7 %collective-permute-done.16 = bf16[8,64,2048]{2,1,0:T(8,128)(2,1)} collective-permute-done((bf16[8,64,2048]{2,1,0:T(8,128)(2,1)}, bf16[8,64,2048]{2,1,0:T(8,128)(2,1)}, u32[]{:S(2)}, u32[]{:S(2)}) %collective-permute-start.16) | collective-permute-done | bytes 2097184 | tf_op jit(solution)/shard_map/ppermute | solution.py:224
  357.3 3.7 fusion.8
  360.9 27.9 %attn_bwd.1 = (bf16[1024,512]{1,0:T(8,128)(2,1)}, bf16[1024,512]{1,0:T(8,128)(2,1)}, bf16[1024,512]{1,0:T(8,128)(2,1)}) custom-call(s32[1024,1]{1,0:T(8,128)} %copy.44.seg_col, s32[1,1024]{1,0:T(1,128)} %bitcast.121, f32[1024,512]{1,0:T(8,128)} %get-tuple-element.34.lse_ref, bf16[1024,1536]{1,0:T(8,128)(2,1)} %add_convert_fusion.q_ref.k_ref.v_ref, ...), custom_call_target="tpu_custom_call" | custom-call | flops 10737418240 | bytes 9437184 | tf_op jit(solution)/shard_map/attn_bwd/pallas_call | solution.py:137
  388.8 1.4 convert_reduce_fusion.1
  390.8 11.3 %collective-permute-done.17 = bf16[8,64,2048]{2,1,0:T(8,128)(2,1)S(1)} collective-permute-done((bf16[8,64,2048]{2,1,0:T(8,128)(2,1)}, bf16[8,64,2048]{2,1,0:T(8,128)(2,1)S(1)}, u32[]{:S(2)}, u32[]{:S(2)}) %collective-permute-start.17) | collective-permute-done | bytes 2097184 | tf_op jit(solution)/shard_map/ppermute | solution.py:224
  402.1 3.7 fusion.7
  407.4 6.5 convolution_convert_fusion
  415.6 1.8 pad_maximum_fusion.2
  418.3 58.2 %collective-permute-done.21 = bf16[8,80,2048]{2,1,0:T(8,128)(2,1)S(1)} collective-permute-done((bf16[8,80,2048]{2,1,0:T(8,128)(2,1)S(1)}, bf16[8,80,2048]{2,1,0:T(8,128)(2,1)S(1)}, u32[]{:S(2)}, u32[]{:S(2)}) %collective-permute-start.21) | collective-permute-done | bytes 2621472 | tf_op jit(solution)/shard_map/ppermute | solution.py:224
  476.5 2.6 fusion.6
  481.0 3.4 fusion.30
  485.2 2.1 collective-permute-start.11
  487.5 2.8 add_convert_fusion.1
  490.3 3.3 collective-permute-start.19
  493.6 53.9 %reduce-scatter.4.cloned.1.call-done = bf16[80,2048]{1,0:T(8,128)(2,1)} async-done(((bf16[640,2048]{1,0:T(8,128)(2,1)}), bf16[80,2048]{1,0:T(8,128)(2,1)}) %reduce-scatter.4.cloned.1.call-update) | async-done | bytes 327696 | tf_op jit(solution)/shard_map/reduce_scatter | solution.py:242
  547.5 4.6 collective-permute-start.22
  552.1 65.1 %reduce-scatter.8.cloned.1.call-done = bf16[64,2048]{1,0:T(8,128)(2,1)} async-done(((bf16[512,2048]{1,0:T(8,128)(2,1)}), bf16[64,2048]{1,0:T(8,128)(2,1)}) %reduce-scatter.8.cloned.1.call-update) | async-done | bytes 262160 | tf_op jit(solution)/shard_map/reduce_scatter | solution.py:242
  617.2 5.2 collective-permute-start.24
  622.4 65.2 %reduce-scatter.6.cloned.1.call-done = bf16[64,2048]{1,0:T(8,128)(2,1)} async-done(((bf16[512,2048]{1,0:T(8,128)(2,1)}), bf16[64,2048]{1,0:T(8,128)(2,1)}) %reduce-scatter.6.cloned.1.call-update) | async-done | bytes 262160 | tf_op jit(solution)/shard_map/reduce_scatter | solution.py:242
  687.6 5.2 collective-permute-start.23
  692.8 1.6 convert_element_type.263
  695.2 1.8 collective-permute-done.23
  699.9 2.3 copy.60
  (191 shorter events, 38.3 us)
Async XLA Ops:
  7.2 71.9 %all-gather.7.cloned.1.call-start = ((), (), s32[]{:S(2)}) async-start(), calls=%async_computation.6 | async-start | bytes 2949120 | tf_op jit(solution)/shard_map/all_gather | solution.py:228
  14.3 9.3 %collective-permute-start.2 = (bf16[80,2048]{1,0:T(8,128)(2,1)S(1)}, bf16[80,2048]{1,0:T(8,128)(2,1)S(1)}, u32[]{:S(2)}, u32[]{:S(2)}) collective-permute-start(bf16[80,2048]{1,0:T(8,128)(2,1)S(1)} %fusion.50), channel_id=1, source_target_pairs={{0,0},{1,2},{2,1},{3,3},{4,4},{5,6},{6,5},{7,7},{8,8},{9,10},{10,9... | collective-permute-start | bytes 983048 | tf_op jit(solution)/shard_map/ppermute | solution.py:184
  24.3 132.3 %all-gather.11.cloned.1.call-start = ((), (), s32[]{:S(2)}) async-start(), calls=%async_computation.8 | async-start | bytes 2359296 | tf_op jit(solution)/shard_map/all_gather | solution.py:228
  24.4 7.9 %collective-permute-start.8 = (bf16[64,2048]{1,0:T(8,128)(2,1)}, bf16[64,2048]{1,0:T(8,128)(2,1)S(1)}, u32[]{:S(2)}, u32[]{:S(2)}) collective-permute-start(bf16[64,2048]{1,0:T(8,128)(2,1)} %param.26), channel_id=1, source_target_pairs={{0,0},{1,2},{2,1},{3,3},{4,4},{5,6},{6,5},{7,7},{8,8},{9,10},{10,9... | collective-permute-start | bytes 786440 | tf_op jit(solution)/shard_map/ppermute | solution.py:184
  33.0 167.8 %all-gather.9.cloned.1.call-start = ((), (), s32[]{:S(2)}) async-start(), calls=%async_computation.7 | async-start | bytes 2359296 | tf_op jit(solution)/shard_map/all_gather | solution.py:228
  79.1 78.0 %collective-permute-start.3 = (bf16[8,80,2048]{2,1,0:T(8,128)(2,1)}, bf16[8,80,2048]{2,1,0:T(8,128)(2,1)}, u32[]{:S(2)}, u32[]{:S(2)}) collective-permute-start(bf16[8,80,2048]{2,1,0:T(8,128)(2,1)} %bitcast.109), channel_id=1, source_target_pairs={{0,1},{1,0},{2,3},{3,2},{4,5},{5,4},{6,7},{7,6},{8,9},{9,8},{10,11... | collective-permute-start | bytes 7864328 | tf_op jit(solution)/shard_map/ppermute | solution.py:224
  80.3 68.8 %collective-permute-start = (bf16[512,1024]{1,0:T(8,128)(2,1)}, bf16[512,1024]{1,0:T(8,128)(2,1)S(1)}, u32[]{:S(2)}, u32[]{:S(2)}) collective-permute-start(bf16[512,1024]{1,0:T(8,128)(2,1)} %param.20), channel_id=1, source_target_pairs={{0,0},{1,2},{2,1},{3,3},{4,4},{5,6},{6,5},{7,7},{8,8},{9,10},{10,9... | collective-permute-start | bytes 3145736 | tf_op jit(solution)/shard_map/ppermute | solution.py:184
  84.5 67.4 %collective-permute-start.6 = (bf16[64,2048]{1,0:T(8,128)(2,1)}, bf16[64,2048]{1,0:T(8,128)(2,1)S(1)}, u32[]{:S(2)}, u32[]{:S(2)}) collective-permute-start(bf16[64,2048]{1,0:T(8,128)(2,1)} %param.25), channel_id=1, source_target_pairs={{0,0},{1,2},{2,1},{3,3},{4,4},{5,6},{6,5},{7,7},{8,8},{9,10},{10,9... | collective-permute-start | bytes 786440 | tf_op jit(solution)/shard_map/ppermute | solution.py:184
  149.1 7.5 %copy-start.19 = (bf16[512,1024]{1,0:T(8,128)(2,1)}, bf16[512,1024]{1,0:T(8,128)(2,1)S(1)}, u32[]{:S(2)}) copy-start(bf16[512,1024]{1,0:T(8,128)(2,1)S(1)} %collective-permute-done) | copy-start | bytes 3145732
  149.1 6.5 collective-permute-start.1
  152.6 394.9 %reduce-scatter.4.cloned.1.call-start = ((), (), s32[]{:S(2)}) async-start(), calls=%async_computation.3 | async-start | bytes 2949120 | tf_op jit(solution)/shard_map/reduce_scatter | solution.py:242
  153.5 3.1 copy-start.30
  156.6 47.4 %collective-permute-start.9 = (bf16[8,64,2048]{2,1,0:T(8,128)(2,1)}, bf16[8,64,2048]{2,1,0:T(8,128)(2,1)}, u32[]{:S(2)}, u32[]{:S(2)}) collective-permute-start(bf16[8,64,2048]{2,1,0:T(8,128)(2,1)} %bitcast.111), channel_id=1, source_target_pairs={{0,1},{1,0},{2,3},{3,2},{4,5},{5,4},{6,7},{7,6},{8,9},{9,8},{10,11... | collective-permute-start | bytes 6291464 | tf_op jit(solution)/shard_map/ppermute | solution.py:224
  160.0 1.5 copy-start
  162.0 1.9 copy-start.1
  163.9 28.6 %copy-start.24 = (bf16[8,2,64,512]{3,2,1,0:T(8,128)(2,1)}, bf16[8,2,64,512]{3,2,1,0:T(8,128)(2,1)S(1)}, u32[]{:S(2)}) copy-start(bf16[8,2,64,512]{3,2,1,0:T(8,128)(2,1)S(1)} %pad_maximum_fusion.12) | copy-start | bytes 3145732
  164.5 7.5 %copy-start.15 = (bf16[8,2,64,1536]{3,2,1,0:T(8,128)(2,1)}, bf16[8,2,64,1536]{3,2,1,0:T(8,128)(2,1)S(1)}, u32[]{:S(2)}) copy-start(bf16[8,2,64,1536]{3,2,1,0:T(8,128)(2,1)S(1)} %fusion.9) | copy-start | bytes 9437188
  192.5 11.6 %copy-start.17 = (bf16[512,2048]{1,0:T(8,128)(2,1)S(1)}, bf16[512,2048]{1,0:T(8,128)(2,1)}, u32[]{:S(2)}) copy-start(bf16[512,2048]{1,0:T(8,128)(2,1)} %all-gather.11.cloned.1.call-done) | copy-start | bytes 6291460
  195.4 13.4 %collective-permute-start.4 = (bf16[512,1024]{1,0:T(8,128)(2,1)}, bf16[512,1024]{1,0:T(8,128)(2,1)}, u32[]{:S(2)}, u32[]{:S(2)}) collective-permute-start(bf16[512,1024]{1,0:T(8,128)(2,1)} %convolution_convert_fusion.5), channel_id=1, source_target_pairs={{0,2},{2,0},{1,3},{3,1},{4,6},{6,4},{5,7},{7,5},{8,10},{10,8},{9,1... | collective-permute-start | bytes 3145736 | tf_op jit(solution)/shard_map/ppermute | solution.py:188
  200.8 47.3 %collective-permute-start.7 = (bf16[8,64,2048]{2,1,0:T(8,128)(2,1)}, bf16[8,64,2048]{2,1,0:T(8,128)(2,1)}, u32[]{:S(2)}, u32[]{:S(2)}) collective-permute-start(bf16[8,64,2048]{2,1,0:T(8,128)(2,1)} %bitcast.113), channel_id=1, source_target_pairs={{0,1},{1,0},{2,3},{3,2},{4,5},{5,4},{6,7},{7,6},{8,9},{9,8},{10,11... | collective-permute-start | bytes 6291464 | tf_op jit(solution)/shard_map/ppermute | solution.py:224
  206.3 2.5 copy-start.20
  211.8 36.3 %copy-start.18 = (bf16[512,2048]{1,0:T(8,128)(2,1)S(1)}, bf16[512,2048]{1,0:T(8,128)(2,1)}, u32[]{:S(2)}) copy-start(bf16[512,2048]{1,0:T(8,128)(2,1)} %all-gather.9.cloned.1.call-done) | copy-start | bytes 6291460
  212.2 38.4 %copy-start.21 = (bf16[512,1024]{1,0:T(8,128)(2,1)}, bf16[512,1024]{1,0:T(8,128)(2,1)S(1)}, u32[]{:S(2)}) copy-start(bf16[512,1024]{1,0:T(8,128)(2,1)S(1)} %fusion.25) | copy-start | bytes 3145732
  212.2 38.4 %collective-permute-start.5 = (bf16[512,1024]{1,0:T(8,128)(2,1)S(1)}, bf16[512,1024]{1,0:T(8,128)(2,1)S(1)}, u32[]{:S(2)}, u32[]{:S(2)}) collective-permute-start(bf16[512,1024]{1,0:T(8,128)(2,1)S(1)} %fusion.25), channel_id=1, source_target_pairs={{0,2},{2,0},{1,3},{3,1},{4,6},{6,4},{5,7},{7,5},{8,10},{10,8},{9,1... | collective-permute-start | bytes 3145736 | tf_op jit(solution)/shard_map/ppermute | solution.py:188
  250.6 8.5 %copy-start.10 = (bf16[8,2,64,2048]{3,2,1,0:T(8,128)(2,1)}, bf16[8,2,64,2048]{3,2,1,0:T(8,128)(2,1)S(1)}, u32[]{:S(2)}) copy-start(bf16[8,2,64,2048]{3,2,1,0:T(8,128)(2,1)S(1)} %pad_maximum_fusion) | copy-start | bytes 12582916
  250.6 8.4 %copy-start.32 = (bf16[512,1024]{1,0:T(8,128)(2,1)}, bf16[512,1024]{1,0:T(8,128)(2,1)S(1)}, u32[]{:S(2)}) copy-start(bf16[512,1024]{1,0:T(8,128)(2,1)S(1)} %collective-permute-done.5) | copy-start | bytes 3145732
  250.7 8.4 %copy-start.8 = (bf16[8,2,64,2048]{3,2,1,0:T(8,128)(2,1)S(1)}, bf16[8,2,64,2048]{3,2,1,0:T(8,128)(2,1)}, u32[]{:S(2)}) copy-start(bf16[8,2,64,2048]{3,2,1,0:T(8,128)(2,1)} %copy.46) | copy-start | bytes 12582916
  259.1 3.4 copy-start.35
  259.1 8.0 %copy-start.31 = (s32[1024]{0:T(1024)S(1)}, s32[1024]{0:T(1024)}, u32[]{:S(2)}) copy-start(s32[1024]{0:T(1024)} %copy-done.30) | copy-start | bytes 12292
  262.5 4.8 collective-permute-start.10
  264.4 16.3 %collective-permute-start.12 = (bf16[512,1024]{1,0:T(8,128)(2,1)}, bf16[512,1024]{1,0:T(8,128)(2,1)S(1)}, u32[]{:S(2)}, u32[]{:S(2)}) collective-permute-start(bf16[512,1024]{1,0:T(8,128)(2,1)} %param.36), channel_id=1, source_target_pairs={{0,0},{1,2},{2,1},{3,3},{4,4},{5,6},{6,5},{7,7},{8,8},{9,10},{10,9... | collective-permute-start | bytes 3145736 | tf_op jit(solution)/shard_map/ppermute | solution.py:184
  283.7 1.3 copy-start.4
  285.2 2.9 collective-permute-start.13
  285.3 9.9 %copy-start.9 = (bf16[8,2,64,2048]{3,2,1,0:T(8,128)(2,1)S(1)}, bf16[8,2,64,2048]{3,2,1,0:T(8,128)(2,1)}, u32[]{:S(2)}) copy-start(bf16[8,2,64,2048]{3,2,1,0:T(8,128)(2,1)} %copy.46) | copy-start | bytes 12582916
  295.1 13.5 %copy-start.6 = (bf16[1024,2048]{1,0:T(8,128)(2,1)}, bf16[1024,2048]{1,0:T(8,128)(2,1)S(1)}, u32[]{:S(2)}) copy-start(bf16[1024,2048]{1,0:T(8,128)(2,1)S(1)} %convolution_convert_fusion.2) | copy-start | bytes 12582916
  295.2 10.9 %copy-start.11 = (bf16[8,2,64,2048]{3,2,1,0:T(8,128)(2,1)S(1)}, bf16[8,2,64,2048]{3,2,1,0:T(8,128)(2,1)}, u32[]{:S(2)}) copy-start(bf16[8,2,64,2048]{3,2,1,0:T(8,128)(2,1)} %copy-done.10) | copy-start | bytes 12582916
  306.0 11.3 %copy-start.12 = (bf16[1024,2048]{1,0:T(8,128)(2,1)}, bf16[1024,2048]{1,0:T(8,128)(2,1)S(1)}, u32[]{:S(2)}) copy-start(bf16[1024,2048]{1,0:T(8,128)(2,1)S(1)} %fusion.5) | copy-start | bytes 12582916
  308.4 8.9 %collective-permute-start.14 = (bf16[512,1024]{1,0:T(8,128)(2,1)S(1)}, bf16[512,1024]{1,0:T(8,128)(2,1)S(1)}, u32[]{:S(2)}, u32[]{:S(2)}) collective-permute-start(bf16[512,1024]{1,0:T(8,128)(2,1)S(1)} %fusion.33), channel_id=1, source_target_pairs={{0,2},{2,0},{1,3},{3,1},{4,6},{6,4},{5,7},{7,5},{8,10},{10,8},{9,1... | collective-permute-start | bytes 3145736 | tf_op jit(solution)/shard_map/ppermute | solution.py:188
  308.6 1.8 copy-start.22
  308.6 2.3 copy-start.33
  310.1 7.3 %copy-start.5 = (f32[512,1024]{1,0:T(8,128)S(1)}, f32[512,1024]{1,0:T(8,128)}, u32[]{:S(2)}) copy-start(f32[512,1024]{1,0:T(8,128)} %copy-done.4) | copy-start | bytes 6291460
  310.1 47.2 %collective-permute-start.16 = (bf16[8,64,2048]{2,1,0:T(8,128)(2,1)}, bf16[8,64,2048]{2,1,0:T(8,128)(2,1)}, u32[]{:S(2)}, u32[]{:S(2)}) collective-permute-start(bf16[8,64,2048]{2,1,0:T(8,128)(2,1)} %dynamic-slice_bitcast_fusion.1), channel_id=1, source_target_pairs={{0,1},{1,0},{2,3},{3,2},{4,5},{5,4},{6,7},{7,6},{8,9},{9,8},{10,11... | collective-permute-start | bytes 6291464 | tf_op jit(solution)/shard_map/ppermute | solution.py:224
  321.5 1.3 copy-start.2
  322.9 8.1 %collective-permute-start.15 = (bf16[512,1024]{1,0:T(8,128)(2,1)S(1)}, bf16[512,1024]{1,0:T(8,128)(2,1)}, u32[]{:S(2)}, u32[]{:S(2)}) collective-permute-start(bf16[512,1024]{1,0:T(8,128)(2,1)S(1)} %convert_element_type.249), channel_id=1, source_target_pairs={{0,2},{2,0},{1,3},{3,1},{4,6},{6,4},{5,7},{7,5},{8,10},{10,8},{9,1... | collective-permute-start | bytes 3145736 | tf_op jit(solution)/shard_map/ppermute | solution.py:188
  329.9 72.2 %collective-permute-start.17 = (bf16[8,64,2048]{2,1,0:T(8,128)(2,1)}, bf16[8,64,2048]{2,1,0:T(8,128)(2,1)S(1)}, u32[]{:S(2)}, u32[]{:S(2)}) collective-permute-start(bf16[8,64,2048]{2,1,0:T(8,128)(2,1)} %dynamic-slice_bitcast_fusion), channel_id=1, source_target_pairs={{0,1},{1,0},{2,3},{3,2},{4,5},{5,4},{6,7},{7,6},{8,9},{9,8},{10,11... | collective-permute-start | bytes 6291464 | tf_op jit(solution)/shard_map/ppermute | solution.py:224
  331.0 3.9 copy-start.34
  334.9 22.4 %copy-start.7 = (bf16[1024,2048]{1,0:T(8,128)(2,1)S(1)}, bf16[1024,2048]{1,0:T(8,128)(2,1)}, u32[]{:S(2)}) copy-start(bf16[1024,2048]{1,0:T(8,128)(2,1)} %copy-done.6) | copy-start | bytes 12582916
  390.8 15.0 %copy-start.14 = (bf16[1024,512]{1,0:T(8,128)(2,1)S(1)}, bf16[1024,512]{1,0:T(8,128)(2,1)}, u32[]{:S(2)}) copy-start(bf16[1024,512]{1,0:T(8,128)(2,1)} %get-tuple-element.39) | copy-start | bytes 3145732
  405.8 1.2 copy-start.23
  405.9 1.5 copy-start.13
  407.4 6.5 copy-start.25
  414.4 3.1 collective-permute-start.20
  417.9 58.6 %collective-permute-start.21 = (bf16[8,80,2048]{2,1,0:T(8,128)(2,1)S(1)}, bf16[8,80,2048]{2,1,0:T(8,128)(2,1)S(1)}, u32[]{:S(2)}, u32[]{:S(2)}) collective-permute-start(bf16[8,80,2048]{2,1,0:T(8,128)(2,1)S(1)} %fusion.11), channel_id=1, source_target_pairs={{0,1},{1,0},{2,3},{3,2},{4,5},{5,4},{6,7},{7,6},{8,9},{9,8},{10,11... | collective-permute-start | bytes 7864328 | tf_op jit(solution)/shard_map/ppermute | solution.py:224
  479.1 1.9 copy-start.16
  479.1 138.2 %reduce-scatter.8.cloned.1.call-start = ((), (), s32[]{:S(2)}) async-start(), calls=%async_computation.5 | async-start | bytes 2359296 | tf_op jit(solution)/shard_map/reduce_scatter | solution.py:242
  479.7 207.9 %reduce-scatter.6.cloned.1.call-start = ((), (), s32[]{:S(2)}) async-start(), calls=%async_computation.4 | async-start | bytes 2359296 | tf_op jit(solution)/shard_map/reduce_scatter | solution.py:242
  481.0 6.5 copy-start.3
  481.0 6.5 copy-start.26
  484.4 3.1 collective-permute-start.18
  485.2 207.6 %collective-permute-start.11 = (bf16[512,1024]{1,0:T(8,128)(2,1)}, bf16[512,1024]{1,0:T(8,128)(2,1)}, u32[]{:S(2)}, u32[]{:S(2)}) collective-permute-start(bf16[512,1024]{1,0:T(8,128)(2,1)} %get-tuple-element.65), channel_id=1, source_target_pairs={{0,0},{1,2},{2,1},{3,3},{4,4},{5,6},{6,5},{7,7},{8,8},{9,10},{10,9... | collective-permute-start | bytes 3145736 | tf_op jit(solution)/shard_map/ppermute | solution.py:184
  490.3 202.5 %collective-permute-start.19 = (bf16[512,1024]{1,0:T(8,128)(2,1)}, bf16[512,1024]{1,0:T(8,128)(2,1)S(1)}, u32[]{:S(2)}, u32[]{:S(2)}) collective-permute-start(bf16[512,1024]{1,0:T(8,128)(2,1)} %add_convert_fusion.1), channel_id=1, source_target_pairs={{0,0},{1,2},{2,1},{3,3},{4,4},{5,6},{6,5},{7,7},{8,8},{9,10},{10,9... | collective-permute-start | bytes 3145736 | tf_op jit(solution)/shard_map/ppermute | solution.py:184
  547.5 150.4 %collective-permute-start.22 = (bf16[80,2048]{1,0:T(8,128)(2,1)}, bf16[80,2048]{1,0:T(8,128)(2,1)S(1)}, u32[]{:S(2)}, u32[]{:S(2)}) collective-permute-start(bf16[80,2048]{1,0:T(8,128)(2,1)} %reduce-scatter.4.cloned.1.call-done), channel_id=1, source_target_pairs={{0,0},{1,2},{2,1},{3,3},{4,4},{5,6},{6,5},{7,7},{8,8},{9,10},{10,9... | collective-permute-start | bytes 983048 | tf_op jit(solution)/shard_map/ppermute | solution.py:184
  617.2 77.1 %collective-permute-start.24 = (bf16[64,2048]{1,0:T(8,128)(2,1)}, bf16[64,2048]{1,0:T(8,128)(2,1)S(1)}, u32[]{:S(2)}, u32[]{:S(2)}) collective-permute-start(bf16[64,2048]{1,0:T(8,128)(2,1)} %reduce-scatter.8.cloned.1.call-done), channel_id=1, source_target_pairs={{0,0},{1,2},{2,1},{3,3},{4,4},{5,6},{6,5},{7,7},{8,8},{9,10},{10,9... | collective-permute-start | bytes 786440 | tf_op jit(solution)/shard_map/ppermute | solution.py:184
  687.6 9.4 %collective-permute-start.23 = (bf16[64,2048]{1,0:T(8,128)(2,1)}, bf16[64,2048]{1,0:T(8,128)(2,1)S(1)}, u32[]{:S(2)}, u32[]{:S(2)}) collective-permute-start(bf16[64,2048]{1,0:T(8,128)(2,1)} %reduce-scatter.6.cloned.1.call-done), channel_id=1, source_target_pairs={{0,0},{1,2},{2,1},{3,3},{4,4},{5,6},{6,5},{7,7},{8,8},{9,10},{10,9... | collective-permute-start | bytes 786440 | tf_op jit(solution)/shard_map/ppermute | solution.py:184
  (3 other events, 2.1 us)
Sparse Core Ops, SparseCore 0:
  24.4 54.5 all-gather.6
  81.8 47.9 all-gather.10
  152.7 47.9 all-gather.8
  479.2 68.2 reduce-scatter.3
  550.9 66.3 reduce-scatter.7
  620.6 66.9 reduce-scatter.5
